TPU v7x, 128 devices: a whole 4x4x4 slice. The times are simulated.
128 devices in a mesh: seq: 8 (over z_hi, x), wide: 16 (over y, z_lo, core).
Axes of the slice: x: 4, y: 4, z: 4 (z_hi: 2, z_lo: 2; z = z_hi * 2 + z_lo), core: 2. Of those that a mesh axis runs over, the one named last changes fastest.
Arguments:
- queries: bfloat16 [16, 2048, 2048], P('wide', 'seq'), may hold values from -30.284271 to 30.284271
- key_vectors: bfloat16 [16, 2048, 2048], P('wide', 'seq'), may hold values from -6 to 6
- values: bfloat16 [16, 2048, 2048], P('wide', 'seq'), may hold values from -6 to 6
- audio_codes: int32 [16, 2048, 4], P(None, ('seq', 'wide')), may hold values from 0 to 1023
- depth_in: bfloat16 [2048, 1024], replicated, may hold values from -1.25 to 1.25
- code_embed: bfloat16 [3, 1024, 1024], replicated, may hold values from -3 to 3
- norm_gain: float32 [4, 1024], replicated, may hold values from 0.5 to 1.5
- out_heads: bfloat16 [1024, 4, 1024], replicated, may hold values from -0.5 to 0.5
- out_bias: float32 [4, 1024], replicated, may hold values from -330 to 330
Outputs:
- frame_losses: float32 [16, 2048, 4], P(None, ('seq', 'wide'))
- context_grad: bfloat16 [16, 2048, 2048], P('wide', 'seq')
- head_grads: float32 [1024, 4, 1024], P(('seq', 'wide'))
All inputs are finite; a program needn't handle non-finite values.
Results may differ from a plain program's by a relative error of at most 0.017.
Values may be sent and summed in bfloat16 or wider, within the bound.
No kernel may reach another device: no remote copies, remote signals or barrier semaphores. Data moves between devices by JAX's collectives and lax.ppermute only.
A program may use at most 192 MiB of HBM per device.

v0:
```python
from functools import partial

import jax
import jax.numpy as jnp
from jax import lax
from jax.sharding import PartitionSpec as P

HEADS = 16
HEAD_DIM = 128
FEATURES = 2048
DEPTH_DIM = 1024
CODEBOOKS = 4
VOCAB = 1024


def normalize(norm_gain, mixed_in):
    return (
        mixed_in
        * lax.rsqrt(jnp.mean(mixed_in * mixed_in, axis=-1, keepdims=True) + 1e-05)
        * norm_gain
    )


def fold_block(running, query_heads, query_pos, key_part, value_part):
    row_count = key_part.shape[1]
    key_heads = key_part[0].reshape(row_count, HEADS, HEAD_DIM)
    value_heads = value_part[0].reshape(row_count, HEADS, HEAD_DIM)
    scores = jnp.einsum(
        "qhd,khd->hqk", query_heads, key_heads, preferred_element_type=jnp.float32
    ) * HEAD_DIM ** (-0.5)
    key_pos = jnp.arange(row_count, dtype=jnp.int32)
    allowed = (key_pos[None, :] <= query_pos[:, None]) & (key_pos[None, :] >= 0)
    scores = jnp.where(allowed[None], scores, -jnp.inf)
    run_peak, run_total, run_acc = running
    new_peak = jnp.maximum(run_peak, jnp.max(scores, axis=2))
    weights = jnp.exp(scores - new_peak[:, :, None])
    new_total = jnp.sum(weights, axis=2)
    update = jnp.einsum(
        "hqk,khd->qhd",
        weights.astype(jnp.bfloat16),
        value_heads,
        preferred_element_type=jnp.float32,
    )
    return (new_peak, new_total, update)


def depth_pass(context, targets, depth_in, code_embed, norm_gain, out_heads, out_bias):
    row_count = context.shape[0]
    projected = jnp.dot(context, depth_in, preferred_element_type=jnp.float32)
    looked = code_embed[jnp.arange(CODEBOOKS - 1)[None, :], targets[:, : CODEBOOKS - 1]].astype(
        jnp.float32
    )
    mixed_in = projected[:, None, :] + jnp.concatenate(
        (jnp.zeros((row_count, 1, DEPTH_DIM), jnp.float32), looked), axis=1
    )
    normed, pullback = jax.vjp(partial(normalize, norm_gain), mixed_in)
    hidden = normed.astype(jnp.bfloat16)
    logits = (
        jnp.einsum("nce,ecv->ncv", hidden, out_heads, preferred_element_type=jnp.float32) + out_bias
    )
    top_logit = jnp.max(logits, axis=2, keepdims=True)
    shifted = jnp.exp(logits - top_logit)
    exp_total = jnp.sum(shifted, axis=2, keepdims=True)
    onehot = jnp.arange(VOCAB, dtype=jnp.int32)[None, None, :] == targets[:, :, None]
    picked = jnp.sum(jnp.where(onehot, logits, 0.0), axis=2)
    losses = top_logit[:, :, 0] + jnp.log(exp_total[:, :, 0]) - picked
    dlogits = (shifted / exp_total - onehot.astype(jnp.float32)).astype(jnp.bfloat16)
    dhidden = jnp.einsum("ncv,ecv->nce", dlogits, out_heads, preferred_element_type=jnp.float32)
    dmixed = pullback(dhidden)[0]
    dprojected = jnp.sum(dmixed, axis=1).astype(jnp.bfloat16)
    context_grad = lax.dot_general(
        dprojected, depth_in, (((1,), (1,)), ((), ())), preferred_element_type=jnp.float32
    ).astype(jnp.bfloat16)
    return (losses, hidden, dlogits, context_grad)


def shards(
    queries, key_vectors, values, audio_codes, depth_in, code_embed, norm_gain, out_heads, out_bias
):
    seq_count = lax.axis_size("seq")
    wide_count = lax.axis_size("wide")
    frames = queries.shape[1]
    seq_place = lax.axis_index("seq")
    position = seq_place * frames
    last_query = position + frames - 1
    query_heads = queries[0].reshape(frames, HEADS, HEAD_DIM)
    query_pos = position + jnp.arange(frames, dtype=jnp.int32)
    start_state = (
        jnp.full((HEADS, frames), -1e30, jnp.float32),
        jnp.zeros((HEADS, frames), jnp.float32),
        jnp.zeros((frames, HEADS, HEAD_DIM), jnp.float32),
    )
    incoming = (
        lax.all_gather(key_vectors, "seq", axis=1, tiled=True),
        lax.all_gather(values, "seq", axis=1, tiled=True),
    )

    def take_piece(state):
        return fold_block(state, query_heads, query_pos, incoming[0], incoming[1])

    carry_state = lax.cond(jnp.int32(0) <= last_query, take_piece, lambda state: state, start_state)
    run_peak, run_total, run_acc = carry_state
    context = (
        (run_acc / jnp.transpose(run_total)[:, :, None])
        .reshape(frames, FEATURES)
        .astype(jnp.bfloat16)
    )
    targets = lax.all_to_all(audio_codes, "wide", split_axis=0, concat_axis=1, tiled=True)[0]
    losses, hidden, dlogits, context_grad = depth_pass(
        context, targets, depth_in, code_embed, norm_gain, out_heads, out_bias
    )
    frame_losses = lax.all_to_all(
        losses.reshape(1, frames, CODEBOOKS), "wide", split_axis=1, concat_axis=0, tiled=True
    )
    grad_scale = (VOCAB / (seq_count * wide_count * frames)) ** 0.5
    head_grads = lax.psum_scatter(
        jnp.einsum("nce,ncv->ecv", hidden, dlogits, preferred_element_type=jnp.float32)
        * grad_scale,
        ("seq", "wide"),
        scatter_dimension=0,
        tiled=True,
    )
    return (frame_losses, context_grad.reshape(1, frames, FEATURES), head_grads)


def solution(mesh):
    return jax.shard_map(
        shards,
        mesh=mesh,
        in_specs=(
            P("wide", "seq", None),
            P("wide", "seq", None),
            P("wide", "seq", None),
            P(None, ("seq", "wide"), None),
            P(),
            P(),
            P(),
            P(),
            P(),
        ),
        out_specs=(
            P(None, ("seq", "wide"), None),
            P("wide", "seq", None),
            P(("seq", "wide"), None, None),
        ),
        check_vma=False,
    )
```

profile of v0, /device:TPU:2, one launch (start us, length us, event | category | flops | bytes accessed | tf_op | source)
XLA Modules:
  0.0 585.3 jit_solution(13195321542980949592)
XLA Ops:
  7.2 0.7 all-gather.3.cloned.1.call-update
  7.9 0.7 all-gather.5.cloned.1.call-update
  8.6 5.9 %all-to-all-start = ((s32[16,16,4]{1,2,0:T(4,128)}), s32[16,16,4]{1,2,0:T(4,128)S(1)}, u32[]{:S(2)}, u32[]{:S(2)}) async-start(s32[16,16,4]{1,2,0:T(4,128)} %param.14), calls=%async_computation | async-start | bytes 65536 | tf_op jit(solution)/shard_map/all_to_all | solution.py:108
  14.7 6.1 %all-to-all-done = s32[16,16,4]{1,2,0:T(4,128)S(1)} async-done(((s32[16,16,4]{1,2,0:T(4,128)}), s32[16,16,4]{1,2,0:T(4,128)S(1)}, u32[]{:S(2)}, u32[]{:S(2)}) %all-to-all-start) | async-done | bytes 4128 | tf_op jit(solution)/shard_map/all_to_all | solution.py:108
  21.2 9.8 %gather_fusion = bf16[768,1024]{1,0:T(8,128)(2,1)S(1)} fusion(bf16[3,1024,1024]{2,1,0:T(8,128)(2,1)} %param.16, s32[768]{0:T(1024)S(1)} %reshape.96), kind=kCustom, calls=%fused_computation | custom fusion | bytes 3151872 | tf_op jit(solution)/shard_map/gather | solution.py:50
  30.9 2.3 reshape.99
  33.3 2.2 copy.53
  35.5 85.0 %all-gather.3.cloned.1.call-done = bf16[1,2048,2048]{2,1,0:T(8,128)(2,1)} async-done(((bf16[1,256,2048]{2,1,0:T(8,128)(2,1)}), bf16[1,2048,2048]{2,1,0:T(8,128)(2,1)}) %all-gather.3.cloned.1.call-update) | async-done | bytes 8388624 | tf_op jit(solution)/shard_map/all_gather | solution.py:94
  120.5 109.0 %all-gather.5.cloned.1.call-done = bf16[1,2048,2048]{2,1,0:T(8,128)(2,1)} async-done(((bf16[1,256,2048]{2,1,0:T(8,128)(2,1)}), bf16[1,2048,2048]{2,1,0:T(8,128)(2,1)}) %all-gather.5.cloned.1.call-update) | async-done | bytes 8388624 | tf_op jit(solution)/shard_map/all_gather | solution.py:95
  229.5 86.1 %conditional.1 = (f32[16,256]{1,0:T(8,128)S(1)}, f32[256,16,128]{0,2,1:T(8,128)}) conditional(s32[]{:T(128)} %convert_element_type.28, () %tuple.16, (s32[]{:T(128)}, s32[256]{0:T(256)S(1)}, bf16[1,256,2048]{2,1,0:T(8,128)(2,1)}, bf16[1,2048,2048]{2,1,0:T(8,128)(2,1)}, bf16[1,2048,2048]{2,1,0:T(8,128)(2,1)}) %tuple.17), branch_computations={%region_0.0_spmd, %region_1.4_spmd} | conditional | flops 4387762176 | bytes 166825008 | solution.py:101
  229.9 9.8 %copy.67 = bf16[256,8,16,128]{3,2,1,0:T(8,128)(2,1)} copy(bf16[256,8,16,128]{3,1,2,0:T(8,128)(2,1)} %bitcast.56) | data formatting | bytes 16777216 | tf_op jit(solution)/shard_map/cond
  240.0 24.1 %fusion = (f32[16,256]{1,0:T(8,128)S(1)}, f32[16,256,2048]{2,1,0:T(8,128)}) fusion(pred[256,2048]{1,0:T(8,128)(4,1)S(1)} %iota_compare_fusion, bf16[2048,16,128]{2,1,0:T(8,128)(2,1)} %bitcast.55, bf16[256,16,128]{2,1,0:T(8,128)(2,1)S(1)} %bitcast.59), kind=kOutput, calls=%fused_computation.3 | convolution fusion | flops 2172645376 | bytes 43532288 | tf_op jit(solution)/shard_map/cond/branch_1_fun/qhd,khd->hqk/dot_general | solution.py:28
  264.1 9.7 %copy.68 = bf16[256,8,16,128]{3,2,1,0:T(8,128)(2,1)} copy(bf16[256,8,16,128]{3,1,2,0:T(8,128)(2,1)} %bitcast.57) | data formatting | bytes 16777216 | tf_op jit(solution)/shard_map/cond
  273.8 23.8 %fusion.9 = f32[256,16,128]{2,0,1:T(8,128)} fusion(bf16[2048,16,128]{2,1,0:T(8,128)(2,1)} %bitcast.58, f32[16,256,2048]{2,1,0:T(8,128)} %get-tuple-element.43, f32[16,256]{1,0:T(8,128)S(1)} %broadcast_maximum_fusion, pred[256,2048]{1,0:T(8,128)(4,1)S(1)} %iota_compare_fusion), kind=kOutput, calls=%fused_computation.12 | convolution fusion | flops 2181038080 | bytes 44580864 | tf_op jit(solution)/shard_map/cond/branch_1_fun/hqk,khd->qhd/dot_general | solution.py:38
  297.6 2.9 copy.65
  300.5 15.2 %fusion.2 = f32[16,256]{1,0:T(8,128)S(1)} fusion(f32[16,256,2048]{2,1,0:T(8,128)} %get-tuple-element.43, f32[16,256]{1,0:T(8,128)S(1)} %broadcast_maximum_fusion, pred[256,2048]{1,0:T(8,128)(4,1)S(1)} %iota_compare_fusion), kind=kLoop, calls=%fused_computation.5 | loop fusion | flops 33550336 | bytes 34111488 | tf_op jit(solution)/shard_map/cond/branch_1_fun/reduce_sum | solution.py:37
  315.7 1.8 divide_convert_fusion
  317.5 3.5 fusion.35
  321.0 0.6 multiply_reduce_fusion
  321.5 9.4 %bitcast_reduce_fusion = (f32[256,4]{0,1:T(4,128)S(1)}, f32[4,256,1024]{2,1,0:T(8,128)S(1)}) fusion(f32[4,1024]{1,0:T(4,128)S(1)} %copy-done.2, bf16[1024,4,1024]{2,1,0:T(4,128)(2,1)} %param.18, bf16[256,3,1024]{2,0,1:T(8,128)(2,1)S(1)} %copy.53, f32[4,1024]{1,0:T(4,128)S(1)} %copy-done.3, f32[256,4]{0,1:T(4,128)S(1)} %fusion.32, f32[256,1024]{1,0:T(8,128)S(1)} %fusion.35), kind=kOutput, calls=%fused_computation.30 | convolution fusion | flops 2154822656 | bytes 15245312 | tf_op jit(solution)/shard_map/nce,ecv->ncv/dot_general | solution.py:59
  330.9 1.6 fusion.25
  333.0 7.9 %multiply_bitcast_fusion = f32[1024,4,1024]{0,2,1:T(8,128)} fusion(bf16[256,3,1024]{2,0,1:T(8,128)(2,1)S(1)} %copy.53, f32[4,1024]{1,0:T(4,128)S(1)} %copy-done.3, f32[256,4]{0,1:T(4,128)S(1)} %fusion.32, f32[256,1024]{1,0:T(8,128)S(1)} %fusion.35, f32[4,256,1024]{2,1,0:T(8,128)S(1)} %get-tuple-element.45, f32[256,4]{0,1:T(4,128)S(1)} %get-tuple-element.40, ...), kind=kOutput, calls=%fused_computation.18 | convolution fusion | flops 2164260864 | bytes 23642112 | tf_op jit(solution)/shard_map/nce,ncv->ecv/dot_general | solution.py:117
  340.8 20.2 %copy.59 = f32[1024,4,1024]{2,1,0:T(4,128)} copy(f32[1024,4,1024]{0,2,1:T(8,128)} %multiply_bitcast_fusion) | data formatting | bytes 33554432 | tf_op jit(solution)/shard_map/mul | solution.py:117
  361.0 0.8 copy.55
  361.8 4.7 all-to-all-start.1
  366.5 12.5 %fusion.22 = (f32[256,4]{0,1:T(4,128)S(1)}, f32[4,256,1024]{2,1,0:T(8,128)S(1)}) fusion(bf16[256,3,1024]{2,0,1:T(8,128)(2,1)S(1)} %copy.53, f32[4,1024]{1,0:T(4,128)S(1)} %copy-done.3, f32[256,1024]{1,0:T(8,128)S(1)} %fusion.35, bf16[1024,4,1024]{2,1,0:T(4,128)(2,1)} %param.18, f32[4,256,1024]{2,1,0:T(8,128)} %copy-done, ...), kind=kOutput, calls=%fused_computation.27 | convolution fusion | flops 2160065536 | bytes 19447808 | tf_op jit(solution)/shard_map/ncv,ecv->nce/dot_general | solution.py:68
  379.1 1.3 fusion.21
  380.4 0.9 copy-done.4
  381.3 2.3 fusion.26
  383.6 0.8 copy.60
  384.4 192.6 %all-reduce.4.cloned.1.call-done = f32[1024,4,1024]{2,1,0:T(4,128)} async-done(((f32[1024,4,1024]{2,1,0:T(4,128)}), f32[1024,4,1024]{2,1,0:T(4,128)}) %all-reduce.4.cloned.1.call-update) | async-done | bytes 16777232
  577.0 1.6 constant_dynamic-slice_fusion
  (27 shorter events, 1.7 us)
Async XLA Ops:
  7.2 113.3 %all-gather.3.cloned.1.call-start = ((), (), s32[]{:S(2)}) async-start(), calls=%async_computation.2 | async-start | bytes 9437184 | tf_op jit(solution)/shard_map/all_gather | solution.py:94
  7.9 221.6 %all-gather.5.cloned.1.call-start = ((), (), s32[]{:S(2)}) async-start(), calls=%async_computation.3 | async-start | bytes 9437184 | tf_op jit(solution)/shard_map/all_gather | solution.py:95
  8.6 12.1 %all-to-all-start = ((s32[16,16,4]{1,2,0:T(4,128)}), s32[16,16,4]{1,2,0:T(4,128)S(1)}, u32[]{:S(2)}, u32[]{:S(2)}) async-start(s32[16,16,4]{1,2,0:T(4,128)} %param.14), calls=%async_computation | async-start | bytes 65536 | tf_op jit(solution)/shard_map/all_to_all | solution.py:108
  14.6 562.4 %all-reduce.4.cloned.1.call-start = ((), (), s32[]{:S(2)}) async-start(), calls=%async_computation.4 | async-start | bytes 33554432
  229.9 9.8 %copy-start.1 = (bf16[1,256,2048]{2,1,0:T(8,128)(2,1)S(1)}, bf16[1,256,2048]{2,1,0:T(8,128)(2,1)}, u32[]{:S(2)}) copy-start(bf16[1,256,2048]{2,1,0:T(8,128)(2,1)} %get-tuple-element.26) | copy-start | bytes 3145732 | tf_op jit(solution)/shard_map/cond
  317.5 4.1 copy-start.2
  317.5 4.1 copy-start.3
  330.9 2.1 copy-start
  361.8 21.8 %all-to-all-start.1 = ((f32[1,256,4]{2,0,1:T(1,128)}), f32[1,256,4]{2,0,1:T(1,128)S(1)}, u32[]{:S(2)}, u32[]{:S(2)}) async-start(f32[1,256,4]{2,0,1:T(1,128)} %copy.55), calls=%async_computation.1 | async-start | bytes 262144 | tf_op jit(solution)/shard_map/all_to_all | solution.py:112
  379.1 2.3 copy-start.4
Sparse Core Ops, SparseCore 0:
  10.3 110.1 all-gather.2
  122.8 106.6 all-gather.4
  361.1 215.8 all-reduce.3
where the time goes:
time: 593 us; the launch traced here: 585 us
  waiting for transfers between devices  394 us (66%)
  matrix products  83.4 us (14%)
  local copies, waits for them, and re-layouts  62.1 us (10%)
  other arithmetic  20.9 us (4%)
  between operations  14.1 us (2%)
  starting transfers between devices  10.8 us (2%)
    unnamed x4, waiting for transfers between devices  194 us
    all_gather x1, waiting for transfers between devices, shards(): lax.all_gather(values, 'seq', axis=1, tiled=True)  109 us
    all_gather x1, waiting for transfers between devices, shards(): lax.all_gather(key_vectors, 'seq', axis=1, tiled=True)  85 us
    dot_general x1, matrix products, fold_block(): jnp.einsum('qhd,khd->hqk', query_heads, key_heads, preferred_element_type...  24.1 us
    dot_general x1, matrix products, fold_block(): jnp.einsum('hqk,khd->qhd', weights.astype(jnp.bfloat16), value_heads, pre...  23.8 us
    mul x1, local copies, waits for them, and re-layouts, shards(): jnp.einsum('nce,ncv->ecv', hidden, dlogits, preferred_element_type=jnp.fl...  20.2 us
    cond x5, local copies, waits for them, and re-layouts  19.8 us
    reduce_sum x1, other arithmetic, fold_block(): new_total = jnp.sum(weights, axis=2)  15.2 us
  transfers between devices with their start and end apart: 5, of which 4 were waited for; matrix products, arithmetic and copies ran while one was open for 6% of the time, Pallas kernels for 0%

commit v1 on v0

v1 whole, which is shorter than its diff:
```python
from functools import partial

import jax
import jax.numpy as jnp
from jax import lax
from jax.experimental import pallas as pl
from jax.experimental.pallas import tpu as pltpu
from jax.sharding import PartitionSpec as P

HEADS = 16
HEAD_DIM = 128
FEATURES = 2048
DEPTH_DIM = 1024
CODEBOOKS = 4
VOCAB = 1024
SEQ = 8
WIDE = 16
FRAMES = 256
LENGTH = SEQ * FRAMES
PAIR = 2 * HEAD_DIM


def attend_kernel(qkv_ref, out_ref):
    to_exp2 = HEAD_DIM ** (-0.5) * 1.4426950408889634
    row = lax.broadcasted_iota(jnp.int32, (FRAMES, FRAMES), 0)
    col = lax.broadcasted_iota(jnp.int32, (FRAMES, FRAMES), 1)
    for head in range(2):
        at = head * HEAD_DIM
        for block in range(SEQ):
            extent = (block + 1) * FRAMES
            first = block * FRAMES
            q = qkv_ref[first:extent, at : at + HEAD_DIM]
            diag = lax.dot_general(
                q,
                qkv_ref[first:extent, PAIR + at : PAIR + at + HEAD_DIM],
                (((1,), (1,)), ((), ())),
                preferred_element_type=jnp.float32,
            )
            diag = jnp.where(col <= row, diag, -jnp.inf)
            top = jnp.max(diag, axis=1, keepdims=True)
            if block:
                past = lax.dot_general(
                    q,
                    qkv_ref[:first, PAIR + at : PAIR + at + HEAD_DIM],
                    (((1,), (1,)), ((), ())),
                    preferred_element_type=jnp.float32,
                )
                top = jnp.maximum(top, jnp.max(past, axis=1, keepdims=True))
            weights = jnp.exp2((diag - top) * to_exp2)
            total = jnp.sum(weights, axis=1, keepdims=True)
            acc = jnp.dot(
                weights.astype(jnp.bfloat16),
                qkv_ref[first:extent, 2 * PAIR + at : 2 * PAIR + at + HEAD_DIM],
                preferred_element_type=jnp.float32,
            )
            if block:
                weights = jnp.exp2((past - top) * to_exp2)
                total = total + jnp.sum(weights, axis=1, keepdims=True)
                acc = acc + jnp.dot(
                    weights.astype(jnp.bfloat16),
                    qkv_ref[:first, 2 * PAIR + at : 2 * PAIR + at + HEAD_DIM],
                    preferred_element_type=jnp.float32,
                )
            out_ref[first:extent, at : at + HEAD_DIM] = (acc / total).astype(jnp.bfloat16)


def attend(qkv):
    return pl.pallas_call(
        attend_kernel,
        out_shape=jax.ShapeDtypeStruct((LENGTH, PAIR), jnp.bfloat16),
        in_specs=[pl.BlockSpec(memory_space=pltpu.VMEM)],
        out_specs=pl.BlockSpec(memory_space=pltpu.VMEM),
        compiler_params=pltpu.CompilerParams(vmem_limit_bytes=40 * 2**20),
        cost_estimate=pl.CostEstimate(
            flops=2 * 36 * FRAMES * FRAMES * HEAD_DIM * 4,
            bytes_accessed=LENGTH * PAIR * 8,
            transcendentals=2 * 36 * FRAMES * FRAMES,
        ),
    )(qkv)


def normalize(norm_gain, mixed_in):
    return (
        mixed_in
        * lax.rsqrt(jnp.mean(mixed_in * mixed_in, axis=-1, keepdims=True) + 1e-05)
        * norm_gain[:, None, :]
    )


def swap_cores(array):
    return lax.ppermute(array, "wide", [(i, i ^ 1) for i in range(WIDE)])


def shards(
    queries, key_vectors, values, audio_codes, depth_in, code_embed, norm_gain, out_heads, out_bias
):
    wide_place = lax.axis_index("wide")
    core = wide_place % 2
    packed = jnp.concatenate(
        [
            a.reshape(FRAMES, SEQ, PAIR).transpose(1, 0, 2)
            for a in (queries[0], key_vectors[0], values[0])
        ],
        axis=2,
    )
    qkv = lax.all_to_all(packed, "seq", 0, 0, tiled=True).reshape(LENGTH, 3 * PAIR)
    codes = lax.all_gather(audio_codes.reshape(WIDE, 64), "wide", axis=0)
    targets = lax.dynamic_index_in_dim(codes, wide_place, 1, keepdims=False).reshape(
        FRAMES, CODEBOOKS
    )
    looked = code_embed[jnp.arange(CODEBOOKS - 1)[:, None], targets.T[: CODEBOOKS - 1]].astype(
        jnp.float32
    )
    heads = out_heads.transpose(1, 0, 2)

    context = attend(qkv).reshape(SEQ, FRAMES, PAIR)
    context = (
        lax.all_to_all(context, "seq", 0, 0, tiled=True)
        .transpose(1, 0, 2)
        .reshape(FRAMES, FEATURES)
    )
    projected = jnp.dot(context, depth_in, preferred_element_type=jnp.float32)
    mixed_in = projected[None] + jnp.concatenate(
        (jnp.zeros((1, FRAMES, DEPTH_DIM), jnp.float32), looked), axis=0
    )
    normed, pullback = jax.vjp(partial(normalize, norm_gain), mixed_in)
    hidden = normed.astype(jnp.bfloat16)
    logits = (
        jnp.einsum("cne,cev->cnv", hidden, heads, preferred_element_type=jnp.float32)
        + out_bias[:, None, :]
    )
    top_logit = jnp.max(logits, axis=2, keepdims=True)
    shifted = jnp.exp(logits - top_logit)
    exp_total = jnp.sum(shifted, axis=2, keepdims=True)
    onehot = jnp.arange(VOCAB, dtype=jnp.int32)[None, None, :] == targets.T[:, :, None]
    picked = jnp.sum(jnp.where(onehot, logits, 0.0), axis=2)
    losses = top_logit[:, :, 0] + jnp.log(exp_total[:, :, 0]) - picked
    dlogits = (shifted / exp_total - onehot.astype(jnp.float32)).astype(jnp.bfloat16)

    mine = 2 * core
    other = 2 - mine

    def pair(array):
        theirs = swap_cores(lax.dynamic_slice_in_dim(array, other, 2, 0))
        return jnp.concatenate((lax.dynamic_slice_in_dim(array, mine, 2, 0), theirs), axis=1)

    partial_grads = jnp.einsum(
        "cne,cnv->ecv", pair(hidden), pair(dlogits), preferred_element_type=jnp.float32
    ).astype(jnp.bfloat16)
    shares = lax.all_to_all(
        partial_grads.reshape(SEQ * WIDE, 8, 2, VOCAB), ("seq", "wide"), 0, 0, tiled=True
    )
    grad_scale = (VOCAB / (SEQ * WIDE * FRAMES)) ** 0.5
    summed = jnp.sum(shares.reshape(SEQ * WIDE // 2, 2, 8, 2, VOCAB).astype(jnp.float32), axis=0)
    head_grads = summed.transpose(1, 0, 2, 3).reshape(8, CODEBOOKS, VOCAB) * grad_scale

    dhidden = jnp.einsum("cnv,cev->cne", dlogits, heads, preferred_element_type=jnp.float32)
    dmixed = pullback(dhidden)[0]
    dprojected = jnp.sum(dmixed, axis=0).astype(jnp.bfloat16)
    context_grad = lax.dot_general(
        dprojected, depth_in, (((1,), (1,)), ((), ())), preferred_element_type=jnp.float32
    ).astype(jnp.bfloat16)

    all_losses = lax.all_gather(losses.T.reshape(WIDE, 64), "wide", axis=0)
    frame_losses = lax.dynamic_index_in_dim(all_losses, wide_place, 1, keepdims=False).reshape(
        WIDE, 16, CODEBOOKS
    )
    return (frame_losses, context_grad.reshape(1, FRAMES, FEATURES), head_grads)


def solution(mesh):
    return jax.shard_map(
        shards,
        mesh=mesh,
        in_specs=(
            P("wide", "seq", None),
            P("wide", "seq", None),
            P("wide", "seq", None),
            P(None, ("seq", "wide"), None),
            P(),
            P(),
            P(),
            P(),
            P(),
        ),
        out_specs=(
            P(None, ("seq", "wide"), None),
            P("wide", "seq", None),
            P(("seq", "wide"), None, None),
        ),
        check_vma=False,
    )
```

time: 593 us -> 224 us (0.38)
  waiting for transfers between devices: 394 us -> 3.65 us
  blocking collectives: 0 us -> 133 us
  matrix products: 83.4 us -> 29.4 us
  local copies, waits for them, and re-layouts: 62.1 us -> 24.7 us
  between operations: 14.1 us -> 0.93 us
  other arithmetic: 20.9 us -> 8.89 us
  Pallas kernels: 0 us -> 8.94 us
    unnamed x4 -> x0, waiting for transfers between devices: 194 us -> none
    all_gather x2 -> x0, waiting for transfers between devices: 194 us -> none  [the longest x1 109 us: shards(): lax.all_gather(values, 'seq', axis=1, tiled=True)]
    all_gather x0 -> x2, blocking collectives: none -> 86 us  [the longest x1 61.2 us: shards(): all_losses = lax.all_gather(losses.T.reshape(WIDE, 64), 'wide', axis=0)]
    dot_general x7 -> x5, matrix products: 83.4 us -> 29.4 us  [the longest x1 11.9 us: shards(): jnp.einsum('cnv,cev->cne', dlogits, heads, preferred_element_type=jnp.flo...]
    all_to_all x0 -> x1, blocking collectives: none -> 46.9 us  [shards(): lax.all_to_all(packed, 'seq', 0, 0, tiled=True).reshape(LENGTH, 3 * PAIR)]
    cond x6 -> x0, local copies, waits for them, and re-layouts: 22.7 us -> none
    mul x1, local copies, waits for them, and re-layouts: 20.2 us -> 0.01 us  [shards(): summed.transpose(1, 0, 2, 3).reshape(8, CODEBOOKS, VOCAB) * grad_scale]
    reduce_sum x3, other arithmetic: 18.1 us -> 5.95 us  [the longest x1 3.03 us: shards(): jnp.sum(shares.reshape(SEQ * WIDE // 2, 2, 8, 2, VOCAB).astype(jnp.float3...]
  transfers between devices with their start and end apart: 5 -> 4, of which waited for: 4 -> 2; matrix products, arithmetic and copies ran while one was open for 6% -> 13% of each run, Pallas kernels for 0% -> 0%
where the time goes in v1:
time: 224 us; the launch traced here: 221 us
  blocking collectives  133 us (59%)
  matrix products  29.4 us (13%)
  local copies, waits for them, and re-layouts  24.7 us (11%)
  starting transfers between devices  11.5 us (5%)
  Pallas kernels  8.94 us (4%)
  other arithmetic  8.89 us (4%)
  waiting for transfers between devices  3.65 us (2%)
    all_gather x1, blocking collectives, shards(): all_losses = lax.all_gather(losses.T.reshape(WIDE, 64), 'wide', axis=0)  61.2 us
    all_to_all x1, blocking collectives, shards(): lax.all_to_all(packed, 'seq', 0, 0, tiled=True).reshape(LENGTH, 3 * PAIR)  46.9 us
    all_gather x1, blocking collectives, shards(): codes = lax.all_gather(audio_codes.reshape(WIDE, 64), 'wide', axis=0)  24.9 us
    dot_general x1, matrix products, shards(): jnp.einsum('cnv,cev->cne', dlogits, heads, preferred_element_type=jnp.flo...  11.9 us
    gather x1, local copies, waits for them, and re-layouts, shards(): code_embed[jnp.arange(CODEBOOKS - 1)[:, None], targets.T[:CODEBOOKS - 1]]  11.3 us
    dot_general x1, matrix products, shards(): jnp.einsum('cne,cev->cnv', hidden, heads, preferred_element_type=jnp.floa...  9.08 us
    pallas_call x1, Pallas kernels, attend(): pl.pallas_call(attend_kernel, out_shape=jax.ShapeDtypeStruct((LENGTH, PAI...  8.94 us
    unnamed x21, local copies, waits for them, and re-layouts  7.86 us
  transfers between devices with their start and end apart: 4, of which 2 were waited for; matrix products, arithmetic and copies ran while one was open for 13% of the time, Pallas kernels for 0%

profile of v1, /device:TPU:2, one launch (start us, length us, event | category | flops | bytes accessed | tf_op | source)
XLA Modules:
  0.0 220.9 jit_solution(16614989332917808290)
XLA Ops:
  0.6 1.6 copy.88
  2.3 1.5 copy.87
  3.8 0.3 copy.86
  4.3 0.5 copy_bitcast_fusion
  5.1 46.9 %all_to_all.15 = bf16[8,256,768]{2,1,0:T(8,128)(2,1)S(1)} all-to-all(bf16[8,256,768]{2,1,0:T(8,128)(2,1)S(1)} %pad_maximum_fusion), channel_id=1, replica_groups=mesh['seq'=8,'wide'=16] {'seq'}, dimensions={0} | all-to-all | bytes 6291456 | tf_op jit(solution)/shard_map/all_to_all | solution.py:106
  51.9 8.9 %shard_map.112 = bf16[2048,256]{1,0:T(8,128)(2,1)S(1)} custom-call(bf16[2048,768]{1,0:T(8,128)(2,1)S(1)} %bitcast.45), custom_call_target="tpu_custom_call" | custom-call | flops 2415919104 | bytes 4194304 | tf_op jit(solution)/shard_map/pallas_call | solution.py:68
  60.9 1.3 copy.69
  62.2 4.2 %all-to-all-start.1 = ((bf16[8,256,256]{1,2,0:T(8,128)(2,1)}), bf16[8,256,256]{1,2,0:T(8,128)(2,1)S(1)}, u32[]{:S(2)}, u32[]{:S(2)}) async-start(bf16[8,256,256]{1,2,0:T(8,128)(2,1)} %copy.69), calls=%async_computation.1 | async-start | bytes 2097152 | tf_op jit(solution)/shard_map/all_to_all | solution.py:118
  66.6 24.9 %all_gather.6 = s32[16,16,64]{2,1,0:T(8,128)S(1)} all-gather(s32[1,16,64]{2,1,0:T(8,128)S(1)} %copy.71), channel_id=1, replica_groups=mesh['seq'=8,'wide'=16] {'wide'}, dimensions={0}, use_global_device_ids=true | all-gather | bytes 69632 | tf_op jit(solution)/shard_map/all_gather | solution.py:107
  91.7 11.3 %gather_fusion = bf16[768,1024]{1,0:T(8,128)(2,1)S(1)} fusion(bf16[3,1024,1024]{2,1,0:T(8,128)(2,1)} %param.14, s32[768]{0:T(1024)S(1)} %reshape.67), kind=kCustom, calls=%fused_computation | custom fusion | bytes 3151872 | tf_op jit(solution)/shard_map/gather | solution.py:111
  103.1 1.0 copy-done.2
  104.0 3.8 %fusion.20 = f32[256,1024]{1,0:T(8,128)S(1)} fusion(bf16[256,2048]{0,1:T(8,128)(2,1)} %bitcast.58, bf16[2048,1024]{1,0:T(8,128)(2,1)} %param.13), kind=kOutput, calls=%fused_computation.50 | convolution fusion | flops 1073741824 | bytes 6291456 | tf_op jit(solution)/shard_map/dot_general | solution.py:122
  107.8 0.6 multiply_reduce_fusion.1
  108.4 0.6 multiply_convert_fusion
  109.0 9.1 %add_reduce_fusion = (f32[4,256]{1,0:T(4,128)S(1)}, f32[4,256,1024]{2,1,0:T(8,128)S(1)}) fusion(f32[4,1024]{1,0:T(4,128)S(1)} %copy-done.3, bf16[4,256,1024]{2,1,0:T(8,128)(2,1)S(1)} %multiply_convert_fusion, bf16[4,1024,1024]{2,0,1:T(4,128)(2,1)} %bitcast.65), kind=kOutput, calls=%fused_computation.18 | convolution fusion | flops 2149579776 | bytes 14700544 | tf_op jit(solution)/shard_map/cne,cev->cnv/dot_general | solution.py:129
  118.1 1.6 fusion.5
  119.7 1.5 subtract_convert_fusion
  121.6 1.0 copy-done
  122.6 0.5 collective-permute-start.1
  123.1 2.1 collective-permute-done
  125.2 1.5 collective-permute-done.1
  126.7 2.4 %convert_bitcast_fusion = bf16[128,8,2,1024]{3,1,0,2:T(8,128)(2,1)S(1)} fusion(bf16[2,256,1024]{2,1,0:T(8,128)(2,1)S(1)} %collective-permute-done, bf16[2,256,1024]{2,1,0:T(8,128)(2,1)S(1)} %get-tuple-element.19, bf16[2,256,1024]{2,1,0:T(8,128)(2,1)S(1)} %collective-permute-done.1, bf16[2,256,1024]{2,1,0:T(8,128)(2,1)S(1)} %get-tuple-element.17), kind=kOutput, calls=%fused_computation.8 | convolution fusion | flops 2157969408 | bytes 8388608 | tf_op jit(solution)/shard_map/cne,cnv->ecv/dot_general | solution.py:147
  129.1 2.6 %copy.78 = bf16[128,8,2,1024]{3,1,2,0:T(8,128)(2,1)} copy(bf16[128,8,2,1024]{3,1,0,2:T(8,128)(2,1)S(1)} %convert_bitcast_fusion) | data formatting | bytes 8388608 | tf_op jit(solution)/shard_map/reshape | solution.py:151
  131.7 6.8 %all-to-all-start.2 = ((bf16[128,8,2,1024]{3,1,2,0:T(8,128)(2,1)}), bf16[128,8,2,1024]{3,1,2,0:T(8,128)(2,1)}, u32[]{:S(2)}, u32[]{:S(2)}) async-start(bf16[128,8,2,1024]{3,1,2,0:T(8,128)(2,1)} %copy.78), calls=%async_computation.2 | async-start | bytes 8388608 | tf_op jit(solution)/shard_map/all_to_all | solution.py:150
  138.8 61.2 %all_gather.7 = f32[16,16,64]{2,1,0:T(8,128)S(1)} all-gather(f32[1,16,64]{2,1,0:T(8,128)S(1)} %all_gather_reshape.7), channel_id=1, replica_groups=mesh['seq'=8,'wide'=16] {'wide'}, dimensions={0}, use_global_device_ids=true | all-gather | bytes 69632 | tf_op jit(solution)/shard_map/all_gather | solution.py:164
  200.1 0.7 copy.81
  200.8 11.9 %multiply_reduce_fusion = (f32[4,256]{1,0:T(4,128)S(1)}, f32[4,256,1024]{2,1,0:T(8,128)S(1)}) fusion(bf16[3,256,1024]{2,1,0:T(8,128)(2,1)S(1)} %bitcast.49, f32[4,1024]{1,0:T(4,128)S(1)} %copy-done.4, f32[256,1024]{1,0:T(8,128)S(1)} %fusion.20, bf16[4,256,1024]{2,1,0:T(8,128)(2,1)} %copy-done, bf16[4,1024,1024]{2,0,1:T(4,128)(2,1)} %bitcast.66), kind=kOutput, calls=%fused_computation.9 | convolution fusion | flops 2152725504 | bytes 17321984 | tf_op jit(solution)/shard_map/cnv,cev->cne/dot_general | solution.py:157
  212.7 1.3 fusion.4
  214.0 0.8 copy-done.6
  214.9 2.3 %fusion.6 = bf16[1,256,2048]{2,1,0:T(8,128)(2,1)} fusion(bf16[2048,1024]{1,0:T(8,128)(2,1)S(1)} %copy-done.6, bf16[256,1024]{1,0:T(8,128)(2,1)S(1)} %fusion.4), kind=kOutput, calls=%fused_computation.21 | convolution fusion | flops 1074266112 | bytes 5767168 | tf_op jit(solution)/shard_map/dot_general | solution.py:160
  217.1 3.0 %convert_reduce_fusion = f32[2,8,2,1024]{3,1,2,0:T(8,128)S(1)} fusion(bf16[64,2,8,2,1024]{4,2,3,1,0:T(8,128)(2,1)} %bitcast.21), kind=kLoop, calls=%fused_computation.1 | loop fusion | flops 4161536 | bytes 4325376 | tf_op jit(solution)/shard_map/reduce_sum | solution.py:154
  220.2 0.7 copy.82
  (35 shorter events, 1.7 us)
Async XLA Ops:
  0.6 3.2 %copy-start.1 = (bf16[1,256,2048]{2,1,0:T(8,128)(2,1)S(1)}, bf16[1,256,2048]{2,1,0:T(8,128)(2,1)}, u32[]{:S(2)}) copy-start(bf16[1,256,2048]{2,1,0:T(8,128)(2,1)} %param.9) | copy-start | bytes 3145732
  60.9 5.5 %copy-start.5 = (s32[16,16,4]{1,2,0:T(4,128)S(1)}, s32[16,16,4]{1,2,0:T(4,128)}, u32[]{:S(2)}) copy-start(s32[16,16,4]{1,2,0:T(4,128)} %param.12) | copy-start | bytes 12292
  62.2 40.8 %all-to-all-start.1 = ((bf16[8,256,256]{1,2,0:T(8,128)(2,1)}), bf16[8,256,256]{1,2,0:T(8,128)(2,1)S(1)}, u32[]{:S(2)}, u32[]{:S(2)}) async-start(bf16[8,256,256]{1,2,0:T(8,128)(2,1)} %copy.69), calls=%async_computation.1 | async-start | bytes 2097152 | tf_op jit(solution)/shard_map/all_to_all | solution.py:118
  103.1 1.0 copy-start.2
  104.0 4.4 %copy-start.4 = (f32[4,1024]{1,0:T(4,128)S(1)}, f32[4,1024]{1,0:T(4,128)}, u32[]{:S(2)}) copy-start(f32[4,1024]{1,0:T(4,128)} %param.15) | copy-start | bytes 49156
  107.8 1.2 copy-start.3
  121.2 1.4 copy-start
  122.6 2.7 %collective-permute-start = (bf16[2,256,1024]{2,1,0:T(8,128)(2,1)S(1)}, bf16[2,256,1024]{2,1,0:T(8,128)(2,1)S(1)}, u32[]{:S(2)}, u32[]{:S(2)}) collective-permute-start(bf16[2,256,1024]{2,1,0:T(8,128)(2,1)S(1)} %get-tuple-element.20), channel_id=1, source_target_pairs={{0,1},{1,0},{2,3},{3,2},{4,5},{5,4},{6,7},{7,6},{8,9},{9,8},{10,11... | collective-permute-start | bytes 3145736 | tf_op jit(solution)/shard_map/ppermute | solution.py:91
  122.6 4.2 %collective-permute-start.1 = (bf16[2,256,1024]{2,1,0:T(8,128)(2,1)S(1)}, bf16[2,256,1024]{2,1,0:T(8,128)(2,1)S(1)}, u32[]{:S(2)}, u32[]{:S(2)}) collective-permute-start(bf16[2,256,1024]{2,1,0:T(8,128)(2,1)S(1)} %get-tuple-element.18), channel_id=1, source_target_pairs={{0,1},{1,0},{2,3},{3,2},{4,5},{5,4},{6,7},{7,6},{8,9},{9,8},{10,11... | collective-permute-start | bytes 3145736 | tf_op jit(solution)/shard_map/ppermute | solution.py:91
  131.7 85.4 %all-to-all-start.2 = ((bf16[128,8,2,1024]{3,1,2,0:T(8,128)(2,1)}), bf16[128,8,2,1024]{3,1,2,0:T(8,128)(2,1)}, u32[]{:S(2)}, u32[]{:S(2)}) async-start(bf16[128,8,2,1024]{3,1,2,0:T(8,128)(2,1)} %copy.78), calls=%async_computation.2 | async-start | bytes 8388608 | tf_op jit(solution)/shard_map/all_to_all | solution.py:150
  212.7 2.2 copy-start.6

commit v2 on v1

v2 whole, which is shorter than its diff:
```python
from functools import partial

import jax
import jax.numpy as jnp
from jax import lax
from jax.experimental import pallas as pl
from jax.experimental.pallas import tpu as pltpu
from jax.sharding import PartitionSpec as P

HEADS = 16
HEAD_DIM = 128
FEATURES = 2048
DEPTH_DIM = 1024
CODEBOOKS = 4
VOCAB = 1024
SEQ = 8
WIDE = 16
FRAMES = 256
LENGTH = SEQ * FRAMES
PAIR = 2 * HEAD_DIM


def attend_kernel(qkv_ref, out_ref):
    to_exp2 = HEAD_DIM ** (-0.5) * 1.4426950408889634
    row = lax.broadcasted_iota(jnp.int32, (FRAMES, FRAMES), 0)
    col = lax.broadcasted_iota(jnp.int32, (FRAMES, FRAMES), 1)
    for head in range(2):
        at = head * HEAD_DIM
        for block in range(SEQ):
            extent = (block + 1) * FRAMES
            first = block * FRAMES
            q = qkv_ref[first:extent, at : at + HEAD_DIM]
            diag = lax.dot_general(
                q,
                qkv_ref[first:extent, PAIR + at : PAIR + at + HEAD_DIM],
                (((1,), (1,)), ((), ())),
                preferred_element_type=jnp.float32,
            )
            diag = jnp.where(col <= row, diag, -jnp.inf)
            top = jnp.max(diag, axis=1, keepdims=True)
            if block:
                past = lax.dot_general(
                    q,
                    qkv_ref[:first, PAIR + at : PAIR + at + HEAD_DIM],
                    (((1,), (1,)), ((), ())),
                    preferred_element_type=jnp.float32,
                )
                top = jnp.maximum(top, jnp.max(past, axis=1, keepdims=True))
            weights = jnp.exp2((diag - top) * to_exp2)
            total = jnp.sum(weights, axis=1, keepdims=True)
            acc = jnp.dot(
                weights.astype(jnp.bfloat16),
                qkv_ref[first:extent, 2 * PAIR + at : 2 * PAIR + at + HEAD_DIM],
                preferred_element_type=jnp.float32,
            )
            if block:
                weights = jnp.exp2((past - top) * to_exp2)
                total = total + jnp.sum(weights, axis=1, keepdims=True)
                acc = acc + jnp.dot(
                    weights.astype(jnp.bfloat16),
                    qkv_ref[:first, 2 * PAIR + at : 2 * PAIR + at + HEAD_DIM],
                    preferred_element_type=jnp.float32,
                )
            out_ref[block, :, at : at + HEAD_DIM] = (acc / total).astype(jnp.bfloat16)


def attend(qkv):
    return pl.pallas_call(
        attend_kernel,
        out_shape=jax.ShapeDtypeStruct((SEQ, FRAMES, PAIR), jnp.bfloat16),
        in_specs=[pl.BlockSpec(memory_space=pltpu.VMEM)],
        out_specs=pl.BlockSpec(memory_space=pltpu.VMEM),
        compiler_params=pltpu.CompilerParams(vmem_limit_bytes=40 * 2**20),
        cost_estimate=pl.CostEstimate(
            flops=2 * 36 * FRAMES * FRAMES * HEAD_DIM * 4,
            bytes_accessed=LENGTH * PAIR * 8,
            transcendentals=2 * 36 * FRAMES * FRAMES,
        ),
    )(qkv)


def pack_kernel(queries, key_vectors, values, out):
    for kind, ref in enumerate((queries, key_vectors, values)):
        out[0, :, kind * PAIR : (kind + 1) * PAIR] = ref[0]


def pack(queries, key_vectors, values):
    return pl.pallas_call(
        pack_kernel,
        grid=(SEQ,),
        out_shape=jax.ShapeDtypeStruct((SEQ, FRAMES, 3 * PAIR), jnp.bfloat16),
        in_specs=[pl.BlockSpec((1, FRAMES, PAIR), lambda i: (0, 0, i))] * 3,
        out_specs=pl.BlockSpec((1, FRAMES, 3 * PAIR), lambda i: (i, 0, 0)),
        cost_estimate=pl.CostEstimate(flops=0, bytes_accessed=6 * 2**20, transcendentals=0),
    )(queries, key_vectors, values)


def depth_head(projected, embed, gain, heads, bias, target):
    mixed = projected + embed.astype(jnp.float32)
    scale = lax.rsqrt(jnp.mean(mixed * mixed, axis=1, keepdims=True) + 1e-05)
    hidden = (mixed * scale * gain).astype(jnp.bfloat16)
    logits = jnp.dot(hidden, heads, preferred_element_type=jnp.float32) + bias
    top = jnp.max(logits, axis=1, keepdims=True)
    shifted = jnp.exp(logits - top)
    total = jnp.sum(shifted, axis=1, keepdims=True)
    onehot = lax.broadcasted_iota(jnp.int32, (FRAMES, VOCAB), 1) == target
    picked = jnp.sum(jnp.where(onehot, logits, 0.0), axis=1, keepdims=True)
    losses = top + jnp.log(total) - picked
    dlogits = (shifted / total - onehot.astype(jnp.float32)).astype(jnp.bfloat16)
    return hidden, dlogits, losses


def depth_kernel(first, book, *refs):
    if first:
        (ctx_hbm, depth_hbm, embed_hbm, heads_hbm, gain, bias, target) = refs[:7]
        (projected, acts, losses, ctx, depth_in, embed, heads, sems) = refs[7:]
    else:
        (projected, embed_hbm, heads_hbm, gain, bias, target) = refs[:6]
        (acts, losses, embed, heads, sems) = refs[6:]
    copies = []

    def fetch(source, target_ref):
        copy = pltpu.make_async_copy(source, target_ref, sems.at[len(copies)])
        copy.start()
        copies.append(copy)
        return copy

    pieces = 4
    rows = FEATURES // pieces
    if first:
        ctx_copy = fetch(ctx_hbm, ctx)
        depth_copies = [
            fetch(
                depth_hbm.at[i * rows : (i + 1) * rows], depth_in.at[i * rows : (i + 1) * rows]
            )
            for i in range(pieces)
        ]
    book_copies = [
        (fetch(embed_hbm.at[book[0] + j], embed.at[j]), fetch(heads_hbm.at[book[0] + j], heads.at[j]))
        for j in range(2)
    ]
    if first:
        ctx_copy.wait()
        total = None
        for i in range(pieces):
            depth_copies[i].wait()
            for part in range(i * SEQ // pieces, (i + 1) * SEQ // pieces):
                term = jnp.dot(
                    ctx[part],
                    depth_in[part * PAIR : (part + 1) * PAIR],
                    preferred_element_type=jnp.float32,
                )
                total = term if total is None else total + term
        projected[...] = total
    lane = lax.broadcasted_iota(jnp.int32, (FRAMES, CODEBOOKS), 1)
    both = []
    for j in range(2):
        c = book[0] + j
        for copy in book_copies[j]:
            copy.wait()
        token = jnp.sum(jnp.where(lane == c, target[...], 0), axis=1, keepdims=True)
        hidden, dlogits, loss = depth_head(
            projected[...], embed[j], gain[c], heads[j], bias[c], token
        )
        acts[0, j] = hidden
        acts[1, j] = dlogits
        both.append(loss)
    pair_lane = lax.broadcasted_iota(jnp.int32, (FRAMES, 2), 1)
    losses[...] = jnp.where(pair_lane == 0, both[0], both[1])


def depth_call(first, outs, book, hbm_args, vmem_args):
    vmem = pl.BlockSpec(memory_space=pltpu.VMEM)
    anywhere = pl.BlockSpec(memory_space=pl.ANY)
    scratch = [
        pltpu.VMEM((2, FRAMES, DEPTH_DIM), jnp.bfloat16),
        pltpu.VMEM((2, DEPTH_DIM, VOCAB), jnp.bfloat16),
        pltpu.SemaphoreType.DMA((9 if first else 4,)),
    ]
    if first:
        scratch = [
            pltpu.VMEM((SEQ, FRAMES, PAIR), jnp.bfloat16),
            pltpu.VMEM((FEATURES, DEPTH_DIM), jnp.bfloat16),
        ] + scratch
    in_specs = [anywhere] * len(hbm_args) + [vmem] * len(vmem_args)
    if not first:
        in_specs[0] = vmem
    return pl.pallas_call(
        partial(depth_kernel, first),
        out_shape=outs,
        in_specs=[pl.BlockSpec(memory_space=pltpu.SMEM)] + in_specs,
        out_specs=(vmem,) * len(outs),
        scratch_shapes=scratch,
        compiler_params=pltpu.CompilerParams(vmem_limit_bytes=40 * 2**20),
        cost_estimate=pl.CostEstimate(
            flops=2 * 2 * FRAMES * DEPTH_DIM * VOCAB,
            bytes_accessed=8 * 2**20,
            transcendentals=2 * FRAMES * VOCAB,
        ),
    )(book.reshape(1), *hbm_args, *vmem_args)


def outer_kernel(mine, theirs, out):
    chunk = 128
    at = pl.multiple_of(pl.program_id(0) * chunk, chunk)
    both = []
    for j in range(2):
        total = None
        for acts in (mine, theirs):
            term = lax.dot_general(
                acts[0, j, :, pl.ds(at, chunk)],
                acts[1, j],
                (((0,), (0,)), ((), ())),
                preferred_element_type=jnp.float32,
            )
            total = term if total is None else total + term
        both.append(total.reshape(chunk // 8, 8, VOCAB))
    out[...] = jnp.concatenate(both, axis=1).astype(jnp.bfloat16)


def outer(mine, theirs):
    vmem = pl.BlockSpec(memory_space=pltpu.VMEM)
    return pl.pallas_call(
        outer_kernel,
        grid=(8,),
        out_shape=jax.ShapeDtypeStruct((SEQ * WIDE, 16, VOCAB), jnp.bfloat16),
        in_specs=[vmem] * 2,
        out_specs=pl.BlockSpec((16, 16, VOCAB), lambda i: (i, 0, 0)),
        compiler_params=pltpu.CompilerParams(vmem_limit_bytes=40 * 2**20),
        cost_estimate=pl.CostEstimate(
            flops=2 * 2 * 2 * FRAMES * DEPTH_DIM * VOCAB,
            bytes_accessed=8 * 2**20,
            transcendentals=0,
        ),
    )(mine, theirs)


def normalize(norm_gain, mixed_in):
    return (
        mixed_in
        * lax.rsqrt(jnp.mean(mixed_in * mixed_in, axis=-1, keepdims=True) + 1e-05)
        * norm_gain[:, None, :]
    )


def swap_wide(array, stride):
    return lax.ppermute(array, "wide", [(i, i ^ stride) for i in range(WIDE)])


def share_out(rows):
    place = lax.axis_index("wide")
    held = rows.reshape(2, 2, 2, 2, rows.shape[1])
    for axis, stride in enumerate((8, 4, 2, 1)):
        high = (place // stride) % 2 == 1
        low_part = lax.index_in_dim(held, 0, axis, keepdims=True)
        high_part = lax.index_in_dim(held, 1, axis, keepdims=True)
        kept = jnp.where(high, high_part, low_part)
        came = swap_wide(jnp.where(high, low_part, high_part), stride)
        held = jnp.concatenate(
            (jnp.where(high, came, kept), jnp.where(high, kept, came)), axis=axis
        )
    return held.reshape(WIDE, rows.shape[1])


def shards(
    queries, key_vectors, values, audio_codes, depth_in, code_embed, norm_gain, out_heads, out_bias
):
    core = lax.axis_index("wide") % 2
    qkv = lax.all_to_all(pack(queries, key_vectors, values), "seq", 0, 0, tiled=True)
    targets = share_out(audio_codes.reshape(WIDE, 64)).reshape(FRAMES, CODEBOOKS).T
    chosen = jnp.arange(VOCAB, dtype=jnp.int32) == targets[: CODEBOOKS - 1, :, None]
    looked = jnp.einsum(
        "cnv,cve->cne",
        chosen.astype(jnp.bfloat16),
        code_embed,
        preferred_element_type=jnp.float32,
    ).astype(jnp.bfloat16)
    looked = jnp.concatenate((jnp.zeros((1, FRAMES, DEPTH_DIM), jnp.bfloat16), looked), axis=0)
    heads = out_heads.transpose(1, 0, 2)
    qkv, looked, heads = lax.optimization_barrier((qkv, looked, heads))
    small = (norm_gain[:, None, :], out_bias[:, None, :], targets.T)

    context = lax.all_to_all(
        attend(qkv.reshape(LENGTH, 3 * PAIR)), "seq", 0, 0, tiled=True
    )
    mine = 2 * core
    other = 2 - mine
    acts_shape = jax.ShapeDtypeStruct((2, 2, FRAMES, DEPTH_DIM), jnp.bfloat16)
    losses_shape = jax.ShapeDtypeStruct((FRAMES, 2), jnp.float32)
    projected, acts_other, losses_other = depth_call(
        True,
        (jax.ShapeDtypeStruct((FRAMES, DEPTH_DIM), jnp.float32), acts_shape, losses_shape),
        other,
        (context, depth_in, looked, heads),
        small,
    )
    came = swap_wide(acts_other, 1)
    acts_mine, losses_mine = depth_call(
        False, (acts_shape, losses_shape), mine, (projected, looked, heads), small
    )
    shares = lax.all_to_all(outer(acts_mine, came), ("seq", "wide"), 0, 0, tiled=True)
    grad_scale = (VOCAB / (SEQ * WIDE * FRAMES)) ** 0.5
    summed = jnp.sum(shares.reshape(SEQ * WIDE // 2, 4, 8, VOCAB).astype(jnp.float32), axis=0)
    head_grads = summed.transpose(1, 0, 2) * grad_scale

    def in_order(of_mine, of_other):
        low = jnp.where(core == 0, of_mine, of_other)
        high = jnp.where(core == 0, of_other, of_mine)
        return jnp.concatenate((low, high), axis=0)

    dlogits = in_order(acts_mine[1], acts_other[1])
    pullback = jax.vjp(
        partial(normalize, norm_gain), projected[None] + looked.astype(jnp.float32)
    )[1]
    dhidden = jnp.einsum("cnv,cev->cne", dlogits, heads, preferred_element_type=jnp.float32)
    dmixed = pullback(dhidden)[0]
    dprojected = jnp.sum(dmixed, axis=0).astype(jnp.bfloat16)
    context_grad = lax.dot_general(
        dprojected, depth_in, (((1,), (1,)), ((), ())), preferred_element_type=jnp.float32
    ).astype(jnp.bfloat16)
    losses = jnp.where(
        core == 0,
        jnp.concatenate((losses_mine, losses_other), axis=1),
        jnp.concatenate((losses_other, losses_mine), axis=1),
    )
    losses, context_grad = lax.optimization_barrier((losses, context_grad))
    frame_losses = share_out(losses.reshape(WIDE, 64)).reshape(WIDE, 16, CODEBOOKS)
    return (frame_losses, context_grad.reshape(1, FRAMES, FEATURES), head_grads)


def solution(mesh):
    return jax.shard_map(
        shards,
        mesh=mesh,
        in_specs=(
            P("wide", "seq", None),
            P("wide", "seq", None),
            P("wide", "seq", None),
            P(None, ("seq", "wide"), None),
            P(),
            P(),
            P(),
            P(),
            P(),
        ),
        out_specs=(
            P(None, ("seq", "wide"), None),
            P("wide", "seq", None),
            P(("seq", "wide"), None, None),
        ),
        check_vma=False,
    )
```

time: 224 us -> 194 us (0.87)
  blocking collectives: 133 us -> 0 us
  waiting for transfers between devices: 3.65 us -> 81.6 us
  starting transfers between devices: 11.5 us -> 39.3 us
  Pallas kernels: 8.94 us -> 29 us
  matrix products: 29.4 us -> 12.4 us
  other arithmetic: 8.89 us -> 6.24 us
    all_gather x2 -> x0, blocking collectives: 86 us -> none  [the longest x1 61.2 us: shards(): all_losses = lax.all_gather(losses.T.reshape(WIDE, 64), 'wide', axis=0)]
    all_to_all x1 -> x0, blocking collectives: 46.9 us -> none  [shards(): lax.all_to_all(packed, 'seq', 0, 0, tiled=True).reshape(LENGTH, 3 * PAIR)]
    ppermute x2 -> x9, waiting for transfers between devices: 3.65 us -> 50.1 us  [swap_wide(): return lax.ppermute(array, 'wide', [(i, i ^ stride) for i in range(WIDE)])]
    all_to_all x2 -> x3, waiting for transfers between devices: 0.01 us -> 31.6 us  [the longest x1 16.6 us: shards(): lax.all_to_all(attend(qkv.reshape(LENGTH, 3 * PAIR)), 'seq', 0, 0, tiled=...]
    pallas_call x1 -> x5, Pallas kernels: 8.94 us -> 29 us  [the longest x1 11.1 us: attend(): pl.pallas_call(attend_kernel, out_shape=jax.ShapeDtypeStruct((SEQ, FRAMES...]
    all_to_all x2 -> x3, starting transfers between devices: 11 us -> 29.8 us  [the longest x1 14.8 us: shards(): lax.all_to_all(attend(qkv.reshape(LENGTH, 3 * PAIR)), 'seq', 0, 0, tiled=...]
    unnamed x21 -> x33, local copies, waits for them, and re-layouts: 7.86 us -> 21.5 us
    gather x1 -> x0, local copies, waits for them, and re-layouts: 11.3 us -> none  [shards(): code_embed[jnp.arange(CODEBOOKS - 1)[:, None], targets.T[:CODEBOOKS - 1]]]
  transfers between devices with their start and end apart: 4 -> 12, of which waited for: 2 -> 10; matrix products, arithmetic and copies ran while one was open for 13% -> 14% of each run, Pallas kernels for 0% -> 2%
where the time goes in v2:
time: 194 us; the launch traced here: 193 us
  waiting for transfers between devices  81.6 us (42%)
  starting transfers between devices  39.3 us (20%)
  Pallas kernels  29 us (15%)
  local copies, waits for them, and re-layouts  23.1 us (12%)
  matrix products  12.4 us (6%)
  other arithmetic  6.24 us (3%)
    ppermute x9, waiting for transfers between devices, swap_wide(): return lax.ppermute(array, 'wide', [(i, i ^ stride) for i in range(WIDE)])  50.1 us
    unnamed x33, local copies, waits for them, and re-layouts  21.5 us
    all_to_all x1, waiting for transfers between devices, shards(): lax.all_to_all(attend(qkv.reshape(LENGTH, 3 * PAIR)), 'seq', 0, 0, tiled=...  16.6 us
    all_to_all x1, waiting for transfers between devices, shards(): lax.all_to_all(pack(queries, key_vectors, values), 'seq', 0, 0, tiled=True)  14.9 us
    all_to_all x1, starting transfers between devices, shards(): lax.all_to_all(attend(qkv.reshape(LENGTH, 3 * PAIR)), 'seq', 0, 0, tiled=...  14.8 us
    pallas_call x1, Pallas kernels, attend(): pl.pallas_call(attend_kernel, out_shape=jax.ShapeDtypeStruct((SEQ, FRAMES...  11.1 us
    ppermute x9, starting transfers between devices, swap_wide(): return lax.ppermute(array, 'wide', [(i, i ^ stride) for i in range(WIDE)])  9.53 us
    all_to_all x1, starting transfers between devices, shards(): lax.all_to_all(pack(queries, key_vectors, values), 'seq', 0, 0, tiled=True)  8.27 us
  transfers between devices with their start and end apart: 12, of which 10 were waited for; matrix products, arithmetic and copies ran while one was open for 14% of the time, Pallas kernels for 2%

profile of v2, /device:TPU:2, one launch (start us, length us, event | category | flops | bytes accessed | tf_op | source)
XLA Modules:
  0.0 192.7 jit_solution(14705339731328617958)
XLA Ops:
  0.6 6.3 %shard_map.112 = bf16[8,256,768]{2,1,0:T(8,128)(2,1)} custom-call(bf16[1,256,2048]{2,1,0:T(8,128)(2,1)} %queries.1, bf16[1,256,2048]{2,1,0:T(8,128)(2,1)} %key_vectors.1, bf16[1,256,2048]{2,1,0:T(8,128)(2,1)} %values.1), custom_call_target="tpu_custom_call" | custom-call | bytes 6291456 | tf_op jit(solution)/shard_map/pallas_call | solution.py:88
  6.9 8.3 %all-to-all-start = ((bf16[8,256,768]{2,1,0:T(8,128)(2,1)}), bf16[8,256,768]{2,1,0:T(8,128)(2,1)}, u32[]{:S(2)}, u32[]{:S(2)}) async-start(bf16[8,256,768]{2,1,0:T(8,128)(2,1)} %shard_map.112), calls=%async_computation | async-start | bytes 6291456 | tf_op jit(solution)/shard_map/all_to_all | solution.py:269
  15.4 3.3 %collective-permute-start = (s32[1,2,2,2,64]{4,3,2,1,0:T(2,128)S(1)}, s32[1,2,2,2,64]{4,3,2,1,0:T(2,128)S(1)}, u32[]{:S(2)}, u32[]{:S(2)}) collective-permute-start(s32[1,2,2,2,64]{4,3,2,1,0:T(2,128)S(1)} %select_n.285), channel_id=1, source_target_pairs={{0,8},{1,9},{2,10},{3,11},{4,12},{5,13},{6,14},{7,15},{8,0},{9,1},... | collective-permute-start | bytes 6152 | tf_op jit(solution)/shard_map/ppermute | solution.py:247
  18.9 1.7 collective-permute-done
  20.6 1.7 collective-permute-start.1
  22.3 2.0 %collective-permute-done.1 = s32[2,1,2,2,64]{4,3,2,1,0:T(2,128)S(1)} collective-permute-done((s32[2,1,2,2,64]{4,3,2,1,0:T(2,128)S(1)}, s32[2,1,2,2,64]{4,3,2,1,0:T(2,128)S(1)}, u32[]{:S(2)}, u32[]{:S(2)}) %collective-permute-start.1) | collective-permute-done | bytes 2080 | tf_op jit(solution)/shard_map/ppermute | solution.py:247
  24.3 1.1 collective-permute-start.2
  25.4 3.0 %collective-permute-done.2 = s32[2,2,1,2,64]{4,3,2,1,0:T(2,128)S(1)} collective-permute-done((s32[2,2,1,2,64]{4,3,2,1,0:T(2,128)S(1)}, s32[2,2,1,2,64]{4,3,2,1,0:T(2,128)S(1)}, u32[]{:S(2)}, u32[]{:S(2)}) %collective-permute-start.2) | collective-permute-done | bytes 2080 | tf_op jit(solution)/shard_map/ppermute | solution.py:247
  28.5 9.5 %copy.32 = bf16[1024,4,1024]{2,0,1:T(8,128)(2,1)} copy(bf16[1024,4,1024]{2,1,0:T(4,128)(2,1)} %param.16) | data formatting | bytes 16777216 | tf_op args[7]
  38.3 4.6 %fusion.6 = bf16[3,256,1024]{2,1,0:T(8,128)(2,1)S(1)} fusion(bf16[3,1024,1024]{2,1,0:T(8,128)(2,1)} %param.14, s32[3,256]{1,0:T(4,128)S(1)} %copy.21), kind=kOutput, calls=%fused_computation.14 | convolution fusion | flops 1612185600 | bytes 7867392 | tf_op jit(solution)/shard_map/cnv,cve->cne/dot_general | solution.py:272
  43.2 14.9 %all-to-all-done = bf16[8,256,768]{2,1,0:T(8,128)(2,1)} async-done(((bf16[8,256,768]{2,1,0:T(8,128)(2,1)}), bf16[8,256,768]{2,1,0:T(8,128)(2,1)}, u32[]{:S(2)}, u32[]{:S(2)}) %all-to-all-start) | async-done | bytes 3145760 | tf_op jit(solution)/shard_map/all_to_all | solution.py:269
  58.1 11.1 %shard_map.113 = bf16[8,256,256]{2,1,0:T(8,128)(2,1)S(1)} custom-call(bf16[2048,768]{1,0:T(8,128)(2,1)} %bitcast.4.qkv_ref), custom_call_target="tpu_custom_call" | custom-call | flops 2415919104 | bytes 4194304 | tf_op jit(solution)/shard_map/pallas_call | solution.py:68
  70.1 14.8 %all-to-all-start.1 = ((bf16[8,256,256]{2,1,0:T(8,128)(2,1)}), bf16[8,256,256]{2,1,0:T(8,128)(2,1)S(1)}, u32[]{:S(2)}, u32[]{:S(2)}) async-start(bf16[8,256,256]{2,1,0:T(8,128)(2,1)} %copy-done.6), calls=%async_computation.1 | async-start | bytes 2097152 | tf_op jit(solution)/shard_map/all_to_all | solution.py:283
  85.0 16.6 %all-to-all-done.1.refs_0_ = bf16[8,256,256]{2,1,0:T(8,128)(2,1)S(1)} async-done(((bf16[8,256,256]{2,1,0:T(8,128)(2,1)}), bf16[8,256,256]{2,1,0:T(8,128)(2,1)S(1)}, u32[]{:S(2)}, u32[]{:S(2)}) %all-to-all-start.1) | async-done | bytes 1048608 | tf_op jit(solution)/shard_map/all_to_all | solution.py:283
  102.6 2.3 %copy-done.2 = bf16[2048,1024]{1,0:T(8,128)(2,1)S(1)} copy-done((bf16[2048,1024]{1,0:T(8,128)(2,1)S(1)}, bf16[2048,1024]{1,0:T(8,128)(2,1)}, u32[]{:S(2)}) %copy-start.2) | copy-done | bytes 4194328
  105.0 1.4 copy-done.5
  106.4 4.8 %shard_map.114 = (f32[256,1024]{1,0:T(8,128)S(1)}, bf16[2,2,256,1024]{3,2,1,0:T(8,128)(2,1)S(1)}, f32[256,2]{1,0:T(8,128)S(1)}) custom-call(s32[1]{0:T(128)} %bitcast.1.book, bf16[8,256,256]{2,1,0:T(8,128)(2,1)S(1)} %copy-done.5, bf16[2048,1024]{1,0:T(8,128)(2,1)S(1)} %copy-done.2, bf16[4,256,1024]{2,1,0:T(8,128)(2,1)S(1)} %concatenate.40.refs_2_.refs_1_, ...), custom_call_target="tpu_custom_call" | custom-call | flops 1073741824 | bytes 8388608 | tf_op jit(solution)/shard_map/pallas_call | solution.py:188
  111.4 3.0 %shard_map.115 = (bf16[2,2,256,1024]{3,2,1,0:T(8,128)(2,1)S(1)}, f32[256,2]{1,0:T(8,128)S(1)}) custom-call(s32[1]{0:T(128)} %bitcast.book, f32[256,1024]{1,0:T(8,128)S(1)} %get-tuple-element.16.refs_0_, bf16[4,256,1024]{2,1,0:T(8,128)(2,1)S(1)} %concatenate.40.refs_2_.refs_1_, bf16[4,1024,1024]{2,1,0:T(8,128)(2,1)S(1)} %bitcast.25, ...), custom_call_target="tpu_custom_call" | custom-call | flops 1073741824 | bytes 8388608 | tf_op jit(solution)/shard_map/pallas_call | solution.py:188
  115.5 3.9 %shard_map.116 = bf16[128,16,1024]{2,1,0:T(8,128)(2,1)S(1)} custom-call(bf16[2,2,256,1024]{3,2,1,0:T(8,128)(2,1)S(1)} %get-tuple-element.19.mine, bf16[2,2,256,1024]{3,2,1,0:T(8,128)(2,1)S(1)} %collective-permute-done.8.theirs), custom_call_target="tpu_custom_call" | custom-call | flops 2147483648 | bytes 8388608 | tf_op jit(solution)/shard_map/pallas_call | solution.py:223
  119.4 2.0 %copy-done = bf16[128,16,1024]{2,1,0:T(8,128)(2,1)} copy-done((bf16[128,16,1024]{2,1,0:T(8,128)(2,1)}, bf16[128,16,1024]{2,1,0:T(8,128)(2,1)S(1)}, u32[]{:S(2)}) %copy-start) | copy-done | bytes 4194328
  121.4 1.3 copy-done.1
  122.7 6.7 %all-to-all-start.2 = ((bf16[128,16,1024]{2,1,0:T(8,128)(2,1)}), bf16[128,16,1024]{2,1,0:T(8,128)(2,1)}, u32[]{:S(2)}, u32[]{:S(2)}) async-start(bf16[128,16,1024]{2,1,0:T(8,128)(2,1)} %copy-done), calls=%async_computation.2 | async-start | bytes 8388608 | tf_op jit(solution)/shard_map/all_to_all | solution.py:301
  129.6 1.7 select_bitcast_fusion.1
  131.3 5.5 %multiply_reduce_fusion.1 = (f32[4,256]{1,0:T(4,128)S(1)}, f32[4,256]{1,0:T(4,128)S(1)}, f32[4,256,1024]{2,1,0:T(8,128)S(1)}) fusion(bf16[4,256,1024]{2,1,0:T(8,128)(2,1)S(1)} %concatenate.40.refs_2_.refs_1_, f32[256,1024]{1,0:T(8,128)S(1)} %get-tuple-element.16.refs_0_, f32[4,1024]{1,0:T(4,128)S(1)} %copy-done.10, bf16[4,1024,1024]{2,1,0:T(8,128)(2,1)} %bitcast.22, ...), kind=kOutput, calls=%fused_computation.5 | convolution fusion | flops 2155870208 | bytes 17850368 | tf_op jit(solution)/shard_map/cnv,cev->cne/dot_general | solution.py:315
  136.8 1.3 fusion
  139.0 2.3 %convolution_convert_fusion = bf16[256,2048]{1,0:T(8,128)(2,1)} fusion(bf16[2048,1024]{1,0:T(8,128)(2,1)S(1)} %copy-done.3, bf16[256,1024]{1,0:T(8,128)(2,1)S(1)} %fusion), kind=kOutput, calls=%fused_computation.9 | convolution fusion | flops 1074266112 | bytes 5767168 | tf_op jit(solution)/shard_map/dot_general | solution.py:318
  141.4 3.1 %collective-permute-start.4 = (f32[1,2,2,2,64]{4,3,2,1,0:T(2,128)S(1)}, f32[1,2,2,2,64]{4,3,2,1,0:T(2,128)S(1)}, u32[]{:S(2)}, u32[]{:S(2)}) collective-permute-start(f32[1,2,2,2,64]{4,3,2,1,0:T(2,128)S(1)} %select_n.309), channel_id=1, source_target_pairs={{0,8},{1,9},{2,10},{3,11},{4,12},{5,13},{6,14},{7,15},{8,0},{9,1},... | collective-permute-start | bytes 6152 | tf_op jit(solution)/shard_map/ppermute | solution.py:247
  144.7 34.5 %collective-permute-done.4 = f32[1,2,2,2,64]{4,3,2,1,0:T(2,128)S(1)} collective-permute-done((f32[1,2,2,2,64]{4,3,2,1,0:T(2,128)S(1)}, f32[1,2,2,2,64]{4,3,2,1,0:T(2,128)S(1)}, u32[]{:S(2)}, u32[]{:S(2)}) %collective-permute-start.4) | collective-permute-done | bytes 2080 | tf_op jit(solution)/shard_map/ppermute | solution.py:247
  179.4 3.6 %collective-permute-done.5 = f32[2,1,2,2,64]{4,3,2,1,0:T(2,128)S(1)} collective-permute-done((f32[2,1,2,2,64]{4,3,2,1,0:T(2,128)S(1)}, f32[2,1,2,2,64]{4,3,2,1,0:T(2,128)S(1)}, u32[]{:S(2)}, u32[]{:S(2)}) %collective-permute-start.5) | collective-permute-done | bytes 2080 | tf_op jit(solution)/shard_map/ppermute | solution.py:247
  183.1 3.6 %collective-permute-done.6 = f32[2,2,1,2,64]{4,3,2,1,0:T(2,128)S(1)} collective-permute-done((f32[2,2,1,2,64]{4,3,2,1,0:T(2,128)S(1)}, f32[2,2,1,2,64]{4,3,2,1,0:T(2,128)S(1)}, u32[]{:S(2)}, u32[]{:S(2)}) %collective-permute-start.6) | collective-permute-done | bytes 2080 | tf_op jit(solution)/shard_map/ppermute | solution.py:247
  186.8 1.2 collective-permute-done.7
  188.9 3.0 %convert_reduce_fusion = f32[4,8,1024]{2,1,0:T(8,128)S(1)} fusion(bf16[64,4,8,1024]{3,2,1,0:T(8,128)(2,1)} %bitcast.10), kind=kLoop, calls=%fused_computation | loop fusion | flops 4161536 | bytes 4325376 | tf_op jit(solution)/shard_map/reduce_sum | solution.py:303
  (74 shorter events, 7.7 us)
Async XLA Ops:
  6.9 8.3 %copy-start.11 = (s32[16,16,4]{1,2,0:T(4,128)S(1)}, s32[16,16,4]{1,2,0:T(4,128)}, u32[]{:S(2)}) copy-start(s32[16,16,4]{1,2,0:T(4,128)} %param.12) | copy-start | bytes 12292
  6.9 51.2 %all-to-all-start = ((bf16[8,256,768]{2,1,0:T(8,128)(2,1)}), bf16[8,256,768]{2,1,0:T(8,128)(2,1)}, u32[]{:S(2)}, u32[]{:S(2)}) async-start(bf16[8,256,768]{2,1,0:T(8,128)(2,1)} %shard_map.112), calls=%async_computation | async-start | bytes 6291456 | tf_op jit(solution)/shard_map/all_to_all | solution.py:269
  15.4 5.2 %collective-permute-start = (s32[1,2,2,2,64]{4,3,2,1,0:T(2,128)S(1)}, s32[1,2,2,2,64]{4,3,2,1,0:T(2,128)S(1)}, u32[]{:S(2)}, u32[]{:S(2)}) collective-permute-start(s32[1,2,2,2,64]{4,3,2,1,0:T(2,128)S(1)} %select_n.285), channel_id=1, source_target_pairs={{0,8},{1,9},{2,10},{3,11},{4,12},{5,13},{6,14},{7,15},{8,0},{9,1},... | collective-permute-start | bytes 6152 | tf_op jit(solution)/shard_map/ppermute | solution.py:247
  20.6 3.7 %collective-permute-start.1 = (s32[2,1,2,2,64]{4,3,2,1,0:T(2,128)S(1)}, s32[2,1,2,2,64]{4,3,2,1,0:T(2,128)S(1)}, u32[]{:S(2)}, u32[]{:S(2)}) collective-permute-start(s32[2,1,2,2,64]{4,3,2,1,0:T(2,128)S(1)} %broadcast_select_fusion.19), channel_id=1, source_target_pairs={{0,4},{1,5},{2,6},{3,7},{4,0},{5,1},{6,2},{7,3},{8,12},{9,13},{10,... | collective-permute-start | bytes 6152 | tf_op jit(solution)/shard_map/ppermute | solution.py:247
  24.3 4.1 %collective-permute-start.2 = (s32[2,2,1,2,64]{4,3,2,1,0:T(2,128)S(1)}, s32[2,2,1,2,64]{4,3,2,1,0:T(2,128)S(1)}, u32[]{:S(2)}, u32[]{:S(2)}) collective-permute-start(s32[2,2,1,2,64]{4,3,2,1,0:T(2,128)S(1)} %broadcast_select_fusion.27), channel_id=1, source_target_pairs={{0,2},{1,3},{2,0},{3,1},{4,6},{5,7},{6,4},{7,5},{8,10},{9,11},{10,... | collective-permute-start | bytes 6152 | tf_op jit(solution)/shard_map/ppermute | solution.py:247
  28.4 9.6 %collective-permute-start.3 = (s32[2,2,2,1,64]{4,3,2,1,0:T(1,128)S(1)}, s32[2,2,2,1,64]{4,3,2,1,0:T(1,128)S(1)}, u32[]{:S(2)}, u32[]{:S(2)}) collective-permute-start(s32[2,2,2,1,64]{4,3,2,1,0:T(1,128)S(1)} %get-tuple-element.33), channel_id=1, source_target_pairs={{0,1},{1,0},{2,3},{3,2},{4,5},{5,4},{6,7},{7,6},{8,9},{9,8},{10,11... | collective-permute-start | bytes 6152 | tf_op jit(solution)/shard_map/ppermute | solution.py:247
  58.1 26.9 %copy-start.12 = (f32[4,1024]{1,0:T(4,128)S(1)}, f32[4,1024]{1,0:T(4,128)}, u32[]{:S(2)}) copy-start(f32[4,1024]{1,0:T(4,128)} %param.17) | copy-start | bytes 49156
  58.1 26.9 %copy-start.10 = (f32[4,1024]{1,0:T(4,128)S(1)}, f32[4,1024]{1,0:T(4,128)}, u32[]{:S(2)}) copy-start(f32[4,1024]{1,0:T(4,128)} %param.15) | copy-start | bytes 49156
  69.2 1.0 copy-start.6
  70.1 31.5 %all-to-all-start.1 = ((bf16[8,256,256]{2,1,0:T(8,128)(2,1)}), bf16[8,256,256]{2,1,0:T(8,128)(2,1)S(1)}, u32[]{:S(2)}, u32[]{:S(2)}) async-start(bf16[8,256,256]{2,1,0:T(8,128)(2,1)} %copy-done.6), calls=%async_computation.1 | async-start | bytes 2097152 | tf_op jit(solution)/shard_map/all_to_all | solution.py:283
  101.7 1.0 copy-start.4
  102.6 8.7 %slice-start = ((s8[8388608]{0:T(1024)(128)(4,1)}), s8[4194304]{0:T(1024)(128)(4,1)S(1)}, s32[]{:S(2)}) async-start(s8[8388608]{0:T(1024)(128)(4,1)} %bitcast.23), calls=%async_computation.3 | async-start | bytes 8388608
  102.6 2.3 %copy-start.2 = (bf16[2048,1024]{1,0:T(8,128)(2,1)S(1)}, bf16[2048,1024]{1,0:T(8,128)(2,1)}, u32[]{:S(2)}) copy-start(bf16[2048,1024]{1,0:T(8,128)(2,1)} %refs_1_.1) | copy-start | bytes 12582916
  105.0 1.4 copy-start.5
  106.4 5.0 %slice-start.1 = ((s8[8388608]{0:T(1024)(128)(4,1)}), s8[4194304]{0:T(1024)(128)(4,1)S(1)}, s32[]{:S(2)}) async-start(s8[8388608]{0:T(1024)(128)(4,1)} %bitcast.23), calls=%async_computation.4 | async-start | bytes 8388608
  111.2 3.1 %copy-start.7 = (bf16[2,2,256,1024]{3,2,1,0:T(8,128)(2,1)}, bf16[2,2,256,1024]{3,2,1,0:T(8,128)(2,1)S(1)}, u32[]{:S(2)}) copy-start(bf16[2,2,256,1024]{3,2,1,0:T(8,128)(2,1)S(1)} %get-tuple-element.20) | copy-start | bytes 6291460
  111.2 4.2 %collective-permute-start.8 = (bf16[2,2,256,1024]{3,2,1,0:T(8,128)(2,1)S(1)}, bf16[2,2,256,1024]{3,2,1,0:T(8,128)(2,1)S(1)}, u32[]{:S(2)}, u32[]{:S(2)}) collective-permute-start(bf16[2,2,256,1024]{3,2,1,0:T(8,128)(2,1)S(1)} %get-tuple-element.20), channel_id=1, source_target_pairs={{0,1},{1,0},{2,3},{3,2},{4,5},{5,4},{6,7},{7,6},{8,9},{9,8},{10,11... | collective-permute-start | bytes 6291464 | tf_op jit(solution)/shard_map/ppermute | solution.py:247
  114.3 0.7 copy-start.8
  119.4 2.0 %copy-start = (bf16[128,16,1024]{2,1,0:T(8,128)(2,1)}, bf16[128,16,1024]{2,1,0:T(8,128)(2,1)S(1)}, u32[]{:S(2)}) copy-start(bf16[128,16,1024]{2,1,0:T(8,128)(2,1)S(1)} %shard_map.116) | copy-start | bytes 12582916
  121.4 1.3 copy-start.1
  122.7 6.8 %copy-start.9 = (f32[256,2]{1,0:T(8,128)S(1)}, f32[256,2]{1,0:T(8,128)}, u32[]{:S(2)}) copy-start(f32[256,2]{1,0:T(8,128)} %copy-done.8) | copy-start | bytes 6148
  122.7 66.2 %all-to-all-start.2 = ((bf16[128,16,1024]{2,1,0:T(8,128)(2,1)}), bf16[128,16,1024]{2,1,0:T(8,128)(2,1)}, u32[]{:S(2)}, u32[]{:S(2)}) async-start(bf16[128,16,1024]{2,1,0:T(8,128)(2,1)} %copy-done), calls=%async_computation.2 | async-start | bytes 8388608 | tf_op jit(solution)/shard_map/all_to_all | solution.py:301
  136.8 2.2 %copy-start.3 = (bf16[2048,1024]{1,0:T(8,128)(2,1)S(1)}, bf16[2048,1024]{1,0:T(8,128)(2,1)}, u32[]{:S(2)}) copy-start(bf16[2048,1024]{1,0:T(8,128)(2,1)} %refs_1_.1) | copy-start | bytes 12582916
  141.4 37.8 %collective-permute-start.4 = (f32[1,2,2,2,64]{4,3,2,1,0:T(2,128)S(1)}, f32[1,2,2,2,64]{4,3,2,1,0:T(2,128)S(1)}, u32[]{:S(2)}, u32[]{:S(2)}) collective-permute-start(f32[1,2,2,2,64]{4,3,2,1,0:T(2,128)S(1)} %select_n.309), channel_id=1, source_target_pairs={{0,8},{1,9},{2,10},{3,11},{4,12},{5,13},{6,14},{7,15},{8,0},{9,1},... | collective-permute-start | bytes 6152 | tf_op jit(solution)/shard_map/ppermute | solution.py:247
  179.3 3.7 %collective-permute-start.5 = (f32[2,1,2,2,64]{4,3,2,1,0:T(2,128)S(1)}, f32[2,1,2,2,64]{4,3,2,1,0:T(2,128)S(1)}, u32[]{:S(2)}, u32[]{:S(2)}) collective-permute-start(f32[2,1,2,2,64]{4,3,2,1,0:T(2,128)S(1)} %broadcast_select_fusion.15), channel_id=1, source_target_pairs={{0,4},{1,5},{2,6},{3,7},{4,0},{5,1},{6,2},{7,3},{8,12},{9,13},{10,... | collective-permute-start | bytes 6152 | tf_op jit(solution)/shard_map/ppermute | solution.py:247
  183.0 3.7 %collective-permute-start.6 = (f32[2,2,1,2,64]{4,3,2,1,0:T(2,128)S(1)}, f32[2,2,1,2,64]{4,3,2,1,0:T(2,128)S(1)}, u32[]{:S(2)}, u32[]{:S(2)}) collective-permute-start(f32[2,2,1,2,64]{4,3,2,1,0:T(2,128)S(1)} %broadcast_select_fusion.23), channel_id=1, source_target_pairs={{0,2},{1,3},{2,0},{3,1},{4,6},{5,7},{6,4},{7,5},{8,10},{9,11},{10,... | collective-permute-start | bytes 6152 | tf_op jit(solution)/shard_map/ppermute | solution.py:247
  186.7 1.2 collective-permute-start.7

commit v3 on v2

v3 whole, which is shorter than its diff:
```python
from functools import partial

import jax
import jax.numpy as jnp
from jax import lax
from jax.experimental import pallas as pl
from jax.experimental.pallas import tpu as pltpu
from jax.sharding import PartitionSpec as P

HEADS = 16
HEAD_DIM = 128
FEATURES = 2048
DEPTH_DIM = 1024
CODEBOOKS = 4
VOCAB = 1024
SEQ = 8
WIDE = 16
FRAMES = 256
LENGTH = SEQ * FRAMES
PAIR = 2 * HEAD_DIM


def attend_kernel(qkv, out_hbm, out, out_sems):
    stores = [
        pltpu.make_async_copy(out.at[i], out_hbm.at[i], out_sems.at[i]) for i in range(SEQ)
    ]
    to_exp2 = HEAD_DIM ** (-0.5) * 1.4426950408889634
    row = lax.broadcasted_iota(jnp.int32, (FRAMES, FRAMES), 0)
    col = lax.broadcasted_iota(jnp.int32, (FRAMES, FRAMES), 1)
    across = (((1,), (1,)), ((), ()))
    for block in range(SEQ):
        for head in range(2):
            at = head * HEAD_DIM
            q = qkv[block, :, at : at + HEAD_DIM]
            diag = lax.dot_general(
                q,
                qkv[block, :, PAIR + at : PAIR + at + HEAD_DIM],
                across,
                preferred_element_type=jnp.float32,
            )
            diag = jnp.where(col <= row, diag, -jnp.inf)
            top = jnp.max(diag, axis=1, keepdims=True)
            if block:
                keys = qkv[:block, :, PAIR + at : PAIR + at + HEAD_DIM]
                past = lax.dot_general(
                    q,
                    keys.reshape(block * FRAMES, HEAD_DIM),
                    across,
                    preferred_element_type=jnp.float32,
                )
                top = jnp.maximum(top, jnp.max(past, axis=1, keepdims=True))
            weights = jnp.exp2((diag - top) * to_exp2)
            total = jnp.sum(weights, axis=1, keepdims=True)
            acc = jnp.dot(
                weights.astype(jnp.bfloat16),
                qkv[block, :, 2 * PAIR + at : 2 * PAIR + at + HEAD_DIM],
                preferred_element_type=jnp.float32,
            )
            if block:
                weights = jnp.exp2((past - top) * to_exp2)
                total = total + jnp.sum(weights, axis=1, keepdims=True)
                vals = qkv[:block, :, 2 * PAIR + at : 2 * PAIR + at + HEAD_DIM]
                acc = acc + jnp.dot(
                    weights.astype(jnp.bfloat16),
                    vals.reshape(block * FRAMES, HEAD_DIM),
                    preferred_element_type=jnp.float32,
                )
            out[block, :, at : at + HEAD_DIM] = (acc / total).astype(jnp.bfloat16)
        stores[block].start()
    for copy in stores:
        copy.wait()


HBM = pl.BlockSpec(memory_space=pltpu.HBM)
VMEM = pl.BlockSpec(memory_space=pltpu.VMEM)
SMEM = pl.BlockSpec(memory_space=pltpu.SMEM)
GRANT = 60 * 2**20
DEPTH_GRANT = 50 * 2**20


def attend(qkv):
    return pl.pallas_call(
        attend_kernel,
        out_shape=pltpu.HBM((SEQ, FRAMES, PAIR), jnp.bfloat16),
        in_specs=[VMEM],
        out_specs=HBM,
        scratch_shapes=[
            pltpu.VMEM((SEQ, FRAMES, PAIR), jnp.bfloat16),
            pltpu.SemaphoreType.DMA((SEQ,)),
        ],
        compiler_params=pltpu.CompilerParams(vmem_limit_bytes=40 * 2**20),
        cost_estimate=pl.CostEstimate(
            flops=2 * 36 * FRAMES * FRAMES * HEAD_DIM * 4,
            bytes_accessed=LENGTH * PAIR * 8,
            transcendentals=2 * 36 * FRAMES * FRAMES,
        ),
    )(qkv)


def pack_kernel(queries, key_vectors, values, out, held, in_sems, out_sems):
    rows = FRAMES // 4
    sources = (queries, key_vectors, values)
    loads = [
        [
            pltpu.make_async_copy(
                ref.at[0, i * rows : (i + 1) * rows],
                held.at[kind, i * rows : (i + 1) * rows],
                in_sems.at[i, kind],
            )
            for kind, ref in enumerate(sources)
        ]
        for i in range(4)
    ]
    for group in loads:
        for copy in group:
            copy.start()
    stores = []
    for i in range(4):
        for kind in range(3):
            loads[i][kind].wait()
            for part in range(SEQ):
                copy = pltpu.make_async_copy(
                    held.at[kind, i * rows : (i + 1) * rows, part * PAIR : (part + 1) * PAIR],
                    out.at[part, i * rows : (i + 1) * rows, kind * PAIR : (kind + 1) * PAIR],
                    out_sems.at[i, kind, part],
                )
                copy.start()
                stores.append(copy)
    for copy in stores:
        copy.wait()


def pack(queries, key_vectors, values):
    return pl.pallas_call(
        pack_kernel,
        out_shape=pltpu.HBM((SEQ, FRAMES, 3 * PAIR), jnp.bfloat16),
        in_specs=[HBM] * 3,
        out_specs=HBM,
        scratch_shapes=[
            pltpu.VMEM((3, FRAMES, FEATURES), jnp.bfloat16),
            pltpu.SemaphoreType.DMA((4, 3)),
            pltpu.SemaphoreType.DMA((4, 3, SEQ)),
        ],
        compiler_params=pltpu.CompilerParams(vmem_limit_bytes=GRANT),
        cost_estimate=pl.CostEstimate(flops=0, bytes_accessed=6 * 2**20, transcendentals=0),
    )(queries, key_vectors, values)


def lookup_kernel(target, table_hbm, out_hbm, table, out, in_sems, out_sems):
    books = CODEBOOKS - 1
    loads = [
        pltpu.make_async_copy(table_hbm.at[c], table.at[c], in_sems.at[c]) for c in range(books)
    ]
    stores = [
        pltpu.make_async_copy(out.at[c], out_hbm.at[c], out_sems.at[c])
        for c in range(CODEBOOKS)
    ]
    for copy in loads:
        copy.start()
    out[0] = jnp.zeros((FRAMES, DEPTH_DIM), jnp.bfloat16)
    stores[0].start()
    for c in range(books):
        loads[c].wait()
        chosen = lax.broadcasted_iota(jnp.int32, (FRAMES, VOCAB), 1) == target[:, c : c + 1]
        out[c + 1] = jnp.dot(
            chosen.astype(jnp.float32).astype(jnp.bfloat16),
            table[c],
            preferred_element_type=jnp.float32,
        ).astype(jnp.bfloat16)
        stores[c + 1].start()
    for copy in stores:
        copy.wait()


def lookup(target, table):
    return pl.pallas_call(
        lookup_kernel,
        out_shape=pltpu.HBM((CODEBOOKS, FRAMES, DEPTH_DIM), jnp.bfloat16),
        in_specs=[VMEM, HBM],
        out_specs=HBM,
        scratch_shapes=[
            pltpu.VMEM((CODEBOOKS - 1, VOCAB, DEPTH_DIM), jnp.bfloat16),
            pltpu.VMEM((CODEBOOKS, FRAMES, DEPTH_DIM), jnp.bfloat16),
            pltpu.SemaphoreType.DMA((CODEBOOKS - 1,)),
            pltpu.SemaphoreType.DMA((CODEBOOKS,)),
        ],
        compiler_params=pltpu.CompilerParams(vmem_limit_bytes=40 * 2**20),
        cost_estimate=pl.CostEstimate(
            flops=6 * FRAMES * VOCAB * DEPTH_DIM, bytes_accessed=8 * 2**20, transcendentals=0
        ),
    )(target, table)


def depth_head(projected, embed, gain, heads, bias, target):
    mixed = projected + embed.astype(jnp.float32)
    scale = lax.rsqrt(jnp.mean(mixed * mixed, axis=1, keepdims=True) + 1e-05)
    hidden = (mixed * scale * gain).astype(jnp.bfloat16)
    logits = jnp.dot(hidden, heads, preferred_element_type=jnp.float32) + bias
    top = jnp.max(logits, axis=1, keepdims=True)
    shifted = jnp.exp(logits - top)
    total = jnp.sum(shifted, axis=1, keepdims=True)
    onehot = lax.broadcasted_iota(jnp.int32, (FRAMES, VOCAB), 1) == target
    picked = jnp.sum(jnp.where(onehot, logits, 0.0), axis=1, keepdims=True)
    losses = top + jnp.log(total) - picked
    dlogits = (shifted / total - onehot.astype(jnp.float32)).astype(jnp.bfloat16)
    return hidden, dlogits, losses


def depth_kernel(first, book, *refs):
    if first:
        (ctx_hbm, depth_hbm, embed_hbm, heads_hbm, gain, bias, target) = refs[:7]
        (projected, acts_hbm, losses, acts, ctx, depth_in, embed, heads, sems) = refs[7:]
    else:
        (projected, embed_hbm, heads_hbm, gain, bias, target) = refs[:6]
        (acts, losses, embed, heads, sems) = refs[6:]
    count = [0]

    def fetch(source, kept, pieces):
        rows = kept.shape[0] // pieces
        copies = []
        for i in range(pieces):
            here = slice(i * rows, (i + 1) * rows)
            copies.append(
                pltpu.make_async_copy(source.at[here], kept.at[here], sems.at[count[0]])
            )
            copies[-1].start()
            count[0] += 1
        return copies

    if first:
        ctx_copies = fetch(ctx_hbm, ctx, SEQ)
        depth_copies = fetch(depth_hbm, depth_in, SEQ)
    book_copies = [
        fetch(embed_hbm.at[book[0] + j], embed.at[j], 2)
        + fetch(heads_hbm.at[book[0] + j], heads.at[j], 4)
        for j in range(2)
    ]
    if first:
        total = None
        for part in range(SEQ):
            ctx_copies[part].wait()
            depth_copies[part].wait()
            term = jnp.dot(
                ctx[part],
                depth_in[part * PAIR : (part + 1) * PAIR],
                preferred_element_type=jnp.float32,
            )
            total = term if total is None else total + term
        projected[...] = total
    lane = lax.broadcasted_iota(jnp.int32, (FRAMES, CODEBOOKS), 1)
    both = []
    stores = []
    for j in range(2):
        c = book[0] + j
        for copy in book_copies[j]:
            copy.wait()
        token = jnp.sum(jnp.where(lane == c, target[...], 0), axis=1, keepdims=True)
        hidden, dlogits, loss = depth_head(
            projected[...], embed[j], gain[c], heads[j], bias[c], token
        )
        acts[0, j] = hidden
        acts[1, j] = dlogits
        both.append(loss)
        if first:
            for kind in range(2):
                copy = pltpu.make_async_copy(
                    acts.at[kind, j], acts_hbm.at[kind, j], sems.at[count[0]]
                )
                copy.start()
                stores.append(copy)
                count[0] += 1
    pair_lane = lax.broadcasted_iota(jnp.int32, (FRAMES, 2), 1)
    losses[...] = jnp.where(pair_lane == 0, both[0], both[1])
    for copy in stores:
        copy.wait()


def depth_call(first, outs, book, hbm_args, vmem_args):
    scratch = [
        pltpu.VMEM((2, FRAMES, DEPTH_DIM), jnp.bfloat16),
        pltpu.VMEM((2, DEPTH_DIM, VOCAB), jnp.bfloat16),
        pltpu.SemaphoreType.DMA((32 if first else 12,)),
    ]
    if first:
        scratch = [
            pltpu.VMEM((2, 2, FRAMES, DEPTH_DIM), jnp.bfloat16),
            pltpu.VMEM((SEQ, FRAMES, PAIR), jnp.bfloat16),
            pltpu.VMEM((FEATURES, DEPTH_DIM), jnp.bfloat16),
        ] + scratch
    in_specs = [HBM] * len(hbm_args) + [VMEM] * len(vmem_args)
    if not first:
        in_specs[0] = VMEM
    return pl.pallas_call(
        partial(depth_kernel, first),
        out_shape=outs,
        in_specs=[SMEM] + in_specs,
        out_specs=(VMEM, HBM, VMEM) if first else (VMEM, VMEM),
        scratch_shapes=scratch,
        compiler_params=pltpu.CompilerParams(vmem_limit_bytes=DEPTH_GRANT),
        cost_estimate=pl.CostEstimate(
            flops=2 * 2 * FRAMES * DEPTH_DIM * VOCAB,
            bytes_accessed=8 * 2**20,
            transcendentals=2 * FRAMES * VOCAB,
        ),
    )(book.reshape(1), *hbm_args, *vmem_args)


def outer_kernel(mine, theirs, out_hbm, out, sems):
    chunk = 128
    stores = []
    for step in range(DEPTH_DIM // chunk):
        at = step * chunk
        both = []
        for j in range(2):
            total = None
            for acts in (mine, theirs):
                term = lax.dot_general(
                    acts[0, j, :, at : at + chunk],
                    acts[1, j],
                    (((0,), (0,)), ((), ())),
                    preferred_element_type=jnp.float32,
                )
                total = term if total is None else total + term
            both.append(total.reshape(chunk // 8, 8, VOCAB))
        here = slice(at // 8, (at + chunk) // 8)
        out[here] = jnp.concatenate(both, axis=1).astype(jnp.bfloat16)
        copy = pltpu.make_async_copy(out.at[here], out_hbm.at[here], sems.at[step])
        copy.start()
        stores.append(copy)
    for copy in stores:
        copy.wait()


def outer(mine, theirs):
    return pl.pallas_call(
        outer_kernel,
        out_shape=pltpu.HBM((SEQ * WIDE, 16, VOCAB), jnp.bfloat16),
        in_specs=[VMEM] * 2,
        out_specs=HBM,
        scratch_shapes=[
            pltpu.VMEM((SEQ * WIDE, 16, VOCAB), jnp.bfloat16),
            pltpu.SemaphoreType.DMA((8,)),
        ],
        compiler_params=pltpu.CompilerParams(vmem_limit_bytes=40 * 2**20),
        cost_estimate=pl.CostEstimate(
            flops=2 * 2 * 2 * FRAMES * DEPTH_DIM * VOCAB,
            bytes_accessed=8 * 2**20,
            transcendentals=0,
        ),
    )(mine, theirs)


def total_kernel(scale, shares_hbm, out, shares, sems):
    chips = SEQ * WIDE // 2
    step = chips // 16
    loads = [
        pltpu.make_async_copy(
            shares_hbm.at[i * step : (i + 1) * step],
            shares.at[i * step : (i + 1) * step],
            sems.at[i],
        )
        for i in range(16)
    ]
    for copy in loads:
        copy.start()
    acc = None
    for i in range(16):
        loads[i].wait()
        term = jnp.sum(shares[i * step : (i + 1) * step].astype(jnp.float32), axis=0)
        acc = term if acc is None else acc + term
    for book in range(CODEBOOKS):
        out[:, book] = acc[book // 2, 8 * (book % 2) : 8 * (book % 2) + 8, :] * scale


def total(shares, scale):
    chips = SEQ * WIDE // 2
    return pl.pallas_call(
        partial(total_kernel, scale),
        out_shape=jax.ShapeDtypeStruct((8, CODEBOOKS, VOCAB), jnp.float32),
        in_specs=[HBM],
        out_specs=VMEM,
        scratch_shapes=[
            pltpu.VMEM((chips, 2, 16, VOCAB), jnp.bfloat16),
            pltpu.SemaphoreType.DMA((16,)),
        ],
        compiler_params=pltpu.CompilerParams(vmem_limit_bytes=GRANT),
        cost_estimate=pl.CostEstimate(
            flops=chips * 32 * VOCAB, bytes_accessed=chips * 64 * VOCAB, transcendentals=0
        ),
    )(shares.reshape(chips, 2, 16, VOCAB))


def normalize(norm_gain, mixed_in):
    return (
        mixed_in
        * lax.rsqrt(jnp.mean(mixed_in * mixed_in, axis=-1, keepdims=True) + 1e-05)
        * norm_gain[:, None, :]
    )


def swap_wide(array, stride):
    return lax.ppermute(array, "wide", [(i, i ^ stride) for i in range(WIDE)])


def share_out(rows):
    place = lax.axis_index("wide")
    held = rows.reshape(2, 2, 2, 2, rows.shape[1])
    for axis, stride in enumerate((8, 4, 2, 1)):
        high = (place // stride) % 2 == 1
        low_part = lax.index_in_dim(held, 0, axis, keepdims=True)
        high_part = lax.index_in_dim(held, 1, axis, keepdims=True)
        kept = jnp.where(high, high_part, low_part)
        came = swap_wide(jnp.where(high, low_part, high_part), stride)
        held = jnp.concatenate(
            (jnp.where(high, came, kept), jnp.where(high, kept, came)), axis=axis
        )
    return held.reshape(WIDE, rows.shape[1])


def shards(
    queries, key_vectors, values, audio_codes, depth_in, code_embed, norm_gain, out_heads, out_bias
):
    core = lax.axis_index("wide") % 2
    qkv = lax.all_to_all(pack(queries, key_vectors, values), "seq", 0, 0, tiled=True)
    targets = share_out(audio_codes.reshape(WIDE, 64)).reshape(FRAMES, CODEBOOKS)
    looked = lookup(targets, code_embed)
    heads = out_heads.transpose(1, 0, 2)
    qkv, looked, heads = lax.optimization_barrier((qkv, looked, heads))
    small = (norm_gain[:, None, :], out_bias[:, None, :], targets)

    context = lax.all_to_all(
        attend(qkv), "seq", 0, 0, tiled=True
    )
    mine = 2 * core
    other = 2 - mine
    acts_shape = jax.ShapeDtypeStruct((2, 2, FRAMES, DEPTH_DIM), jnp.bfloat16)
    losses_shape = jax.ShapeDtypeStruct((FRAMES, 2), jnp.float32)
    projected, acts_other, losses_other = depth_call(
        True,
        (
            jax.ShapeDtypeStruct((FRAMES, DEPTH_DIM), jnp.float32),
            pltpu.HBM(acts_shape.shape, acts_shape.dtype),
            losses_shape,
        ),
        other,
        (context, depth_in, looked, heads),
        small,
    )
    came = swap_wide(acts_other, 1)
    acts_mine, losses_mine = depth_call(
        False, (acts_shape, losses_shape), mine, (projected, looked, heads), small
    )
    shares = lax.all_to_all(outer(acts_mine, came), ("seq", "wide"), 0, 0, tiled=True)
    grad_scale = (VOCAB / (SEQ * WIDE * FRAMES)) ** 0.5
    head_grads = total(shares, grad_scale)

    def in_order(of_mine, of_other):
        low = jnp.where(core == 0, of_mine, of_other)
        high = jnp.where(core == 0, of_other, of_mine)
        return jnp.concatenate((low, high), axis=0)

    dlogits = in_order(acts_mine[1], acts_other[1])
    pullback = jax.vjp(
        partial(normalize, norm_gain), projected[None] + looked.astype(jnp.float32)
    )[1]
    dhidden = jnp.einsum("cnv,cev->cne", dlogits, heads, preferred_element_type=jnp.float32)
    dmixed = pullback(dhidden)[0]
    dprojected = jnp.sum(dmixed, axis=0).astype(jnp.bfloat16)
    context_grad = lax.dot_general(
        dprojected, depth_in, (((1,), (1,)), ((), ())), preferred_element_type=jnp.float32
    ).astype(jnp.bfloat16)
    losses = jnp.where(
        core == 0,
        jnp.concatenate((losses_mine, losses_other), axis=1),
        jnp.concatenate((losses_other, losses_mine), axis=1),
    )
    losses, context_grad = lax.optimization_barrier((losses, context_grad))
    frame_losses = share_out(losses.reshape(WIDE, 64)).reshape(WIDE, 16, CODEBOOKS)
    return (frame_losses, context_grad.reshape(1, FRAMES, FEATURES), head_grads)


def solution(mesh):
    return jax.shard_map(
        shards,
        mesh=mesh,
        in_specs=(
            P("wide", "seq", None),
            P("wide", "seq", None),
            P("wide", "seq", None),
            P(None, ("seq", "wide"), None),
            P(),
            P(),
            P(),
            P(),
            P(),
        ),
        out_specs=(
            P(None, ("seq", "wide"), None),
            P("wide", "seq", None),
            P(("seq", "wide"), None, None),
        ),
        check_vma=False,
    )
```

time: 194 us -> 185 us (0.954)
  local copies, waits for them, and re-layouts: 23.1 us -> 16.2 us
  Pallas kernels: 29 us -> 35.6 us
  matrix products: 12.4 us -> 7.74 us
  other arithmetic: 6.24 us -> 3.03 us
  waiting for transfers between devices: 81.6 us -> 79.6 us
    unnamed x33 -> x18, local copies, waits for them, and re-layouts: 21.5 us -> 14.9 us
    pallas_call x5 -> x7, Pallas kernels: 29 us -> 35.6 us  [the longest x2 12.4 us: depth_call(): pl.pallas_call(partial(depth_kernel, first), out_shape=outs, in_specs=[SM...]
    dot_general x1 -> x0, matrix products: 4.64 us -> none  [shards(): jnp.einsum('cnv,cve->cne', chosen.astype(jnp.bfloat16), code_embed, prefe...]
    reduce_sum x1 -> x0, other arithmetic: 3.03 us -> none  [shards(): jnp.sum(shares.reshape(SEQ * WIDE // 2, 4, 8, VOCAB).astype(jnp.float32),...]
  transfers between devices with their start and end apart: 12 -> 12, of which waited for: 10 -> 9; matrix products, arithmetic and copies ran while one was open for 14% -> 12% of each run, Pallas kernels for 2% -> 4%
where the time goes in v3:
time: 185 us; the launch traced here: 184 us
  waiting for transfers between devices  79.6 us (43%)
  starting transfers between devices  40.7 us (22%)
  Pallas kernels  35.6 us (19%)
  local copies, waits for them, and re-layouts  16.2 us (9%)
  matrix products  7.74 us (4%)
  other arithmetic  3.03 us (2%)
    ppermute x9, waiting for transfers between devices, swap_wide(): return lax.ppermute(array, 'wide', [(i, i ^ stride) for i in range(WIDE)])  49.5 us
    all_to_all x1, waiting for transfers between devices, shards(): context = lax.all_to_all(attend(qkv), 'seq', 0, 0, tiled=True)  16.6 us
    all_to_all x1, starting transfers between devices, shards(): context = lax.all_to_all(attend(qkv), 'seq', 0, 0, tiled=True)  16.3 us
    unnamed x18, local copies, waits for them, and re-layouts  14.9 us
    all_to_all x1, waiting for transfers between devices, shards(): lax.all_to_all(pack(queries, key_vectors, values), 'seq', 0, 0, tiled=True)  13.5 us
    pallas_call x2, Pallas kernels, depth_call(): pl.pallas_call(partial(depth_kernel, first), out_shape=outs, in_specs=[SM...  12.4 us
    pallas_call x1, Pallas kernels, attend(): pl.pallas_call(attend_kernel, out_shape=pltpu.HBM((SEQ, FRAMES, PAIR), jn...  9.51 us
    ppermute x9, starting transfers between devices, swap_wide(): return lax.ppermute(array, 'wide', [(i, i ^ stride) for i in range(WIDE)])  9.5 us
  transfers between devices with their start and end apart: 12, of which 9 were waited for; matrix products, arithmetic and copies ran while one was open for 12% of the time, Pallas kernels for 4%

profile of v3, /device:TPU:2, one launch (start us, length us, event | category | flops | bytes accessed | tf_op | source)
XLA Modules:
  0.0 184.0 jit_solution(17458746358609771929)
XLA Ops:
  0.6 3.7 %shard_map.112 = bf16[8,256,768]{2,1,0:T(8,128)(2,1)} custom-call(bf16[1,256,2048]{2,1,0:T(8,128)(2,1)} %queries.1, bf16[1,256,2048]{2,1,0:T(8,128)(2,1)} %key_vectors.1, bf16[1,256,2048]{2,1,0:T(8,128)(2,1)} %values.1), custom_call_target="tpu_custom_call" | custom-call | bytes 6291456 | tf_op jit(solution)/shard_map/pallas_call | solution.py:134
  4.3 8.2 %all-to-all-start = ((bf16[8,256,768]{2,1,0:T(8,128)(2,1)}), bf16[8,256,768]{2,1,0:T(8,128)(2,1)S(1)}, u32[]{:S(2)}, u32[]{:S(2)}) async-start(bf16[8,256,768]{2,1,0:T(8,128)(2,1)} %shard_map.112), calls=%async_computation | async-start | bytes 6291456 | tf_op jit(solution)/shard_map/all_to_all | solution.py:424
  12.7 3.3 %collective-permute-start = (s32[1,2,2,2,64]{4,3,2,1,0:T(2,128)S(1)}, s32[1,2,2,2,64]{4,3,2,1,0:T(2,128)S(1)}, u32[]{:S(2)}, u32[]{:S(2)}) collective-permute-start(s32[1,2,2,2,64]{4,3,2,1,0:T(2,128)S(1)} %select_n.285), channel_id=1, source_target_pairs={{0,8},{1,9},{2,10},{3,11},{4,12},{5,13},{6,14},{7,15},{8,0},{9,1},... | collective-permute-start | bytes 6152 | tf_op jit(solution)/shard_map/ppermute | solution.py:402
  16.2 1.7 collective-permute-done
  17.9 1.7 collective-permute-start.1
  19.6 2.0 %collective-permute-done.1 = s32[2,1,2,2,64]{4,3,2,1,0:T(2,128)S(1)} collective-permute-done((s32[2,1,2,2,64]{4,3,2,1,0:T(2,128)S(1)}, s32[2,1,2,2,64]{4,3,2,1,0:T(2,128)S(1)}, u32[]{:S(2)}, u32[]{:S(2)}) %collective-permute-start.1) | collective-permute-done | bytes 2080 | tf_op jit(solution)/shard_map/ppermute | solution.py:402
  21.6 1.1 collective-permute-start.2
  22.7 3.0 %collective-permute-done.2 = s32[2,2,1,2,64]{4,3,2,1,0:T(2,128)S(1)} collective-permute-done((s32[2,2,1,2,64]{4,3,2,1,0:T(2,128)S(1)}, s32[2,2,1,2,64]{4,3,2,1,0:T(2,128)S(1)}, u32[]{:S(2)}, u32[]{:S(2)}) %collective-permute-start.2) | collective-permute-done | bytes 2080 | tf_op jit(solution)/shard_map/ppermute | solution.py:402
  25.9 9.5 %copy.28 = bf16[1024,4,1024]{2,0,1:T(8,128)(2,1)} copy(bf16[1024,4,1024]{2,1,0:T(4,128)(2,1)} %param.16) | data formatting | bytes 16777216 | tf_op args[7]
  35.5 2.8 %copy-done = bf16[3,1024,1024]{2,1,0:T(8,128)(2,1)S(1)} copy-done((bf16[3,1024,1024]{2,1,0:T(8,128)(2,1)S(1)}, bf16[3,1024,1024]{2,1,0:T(8,128)(2,1)}, u32[]{:S(2)}) %copy-start) | copy-done | bytes 6291480
  38.3 3.6 %shard_map.113.refs_2_.refs_1_ = bf16[4,256,1024]{2,1,0:T(8,128)(2,1)} custom-call(s32[256,4]{1,0:T(8,128)S(1)} %reshape_reshape.8.target.refs_6_.refs_5_, bf16[3,1024,1024]{2,1,0:T(8,128)(2,1)S(1)} %copy-done), custom_call_target="tpu_custom_call" | custom-call | flops 1610612736 | bytes 8388608 | tf_op jit(solution)/shard_map/pallas_call | solution.py:176
  42.0 13.5 %all-to-all-done.qkv = bf16[8,256,768]{2,1,0:T(8,128)(2,1)S(1)} async-done(((bf16[8,256,768]{2,1,0:T(8,128)(2,1)}), bf16[8,256,768]{2,1,0:T(8,128)(2,1)S(1)}, u32[]{:S(2)}, u32[]{:S(2)}) %all-to-all-start) | async-done | bytes 3145760 | tf_op jit(solution)/shard_map/all_to_all | solution.py:424
  55.4 9.5 %shard_map.114 = bf16[8,256,256]{2,1,0:T(8,128)(2,1)} custom-call(bf16[8,256,768]{2,1,0:T(8,128)(2,1)S(1)} %all-to-all-done.qkv), custom_call_target="tpu_custom_call" | custom-call | flops 2415919104 | bytes 4194304 | tf_op jit(solution)/shard_map/pallas_call | solution.py:82
  64.9 16.3 %all-to-all-start.1 = ((bf16[8,256,256]{2,1,0:T(8,128)(2,1)}), bf16[8,256,256]{2,1,0:T(8,128)(2,1)S(1)}, u32[]{:S(2)}, u32[]{:S(2)}) async-start(bf16[8,256,256]{2,1,0:T(8,128)(2,1)} %shard_map.114), calls=%async_computation.1 | async-start | bytes 2097152 | tf_op jit(solution)/shard_map/all_to_all | solution.py:431
  81.3 16.6 %all-to-all-done.1.refs_0_ = bf16[8,256,256]{2,1,0:T(8,128)(2,1)S(1)} async-done(((bf16[8,256,256]{2,1,0:T(8,128)(2,1)}), bf16[8,256,256]{2,1,0:T(8,128)(2,1)S(1)}, u32[]{:S(2)}, u32[]{:S(2)}) %all-to-all-start.1) | async-done | bytes 1048608 | tf_op jit(solution)/shard_map/all_to_all | solution.py:431
  98.0 8.1 %shard_map.115 = (f32[256,1024]{1,0:T(8,128)S(1)}, bf16[2,2,256,1024]{3,2,1,0:T(8,128)(2,1)}, f32[256,2]{1,0:T(8,128)S(1)}) custom-call(s32[1]{0:T(128)} %bitcast.1.book, bf16[8,256,256]{2,1,0:T(8,128)(2,1)S(1)} %all-to-all-done.1.refs_0_, bf16[2048,1024]{1,0:T(8,128)(2,1)} %refs_1_.1, bf16[4,256,1024]{2,1,0:T(8,128)(2,1)} %shard_map.113.refs_2_.refs_1_, ...), custom_call_target="tpu_custom_call" | custom-call | flops 1073741824 | bytes 8388608 | tf_op jit(solution)/shard_map/pallas_call | solution.py:293
  106.1 4.3 %shard_map.116 = (bf16[2,2,256,1024]{3,2,1,0:T(8,128)(2,1)S(1)}, f32[256,2]{1,0:T(8,128)S(1)}) custom-call(s32[1]{0:T(128)} %bitcast.book, f32[256,1024]{1,0:T(8,128)S(1)} %get-tuple-element.16.refs_0_, bf16[4,256,1024]{2,1,0:T(8,128)(2,1)} %shard_map.113.refs_2_.refs_1_, bf16[4,1024,1024]{2,1,0:T(8,128)(2,1)} %bitcast.15, ...), custom_call_target="tpu_custom_call" | custom-call | flops 1073741824 | bytes 8388608 | tf_op jit(solution)/shard_map/pallas_call | solution.py:293
  110.5 0.6 copy-done.1
  111.1 3.3 %shard_map.117 = bf16[128,16,1024]{2,1,0:T(8,128)(2,1)} custom-call(bf16[2,2,256,1024]{3,2,1,0:T(8,128)(2,1)S(1)} %get-tuple-element.19.mine, bf16[2,2,256,1024]{3,2,1,0:T(8,128)(2,1)S(1)} %collective-permute-done.8.theirs), custom_call_target="tpu_custom_call" | custom-call | flops 2147483648 | bytes 8388608 | tf_op jit(solution)/shard_map/pallas_call | solution.py:335
  114.5 6.8 %all-to-all-start.2 = ((bf16[128,16,1024]{2,1,0:T(8,128)(2,1)}), bf16[128,16,1024]{2,1,0:T(8,128)(2,1)}, u32[]{:S(2)}, u32[]{:S(2)}) async-start(bf16[128,16,1024]{2,1,0:T(8,128)(2,1)} %shard_map.117), calls=%async_computation.2 | async-start | bytes 8388608 | tf_op jit(solution)/shard_map/all_to_all | solution.py:453
  121.4 1.5 select_bitcast_fusion.1
  123.3 5.5 %multiply_reduce_fusion.1 = (f32[4,256]{1,0:T(4,128)S(1)}, f32[4,256]{1,0:T(4,128)S(1)}, f32[4,256,1024]{2,1,0:T(8,128)S(1)}) fusion(bf16[4,256,1024]{2,1,0:T(8,128)(2,1)S(1)} %copy-done.3, f32[256,1024]{1,0:T(8,128)S(1)} %get-tuple-element.16.refs_0_, f32[4,1024]{1,0:T(4,128)S(1)} %copy-done.5, bf16[4,1024,1024]{2,1,0:T(8,128)(2,1)} %bitcast.16, ...), kind=kOutput, calls=%fused_computation.4 | convolution fusion | flops 2155870208 | bytes 17850368 | tf_op jit(solution)/shard_map/cnv,cev->cne/dot_general | solution.py:466
  128.9 1.3 fusion
  130.2 0.8 copy-done.4
  131.0 2.3 %convolution_convert_fusion = bf16[256,2048]{1,0:T(8,128)(2,1)} fusion(bf16[2048,1024]{1,0:T(8,128)(2,1)S(1)} %copy-done.4, bf16[256,1024]{1,0:T(8,128)(2,1)S(1)} %fusion), kind=kOutput, calls=%fused_computation.6 | convolution fusion | flops 1074266112 | bytes 5767168 | tf_op jit(solution)/shard_map/dot_general | solution.py:469
  133.5 3.0 %collective-permute-start.4 = (f32[1,2,2,2,64]{4,3,2,1,0:T(2,128)S(1)}, f32[1,2,2,2,64]{4,3,2,1,0:T(2,128)S(1)}, u32[]{:S(2)}, u32[]{:S(2)}) collective-permute-start(f32[1,2,2,2,64]{4,3,2,1,0:T(2,128)S(1)} %select_n.309), channel_id=1, source_target_pairs={{0,8},{1,9},{2,10},{3,11},{4,12},{5,13},{6,14},{7,15},{8,0},{9,1},... | collective-permute-start | bytes 6152 | tf_op jit(solution)/shard_map/ppermute | solution.py:402
  136.8 34.4 %collective-permute-done.4 = f32[1,2,2,2,64]{4,3,2,1,0:T(2,128)S(1)} collective-permute-done((f32[1,2,2,2,64]{4,3,2,1,0:T(2,128)S(1)}, f32[1,2,2,2,64]{4,3,2,1,0:T(2,128)S(1)}, u32[]{:S(2)}, u32[]{:S(2)}) %collective-permute-start.4) | collective-permute-done | bytes 2080 | tf_op jit(solution)/shard_map/ppermute | solution.py:402
  171.3 3.6 %collective-permute-done.5 = f32[2,1,2,2,64]{4,3,2,1,0:T(2,128)S(1)} collective-permute-done((f32[2,1,2,2,64]{4,3,2,1,0:T(2,128)S(1)}, f32[2,1,2,2,64]{4,3,2,1,0:T(2,128)S(1)}, u32[]{:S(2)}, u32[]{:S(2)}) %collective-permute-start.5) | collective-permute-done | bytes 2080 | tf_op jit(solution)/shard_map/ppermute | solution.py:402
  175.0 3.6 %collective-permute-done.6 = f32[2,2,1,2,64]{4,3,2,1,0:T(2,128)S(1)} collective-permute-done((f32[2,2,1,2,64]{4,3,2,1,0:T(2,128)S(1)}, f32[2,2,1,2,64]{4,3,2,1,0:T(2,128)S(1)}, u32[]{:S(2)}, u32[]{:S(2)}) %collective-permute-start.6) | collective-permute-done | bytes 2080 | tf_op jit(solution)/shard_map/ppermute | solution.py:402
  178.7 1.2 collective-permute-done.7
  180.0 0.8 copy.26
  180.8 3.0 %shard_map.118 = f32[8,4,1024]{2,1,0:T(4,128)} custom-call(bf16[64,2,16,1024]{3,2,1,0:T(8,128)(2,1)} %bitcast.6.shares_hbm), custom_call_target="tpu_custom_call" | custom-call | flops 2097152 | bytes 4194304 | tf_op jit(solution)/shard_map/pallas_call | solution.py:377
  (55 shorter events, 2.3 us)
Async XLA Ops:
  4.3 8.2 %copy-start.6 = (s32[16,16,4]{1,2,0:T(4,128)S(1)}, s32[16,16,4]{1,2,0:T(4,128)}, u32[]{:S(2)}) copy-start(s32[16,16,4]{1,2,0:T(4,128)} %param.12) | copy-start | bytes 12292
  4.3 51.1 %all-to-all-start = ((bf16[8,256,768]{2,1,0:T(8,128)(2,1)}), bf16[8,256,768]{2,1,0:T(8,128)(2,1)S(1)}, u32[]{:S(2)}, u32[]{:S(2)}) async-start(bf16[8,256,768]{2,1,0:T(8,128)(2,1)} %shard_map.112), calls=%async_computation | async-start | bytes 6291456 | tf_op jit(solution)/shard_map/all_to_all | solution.py:424
  12.7 5.2 %collective-permute-start = (s32[1,2,2,2,64]{4,3,2,1,0:T(2,128)S(1)}, s32[1,2,2,2,64]{4,3,2,1,0:T(2,128)S(1)}, u32[]{:S(2)}, u32[]{:S(2)}) collective-permute-start(s32[1,2,2,2,64]{4,3,2,1,0:T(2,128)S(1)} %select_n.285), channel_id=1, source_target_pairs={{0,8},{1,9},{2,10},{3,11},{4,12},{5,13},{6,14},{7,15},{8,0},{9,1},... | collective-permute-start | bytes 6152 | tf_op jit(solution)/shard_map/ppermute | solution.py:402
  17.9 3.7 %collective-permute-start.1 = (s32[2,1,2,2,64]{4,3,2,1,0:T(2,128)S(1)}, s32[2,1,2,2,64]{4,3,2,1,0:T(2,128)S(1)}, u32[]{:S(2)}, u32[]{:S(2)}) collective-permute-start(s32[2,1,2,2,64]{4,3,2,1,0:T(2,128)S(1)} %broadcast_select_fusion.19), channel_id=1, source_target_pairs={{0,4},{1,5},{2,6},{3,7},{4,0},{5,1},{6,2},{7,3},{8,12},{9,13},{10,... | collective-permute-start | bytes 6152 | tf_op jit(solution)/shard_map/ppermute | solution.py:402
  21.6 4.1 %collective-permute-start.2 = (s32[2,2,1,2,64]{4,3,2,1,0:T(2,128)S(1)}, s32[2,2,1,2,64]{4,3,2,1,0:T(2,128)S(1)}, u32[]{:S(2)}, u32[]{:S(2)}) collective-permute-start(s32[2,2,1,2,64]{4,3,2,1,0:T(2,128)S(1)} %broadcast_select_fusion.27), channel_id=1, source_target_pairs={{0,2},{1,3},{2,0},{3,1},{4,6},{5,7},{6,4},{7,5},{8,10},{9,11},{10,... | collective-permute-start | bytes 6152 | tf_op jit(solution)/shard_map/ppermute | solution.py:402
  25.8 9.6 %collective-permute-start.3 = (s32[2,2,2,1,64]{4,3,2,1,0:T(1,128)S(1)}, s32[2,2,2,1,64]{4,3,2,1,0:T(1,128)S(1)}, u32[]{:S(2)}, u32[]{:S(2)}) collective-permute-start(s32[2,2,2,1,64]{4,3,2,1,0:T(1,128)S(1)} %get-tuple-element.33), channel_id=1, source_target_pairs={{0,1},{1,0},{2,3},{3,2},{4,5},{5,4},{6,7},{7,6},{8,9},{9,8},{10,11... | collective-permute-start | bytes 6152 | tf_op jit(solution)/shard_map/ppermute | solution.py:402
  35.5 2.8 %copy-start = (bf16[3,1024,1024]{2,1,0:T(8,128)(2,1)S(1)}, bf16[3,1024,1024]{2,1,0:T(8,128)(2,1)}, u32[]{:S(2)}) copy-start(bf16[3,1024,1024]{2,1,0:T(8,128)(2,1)} %table_hbm.1) | copy-start | bytes 18874372
  55.4 25.8 %copy-start.7 = (f32[4,1024]{1,0:T(4,128)S(1)}, f32[4,1024]{1,0:T(4,128)}, u32[]{:S(2)}) copy-start(f32[4,1024]{1,0:T(4,128)} %param.17) | copy-start | bytes 49156
  55.4 25.9 %copy-start.5 = (f32[4,1024]{1,0:T(4,128)S(1)}, f32[4,1024]{1,0:T(4,128)}, u32[]{:S(2)}) copy-start(f32[4,1024]{1,0:T(4,128)} %param.15) | copy-start | bytes 49156
  64.9 33.0 %all-to-all-start.1 = ((bf16[8,256,256]{2,1,0:T(8,128)(2,1)}), bf16[8,256,256]{2,1,0:T(8,128)(2,1)S(1)}, u32[]{:S(2)}, u32[]{:S(2)}) async-start(bf16[8,256,256]{2,1,0:T(8,128)(2,1)} %shard_map.114), calls=%async_computation.1 | async-start | bytes 2097152 | tf_op jit(solution)/shard_map/all_to_all | solution.py:431
  106.0 5.1 %collective-permute-start.8 = (bf16[2,2,256,1024]{3,2,1,0:T(8,128)(2,1)}, bf16[2,2,256,1024]{3,2,1,0:T(8,128)(2,1)S(1)}, u32[]{:S(2)}, u32[]{:S(2)}) collective-permute-start(bf16[2,2,256,1024]{3,2,1,0:T(8,128)(2,1)} %get-tuple-element.20), channel_id=1, source_target_pairs={{0,1},{1,0},{2,3},{3,2},{4,5},{5,4},{6,7},{7,6},{8,9},{9,8},{10,11... | collective-permute-start | bytes 6291464 | tf_op jit(solution)/shard_map/ppermute | solution.py:402
  110.5 0.7 copy-start.1
  114.4 6.9 %copy-start.2 = (f32[256,2]{1,0:T(8,128)S(1)}, f32[256,2]{1,0:T(8,128)}, u32[]{:S(2)}) copy-start(f32[256,2]{1,0:T(8,128)} %copy-done.1) | copy-start | bytes 6148
  114.5 66.3 %all-to-all-start.2 = ((bf16[128,16,1024]{2,1,0:T(8,128)(2,1)}), bf16[128,16,1024]{2,1,0:T(8,128)(2,1)}, u32[]{:S(2)}, u32[]{:S(2)}) async-start(bf16[128,16,1024]{2,1,0:T(8,128)(2,1)} %shard_map.117), calls=%async_computation.2 | async-start | bytes 8388608 | tf_op jit(solution)/shard_map/all_to_all | solution.py:453
  121.4 1.9 %copy-start.3 = (bf16[4,256,1024]{2,1,0:T(8,128)(2,1)S(1)}, bf16[4,256,1024]{2,1,0:T(8,128)(2,1)}, u32[]{:S(2)}) copy-start(bf16[4,256,1024]{2,1,0:T(8,128)(2,1)} %shard_map.113.refs_2_.refs_1_) | copy-start | bytes 6291460
  128.8 2.2 %copy-start.4 = (bf16[2048,1024]{1,0:T(8,128)(2,1)S(1)}, bf16[2048,1024]{1,0:T(8,128)(2,1)}, u32[]{:S(2)}) copy-start(bf16[2048,1024]{1,0:T(8,128)(2,1)} %refs_1_.1) | copy-start | bytes 12582916
  133.5 37.7 %collective-permute-start.4 = (f32[1,2,2,2,64]{4,3,2,1,0:T(2,128)S(1)}, f32[1,2,2,2,64]{4,3,2,1,0:T(2,128)S(1)}, u32[]{:S(2)}, u32[]{:S(2)}) collective-permute-start(f32[1,2,2,2,64]{4,3,2,1,0:T(2,128)S(1)} %select_n.309), channel_id=1, source_target_pairs={{0,8},{1,9},{2,10},{3,11},{4,12},{5,13},{6,14},{7,15},{8,0},{9,1},... | collective-permute-start | bytes 6152 | tf_op jit(solution)/shard_map/ppermute | solution.py:402
  171.2 3.7 %collective-permute-start.5 = (f32[2,1,2,2,64]{4,3,2,1,0:T(2,128)S(1)}, f32[2,1,2,2,64]{4,3,2,1,0:T(2,128)S(1)}, u32[]{:S(2)}, u32[]{:S(2)}) collective-permute-start(f32[2,1,2,2,64]{4,3,2,1,0:T(2,128)S(1)} %broadcast_select_fusion.15), channel_id=1, source_target_pairs={{0,4},{1,5},{2,6},{3,7},{4,0},{5,1},{6,2},{7,3},{8,12},{9,13},{10,... | collective-permute-start | bytes 6152 | tf_op jit(solution)/shard_map/ppermute | solution.py:402
  174.9 3.7 %collective-permute-start.6 = (f32[2,2,1,2,64]{4,3,2,1,0:T(2,128)S(1)}, f32[2,2,1,2,64]{4,3,2,1,0:T(2,128)S(1)}, u32[]{:S(2)}, u32[]{:S(2)}) collective-permute-start(f32[2,2,1,2,64]{4,3,2,1,0:T(2,128)S(1)} %broadcast_select_fusion.23), channel_id=1, source_target_pairs={{0,2},{1,3},{2,0},{3,1},{4,6},{5,7},{6,4},{7,5},{8,10},{9,11},{10,... | collective-permute-start | bytes 6152 | tf_op jit(solution)/shard_map/ppermute | solution.py:402
  178.6 1.2 collective-permute-start.7

commit v4 on v3

--- a/solution.py
+++ b/solution.py
@@ -75,7 +75,7 @@
 VMEM = pl.BlockSpec(memory_space=pltpu.VMEM)
 SMEM = pl.BlockSpec(memory_space=pltpu.SMEM)
 GRANT = 60 * 2**20
-DEPTH_GRANT = 50 * 2**20
+DEPTH_GRANT = 44 * 2**20
 
 
 def attend(qkv):
@@ -146,13 +146,13 @@
     )(queries, key_vectors, values)
 
 
-def lookup_kernel(target, table_hbm, out_hbm, table, out, in_sems, out_sems):
+def lookup_kernel(target, table_hbm, looked_hbm, table, out, in_sems, out_sems):
     books = CODEBOOKS - 1
     loads = [
         pltpu.make_async_copy(table_hbm.at[c], table.at[c], in_sems.at[c]) for c in range(books)
     ]
     stores = [
-        pltpu.make_async_copy(out.at[c], out_hbm.at[c], out_sems.at[c])
+        pltpu.make_async_copy(out.at[c], looked_hbm.at[c], out_sems.at[c])
         for c in range(CODEBOOKS)
     ]
     for copy in loads:
@@ -184,9 +184,9 @@
             pltpu.SemaphoreType.DMA((CODEBOOKS - 1,)),
             pltpu.SemaphoreType.DMA((CODEBOOKS,)),
         ],
-        compiler_params=pltpu.CompilerParams(vmem_limit_bytes=40 * 2**20),
+        compiler_params=pltpu.CompilerParams(vmem_limit_bytes=GRANT),
         cost_estimate=pl.CostEstimate(
-            flops=6 * FRAMES * VOCAB * DEPTH_DIM, bytes_accessed=8 * 2**20, transcendentals=0
+            flops=6 * FRAMES * VOCAB * DEPTH_DIM, bytes_accessed=10 * 2**20, transcendentals=0
         ),
     )(target, table)
 
@@ -206,103 +206,152 @@
     return hidden, dlogits, losses
 
 
-def depth_kernel(first, book, *refs):
-    if first:
-        (ctx_hbm, depth_hbm, embed_hbm, heads_hbm, gain, bias, target) = refs[:7]
-        (projected, acts_hbm, losses, acts, ctx, depth_in, embed, heads, sems) = refs[7:]
-    else:
-        (projected, embed_hbm, heads_hbm, gain, bias, target) = refs[:6]
-        (acts, losses, embed, heads, sems) = refs[6:]
-    count = [0]
-
-    def fetch(source, kept, pieces):
-        rows = kept.shape[0] // pieces
-        copies = []
-        for i in range(pieces):
-            here = slice(i * rows, (i + 1) * rows)
-            copies.append(
-                pltpu.make_async_copy(source.at[here], kept.at[here], sems.at[count[0]])
-            )
-            copies[-1].start()
-            count[0] += 1
-        return copies
-
-    if first:
-        ctx_copies = fetch(ctx_hbm, ctx, SEQ)
-        depth_copies = fetch(depth_hbm, depth_in, SEQ)
-    book_copies = [
-        fetch(embed_hbm.at[book[0] + j], embed.at[j], 2)
-        + fetch(heads_hbm.at[book[0] + j], heads.at[j], 4)
-        for j in range(2)
-    ]
-    if first:
-        total = None
-        for part in range(SEQ):
-            ctx_copies[part].wait()
-            depth_copies[part].wait()
-            term = jnp.dot(
-                ctx[part],
-                depth_in[part * PAIR : (part + 1) * PAIR],
-                preferred_element_type=jnp.float32,
-            )
-            total = term if total is None else total + term
-        projected[...] = total
+def depth_pair(
+    book, projected, embed, heads, gain, bias, target, acts, losses, begin=None, finish=None
+):
     lane = lax.broadcasted_iota(jnp.int32, (FRAMES, CODEBOOKS), 1)
     both = []
-    stores = []
     for j in range(2):
         c = book[0] + j
-        for copy in book_copies[j]:
-            copy.wait()
+        if begin:
+            begin(j)
         token = jnp.sum(jnp.where(lane == c, target[...], 0), axis=1, keepdims=True)
         hidden, dlogits, loss = depth_head(
             projected[...], embed[j], gain[c], heads[j], bias[c], token
         )
         acts[0, j] = hidden
         acts[1, j] = dlogits
+        if finish:
+            finish(j)
         both.append(loss)
-        if first:
-            for kind in range(2):
-                copy = pltpu.make_async_copy(
-                    acts.at[kind, j], acts_hbm.at[kind, j], sems.at[count[0]]
-                )
-                copy.start()
-                stores.append(copy)
-                count[0] += 1
     pair_lane = lax.broadcasted_iota(jnp.int32, (FRAMES, 2), 1)
     losses[...] = jnp.where(pair_lane == 0, both[0], both[1])
-    for copy in stores:
+
+
+def first_kernel(
+    book,
+    ctx,
+    gain,
+    bias,
+    target,
+    depth_hbm,
+    looked_hbm,
+    heads_hbm,
+    projected,
+    acts_hbm,
+    losses,
+    next_embed,
+    next_heads,
+    acts,
+    depth_in,
+    embed,
+    heads,
+    depth_sems,
+    book_sems,
+    next_sems,
+    out_sems,
+):
+    rows = [slice(part * PAIR, (part + 1) * PAIR) for part in range(SEQ)]
+    depth_copies = [
+        pltpu.make_async_copy(depth_hbm.at[rows[part]], depth_in.at[rows[part]], depth_sems.at[part])
+        for part in range(SEQ)
+    ]
+    book_copies = [
+        [
+            pltpu.make_async_copy(looked_hbm.at[book[0] + j], embed.at[j], book_sems.at[0, j]),
+            pltpu.make_async_copy(heads_hbm.at[book[0] + j], heads.at[j], book_sems.at[1, j]),
+        ]
+        for j in range(2)
+    ]
+    staged = []
+    for j in range(2):
+        c = book[1] + j
+        staged.append(
+            pltpu.make_async_copy(looked_hbm.at[c], next_embed.at[j], next_sems.at[0, j])
+        )
+        staged.append(
+            pltpu.make_async_copy(heads_hbm.at[c], next_heads.at[j], next_sems.at[1, j])
+        )
+    for copy in depth_copies + book_copies[0] + book_copies[1] + staged:
+        copy.start()
+    total = None
+    for part in range(SEQ):
+        depth_copies[part].wait()
+        term = jnp.dot(ctx[part], depth_in[rows[part]], preferred_element_type=jnp.float32)
+        total = term if total is None else total + term
+    projected[...] = total
+    stores = [
+        [
+            pltpu.make_async_copy(acts.at[kind, j], acts_hbm.at[kind, j], out_sems.at[kind, j])
+            for kind in range(2)
+        ]
+        for j in range(2)
+    ]
+
+    def begin(j):
+        for copy in book_copies[j]:
+            copy.wait()
+
+    def finish(j):
+        for copy in stores[j]:
+            copy.start()
+
+    depth_pair(book, projected, embed, heads, gain, bias, target, acts, losses, begin, finish)
+    for copy in staged + stores[0] + stores[1]:
         copy.wait()
 
 
-def depth_call(first, outs, book, hbm_args, vmem_args):
-    scratch = [
-        pltpu.VMEM((2, FRAMES, DEPTH_DIM), jnp.bfloat16),
-        pltpu.VMEM((2, DEPTH_DIM, VOCAB), jnp.bfloat16),
-        pltpu.SemaphoreType.DMA((32 if first else 12,)),
-    ]
-    if first:
-        scratch = [
-            pltpu.VMEM((2, 2, FRAMES, DEPTH_DIM), jnp.bfloat16),
-            pltpu.VMEM((SEQ, FRAMES, PAIR), jnp.bfloat16),
+def second_kernel(book, projected, embed, heads, gain, bias, target, acts, losses):
+    depth_pair(book, projected, embed, heads, gain, bias, target, acts, losses)
+
+
+DEPTH_COST = pl.CostEstimate(
+    flops=2 * 2 * FRAMES * DEPTH_DIM * VOCAB,
+    bytes_accessed=8 * 2**20,
+    transcendentals=2 * FRAMES * VOCAB,
+)
+ACTS = (2, 2, FRAMES, DEPTH_DIM)
+
+
+def depth_first(books, context, small, depth_in, looked, heads):
+    return pl.pallas_call(
+        first_kernel,
+        out_shape=(
+            jax.ShapeDtypeStruct((FRAMES, DEPTH_DIM), jnp.float32),
+            pltpu.HBM(ACTS, jnp.bfloat16),
+            jax.ShapeDtypeStruct((FRAMES, 2), jnp.float32),
+            pltpu.VMEM((2, FRAMES, DEPTH_DIM), jnp.bfloat16),
+            pltpu.VMEM((2, DEPTH_DIM, VOCAB), jnp.bfloat16),
+        ),
+        in_specs=[SMEM] + [VMEM] * 4 + [HBM] * 3,
+        out_specs=(VMEM, HBM, VMEM, VMEM, VMEM),
+        scratch_shapes=[
+            pltpu.VMEM(ACTS, jnp.bfloat16),
             pltpu.VMEM((FEATURES, DEPTH_DIM), jnp.bfloat16),
-        ] + scratch
-    in_specs = [HBM] * len(hbm_args) + [VMEM] * len(vmem_args)
-    if not first:
-        in_specs[0] = VMEM
-    return pl.pallas_call(
-        partial(depth_kernel, first),
-        out_shape=outs,
-        in_specs=[SMEM] + in_specs,
-        out_specs=(VMEM, HBM, VMEM) if first else (VMEM, VMEM),
-        scratch_shapes=scratch,
+            pltpu.VMEM((2, FRAMES, DEPTH_DIM), jnp.bfloat16),
+            pltpu.VMEM((2, DEPTH_DIM, VOCAB), jnp.bfloat16),
+            pltpu.SemaphoreType.DMA((SEQ,)),
+            pltpu.SemaphoreType.DMA((2, 2)),
+            pltpu.SemaphoreType.DMA((2, 2)),
+            pltpu.SemaphoreType.DMA((2, 2)),
+        ],
         compiler_params=pltpu.CompilerParams(vmem_limit_bytes=DEPTH_GRANT),
-        cost_estimate=pl.CostEstimate(
-            flops=2 * 2 * FRAMES * DEPTH_DIM * VOCAB,
-            bytes_accessed=8 * 2**20,
-            transcendentals=2 * FRAMES * VOCAB,
-        ),
-    )(book.reshape(1), *hbm_args, *vmem_args)
+        cost_estimate=DEPTH_COST,
+    )(books, context, *small, depth_in, looked, heads)
+
+
+def depth_second(book, projected, embed, heads, small):
+    return pl.pallas_call(
+        second_kernel,
+        out_shape=(
+            jax.ShapeDtypeStruct(ACTS, jnp.bfloat16),
+            jax.ShapeDtypeStruct((FRAMES, 2), jnp.float32),
+        ),
+        in_specs=[SMEM] + [VMEM] * 6,
+        out_specs=(VMEM, VMEM),
+        compiler_params=pltpu.CompilerParams(vmem_limit_bytes=DEPTH_GRANT),
+        cost_estimate=DEPTH_COST,
+    )(book.reshape(1), projected, embed, heads, *small)
 
 
 def outer_kernel(mine, theirs, out_hbm, out, sems):
@@ -402,54 +451,56 @@
     return lax.ppermute(array, "wide", [(i, i ^ stride) for i in range(WIDE)])
 
 
+def share_step(held, axis, stride):
+    high = (lax.axis_index("wide") // stride) % 2 == 1
+    low_part = lax.index_in_dim(held, 0, axis, keepdims=True)
+    high_part = lax.index_in_dim(held, 1, axis, keepdims=True)
+    kept = jnp.where(high, high_part, low_part)
+    came = swap_wide(jnp.where(high, low_part, high_part), stride)
+    return jnp.concatenate(
+        (jnp.where(high, came, kept), jnp.where(high, kept, came)), axis=axis
+    )
+
+
+def by_distance(rows):
+    index = jnp.arange(WIDE, dtype=jnp.int32)
+    pick = index[:, None] == (index[None, :] ^ lax.axis_index("wide"))
+    return jnp.sum(jnp.where(pick[:, :, None], rows[None], 0), axis=1)
+
+
 def share_out(rows):
-    place = lax.axis_index("wide")
-    held = rows.reshape(2, 2, 2, 2, rows.shape[1])
-    for axis, stride in enumerate((8, 4, 2, 1)):
-        high = (place // stride) % 2 == 1
-        low_part = lax.index_in_dim(held, 0, axis, keepdims=True)
-        high_part = lax.index_in_dim(held, 1, axis, keepdims=True)
-        kept = jnp.where(high, high_part, low_part)
-        came = swap_wide(jnp.where(high, low_part, high_part), stride)
-        held = jnp.concatenate(
-            (jnp.where(high, came, kept), jnp.where(high, kept, came)), axis=axis
-        )
-    return held.reshape(WIDE, rows.shape[1])
+    sent = by_distance(rows).reshape(4, 4, rows.shape[1])
+    first = jnp.stack([sent[0]] + [swap_wide(sent[k], 4 * k) for k in range(1, 4)])
+    second = [first[:, 0]] + [swap_wide(first[:, k], k) for k in range(1, 4)]
+    return by_distance(jnp.stack(second, axis=1).reshape(WIDE, rows.shape[1]))
 
 
 def shards(
     queries, key_vectors, values, audio_codes, depth_in, code_embed, norm_gain, out_heads, out_bias
 ):
     core = lax.axis_index("wide") % 2
-    qkv = lax.all_to_all(pack(queries, key_vectors, values), "seq", 0, 0, tiled=True)
-    targets = share_out(audio_codes.reshape(WIDE, 64)).reshape(FRAMES, CODEBOOKS)
-    looked = lookup(targets, code_embed)
+    packed = pack(queries, key_vectors, values)
+    held, packed = lax.optimization_barrier((audio_codes, packed))
+    held = share_step(held.reshape(2, 2, 2, 2, 64), 0, 8)
+    held = share_step(held, 1, 4)
+    qkv = lax.all_to_all(packed, "seq", 0, 0, tiled=True)
     heads = out_heads.transpose(1, 0, 2)
-    qkv, looked, heads = lax.optimization_barrier((qkv, looked, heads))
+    held, qkv, heads = lax.optimization_barrier((held, qkv, heads))
+    held = share_step(held, 2, 2)
+    context = attend(qkv)
+    held, context = lax.optimization_barrier((held, context))
+    context = lax.all_to_all(context, "seq", 0, 0, tiled=True)
+    held = share_step(held, 3, 1)
+    targets = held.reshape(FRAMES, CODEBOOKS)
     small = (norm_gain[:, None, :], out_bias[:, None, :], targets)
-
-    context = lax.all_to_all(
-        attend(qkv), "seq", 0, 0, tiled=True
-    )
     mine = 2 * core
     other = 2 - mine
-    acts_shape = jax.ShapeDtypeStruct((2, 2, FRAMES, DEPTH_DIM), jnp.bfloat16)
-    losses_shape = jax.ShapeDtypeStruct((FRAMES, 2), jnp.float32)
-    projected, acts_other, losses_other = depth_call(
-        True,
-        (
-            jax.ShapeDtypeStruct((FRAMES, DEPTH_DIM), jnp.float32),
-            pltpu.HBM(acts_shape.shape, acts_shape.dtype),
-            losses_shape,
-        ),
-        other,
-        (context, depth_in, looked, heads),
-        small,
+    looked = lookup(targets, code_embed)
+    projected, acts_other, losses_other, *staged = depth_first(
+        jnp.stack([other, mine]), context, small, depth_in, pltpu.with_memory_space_constraint(looked, pltpu.HBM), heads
     )
     came = swap_wide(acts_other, 1)
-    acts_mine, losses_mine = depth_call(
-        False, (acts_shape, losses_shape), mine, (projected, looked, heads), small
-    )
+    acts_mine, losses_mine = depth_second(mine, projected, *staged, small)
     shares = lax.all_to_all(outer(acts_mine, came), ("seq", "wide"), 0, 0, tiled=True)
     grad_scale = (VOCAB / (SEQ * WIDE * FRAMES)) ** 0.5
     head_grads = total(shares, grad_scale)

time: 185 us -> 171 us (0.924)
  waiting for transfers between devices: 79.6 us -> 71.9 us
  starting transfers between devices: 40.7 us -> 36.9 us
  local copies, waits for them, and re-layouts: 16.2 us -> 13.8 us
    ppermute x9 -> x11, waiting for transfers between devices: 49.5 us -> 39.4 us  [swap_wide(): return lax.ppermute(array, 'wide', [(i, i ^ stride) for i in range(WIDE)])]
    all_to_all x2, starting transfers between devices: 24.5 us -> 17.6 us  [the longest x1 9.4 us: shards(): context = lax.all_to_all(context, 'seq', 0, 0, tiled=True)]
    ppermute x9 -> x11, starting transfers between devices: 9.5 us -> 12.7 us  [swap_wide(): return lax.ppermute(array, 'wide', [(i, i ^ stride) for i in range(WIDE)])]
    unnamed x18, local copies, waits for them, and re-layouts: 14.9 us -> 12.1 us
    all_to_all x2, waiting for transfers between devices: 30.1 us -> 32.5 us  [the longest x1 26.2 us: shards(): qkv = lax.all_to_all(packed, 'seq', 0, 0, tiled=True)]
    pallas_call x1, Pallas kernels: 3.65 us -> 5.96 us  [lookup(): pl.pallas_call(lookup_kernel, out_shape=pltpu.HBM((CODEBOOKS, FRAMES, DEP...]
  transfers between devices with their start and end apart: 12 -> 14, of which waited for: 9 -> 8; matrix products, arithmetic and copies ran while one was open for 12% -> 13% of each run, Pallas kernels for 4% -> 10%
where the time goes in v4:
time: 171 us
  waiting for transfers between devices  71.9 us (42%)
  starting transfers between devices  36.9 us (22%)
  Pallas kernels  36.2 us (21%)
  local copies, waits for them, and re-layouts  13.8 us (8%)
  matrix products  7.73 us (5%)
  other arithmetic  3.28 us (2%)
    ppermute x11, waiting for transfers between devices, swap_wide(): return lax.ppermute(array, 'wide', [(i, i ^ stride) for i in range(WIDE)])  39.4 us
    all_to_all x1, waiting for transfers between devices, shards(): qkv = lax.all_to_all(packed, 'seq', 0, 0, tiled=True)  26.2 us
    ppermute x11, starting transfers between devices, swap_wide(): return lax.ppermute(array, 'wide', [(i, i ^ stride) for i in range(WIDE)])  12.7 us
    unnamed x18, local copies, waits for them, and re-layouts  12.1 us
    pallas_call x1, Pallas kernels, attend(): pl.pallas_call(attend_kernel, out_shape=pltpu.HBM((SEQ, FRAMES, PAIR), jn...  9.52 us
    all_to_all x1, starting transfers between devices, shards(): context = lax.all_to_all(context, 'seq', 0, 0, tiled=True)  9.4 us
    pallas_call x1, Pallas kernels, depth_first(): pl.pallas_call(first_kernel, out_shape=(jax.ShapeDtypeStruct((FRAMES, DEP...  8.5 us
    all_to_all x1, starting transfers between devices, shards(): qkv = lax.all_to_all(packed, 'seq', 0, 0, tiled=True)  8.15 us
  transfers between devices with their start and end apart: 14, of which 8 were waited for; matrix products, arithmetic and copies ran while one was open for 13% of the time, Pallas kernels for 10%

profile of v4, /device:TPU:2, one launch (start us, length us, event | category | flops | bytes accessed | tf_op | source)
XLA Modules:
  0.0 170.9 jit_solution(3119530381567283956)
XLA Ops:
  0.6 3.7 %shard_map.112 = bf16[8,256,768]{2,1,0:T(8,128)(2,1)} custom-call(bf16[1,256,2048]{2,1,0:T(8,128)(2,1)} %queries.1, bf16[1,256,2048]{2,1,0:T(8,128)(2,1)} %key_vectors.1, bf16[1,256,2048]{2,1,0:T(8,128)(2,1)} %values.1), custom_call_target="tpu_custom_call" | custom-call | bytes 6291456 | tf_op jit(solution)/shard_map/pallas_call | solution.py:134
  4.3 8.2 %all-to-all-start = ((bf16[8,256,768]{2,1,0:T(8,128)(2,1)}), bf16[8,256,768]{2,1,0:T(8,128)(2,1)S(1)}, u32[]{:S(2)}, u32[]{:S(2)}) async-start(bf16[8,256,768]{2,1,0:T(8,128)(2,1)} %shard_map.112), calls=%async_computation | async-start | bytes 6291456 | tf_op jit(solution)/shard_map/all_to_all | solution.py:486
  12.7 3.3 %collective-permute-start = (s32[1,2,2,2,64]{4,3,2,1,0:T(2,128)S(1)}, s32[1,2,2,2,64]{4,3,2,1,0:T(2,128)S(1)}, u32[]{:S(2)}, u32[]{:S(2)}) collective-permute-start(s32[1,2,2,2,64]{4,3,2,1,0:T(2,128)S(1)} %select_n.182), channel_id=1, source_target_pairs={{0,8},{1,9},{2,10},{3,11},{4,12},{5,13},{6,14},{7,15},{8,0},{9,1},... | collective-permute-start | bytes 6152 | tf_op jit(solution)/shard_map/ppermute | solution.py:451
  16.2 1.7 collective-permute-done
  17.9 1.7 collective-permute-start.1
  19.6 9.5 %copy.75 = bf16[1024,4,1024]{2,0,1:T(8,128)(2,1)} copy(bf16[1024,4,1024]{2,1,0:T(4,128)(2,1)} %param.16) | data formatting | bytes 16777216 | tf_op args[7]
  29.1 26.2 %all-to-all-done.qkv = bf16[8,256,768]{2,1,0:T(8,128)(2,1)S(1)} async-done(((bf16[8,256,768]{2,1,0:T(8,128)(2,1)}), bf16[8,256,768]{2,1,0:T(8,128)(2,1)S(1)}, u32[]{:S(2)}, u32[]{:S(2)}) %all-to-all-start) | async-done | bytes 3145760 | tf_op jit(solution)/shard_map/all_to_all | solution.py:486
  55.3 1.3 collective-permute-start.2
  56.6 9.5 %shard_map.113 = bf16[8,256,256]{2,1,0:T(8,128)(2,1)} custom-call(bf16[8,256,768]{2,1,0:T(8,128)(2,1)S(1)} %all-to-all-done.qkv), custom_call_target="tpu_custom_call" | custom-call | flops 2415919104 | bytes 4194304 | tf_op jit(solution)/shard_map/pallas_call | solution.py:82
  66.2 9.4 %all-to-all-start.1 = ((bf16[8,256,256]{2,1,0:T(8,128)(2,1)}), bf16[8,256,256]{2,1,0:T(8,128)(2,1)S(1)}, u32[]{:S(2)}, u32[]{:S(2)}) async-start(bf16[8,256,256]{2,1,0:T(8,128)(2,1)} %shard_map.113), calls=%async_computation.1 | async-start | bytes 2097152 | tf_op jit(solution)/shard_map/all_to_all | solution.py:492
  76.0 1.0 collective-permute-done.3
  77.1 0.8 reshape.125.target
  77.9 6.0 %shard_map.114.looked_hbm = bf16[4,256,1024]{2,1,0:T(8,128)(2,1)} custom-call(s32[256,4]{1,0:T(8,128)} %reshape.125.target, bf16[3,1024,1024]{2,1,0:T(8,128)(2,1)} %table_hbm.1), custom_call_target="tpu_custom_call" | custom-call | flops 1610612736 | bytes 10485760 | tf_op jit(solution)/shard_map/pallas_call | solution.py:176
  83.8 6.3 %all-to-all-done.1.ctx = bf16[8,256,256]{2,1,0:T(8,128)(2,1)S(1)} async-done(((bf16[8,256,256]{2,1,0:T(8,128)(2,1)}), bf16[8,256,256]{2,1,0:T(8,128)(2,1)S(1)}, u32[]{:S(2)}, u32[]{:S(2)}) %all-to-all-start.1) | async-done | bytes 1048608 | tf_op jit(solution)/shard_map/all_to_all | solution.py:492
  90.1 8.5 %shard_map.115 = (f32[256,1024]{1,0:T(8,128)S(1)}, bf16[2,2,256,1024]{3,2,1,0:T(8,128)(2,1)}, f32[256,2]{1,0:T(8,128)S(1)}, bf16[2,256,1024]{2,1,0:T(8,128)(2,1)S(1)}, bf16[2,1024,1024]{2,1,0:T(8,128)(2,1)S(1)}) custom-call(s32[2]{0:T(128)S(1)} %pad_add_fusion.4.book, bf16[8,256,256]{2,1,0:T(8,128)(2,1)S(1)} %all-to-all-done.1.ctx, ...), custom_call_target="tpu_custom_call" | custom-call | flops 1073741824 | bytes 8388608 | tf_op jit(solution)/shard_map/pallas_call | solution.py:317
  98.7 2.3 %shard_map.116 = (bf16[2,2,256,1024]{3,2,1,0:T(8,128)(2,1)S(1)}, f32[256,2]{1,0:T(8,128)S(1)}) custom-call(s32[1]{0:T(128)} %bitcast.book, f32[256,1024]{1,0:T(8,128)S(1)} %get-tuple-element.26.projected, bf16[2,256,1024]{2,1,0:T(8,128)(2,1)S(1)} %get-tuple-element.27.embed, bf16[2,1024,1024]{2,1,0:T(8,128)(2,1)S(1)} %get-tuple-element.28.heads, ...), custom_call_target="tpu_custom_call" | custom-call | flops 1073741824 | bytes 8388608 | tf_op jit(solution)/shard_map/pallas_call | solution.py:344
  101.7 1.4 collective-permute-done.10.theirs
  103.1 3.3 %shard_map.117 = bf16[128,16,1024]{2,1,0:T(8,128)(2,1)} custom-call(bf16[2,2,256,1024]{3,2,1,0:T(8,128)(2,1)S(1)} %get-tuple-element.31.mine, bf16[2,2,256,1024]{3,2,1,0:T(8,128)(2,1)S(1)} %collective-permute-done.10.theirs), custom_call_target="tpu_custom_call" | custom-call | flops 2147483648 | bytes 8388608 | tf_op jit(solution)/shard_map/pallas_call | solution.py:384
  106.4 6.6 %all-to-all-start.2 = ((bf16[128,16,1024]{2,1,0:T(8,128)(2,1)}), bf16[128,16,1024]{2,1,0:T(8,128)(2,1)}, u32[]{:S(2)}, u32[]{:S(2)}) async-start(bf16[128,16,1024]{2,1,0:T(8,128)(2,1)} %shard_map.117), calls=%async_computation.2 | async-start | bytes 8388608 | tf_op jit(solution)/shard_map/all_to_all | solution.py:504
  113.2 1.5 select_bitcast_fusion.1
  115.1 5.5 %multiply_reduce_fusion.1 = (f32[4,256]{1,0:T(4,128)S(1)}, f32[4,256]{1,0:T(4,128)S(1)}, f32[4,256,1024]{2,1,0:T(8,128)S(1)}) fusion(bf16[4,256,1024]{2,1,0:T(8,128)(2,1)S(1)} %copy-done.3, f32[256,1024]{1,0:T(8,128)S(1)} %get-tuple-element.26.projected, f32[4,1024]{1,0:T(4,128)S(1)} %copy-done.5, bf16[4,1024,1024]{2,1,0:T(8,128)(2,1)} %bitcast.33, ...), kind=kOutput, calls=%fused_computation.4 | convolution fusion | flops 2155870208 | bytes 17850368 | tf_op jit(solution)/shard_map/cnv,cev->cne/dot_general | solution.py:517
  120.6 1.3 fusion
  121.9 0.8 copy-done.4
  122.8 2.3 %convolution_convert_fusion = bf16[256,2048]{1,0:T(8,128)(2,1)} fusion(bf16[2048,1024]{1,0:T(8,128)(2,1)S(1)} %copy-done.4, bf16[256,1024]{1,0:T(8,128)(2,1)S(1)} %fusion), kind=kOutput, calls=%fused_computation.6 | convolution fusion | flops 1074266112 | bytes 5767168 | tf_op jit(solution)/shard_map/dot_general | solution.py:520
  125.4 2.8 %collective-permute-start.6 = (f32[4,64]{1,0:T(4,128)S(1)}, f32[4,64]{1,0:T(4,128)S(1)}, u32[]{:S(2)}, u32[]{:S(2)}) collective-permute-start(f32[4,64]{1,0:T(4,128)S(1)} %get-tuple-element.64), channel_id=1, source_target_pairs={{0,12},{1,13},{2,14},{3,15},{4,8},{5,9},{6,10},{7,11},{8,4},{9,5},... | collective-permute-start | bytes 3080 | tf_op jit(solution)/shard_map/ppermute | solution.py:451
  128.2 0.8 collective-permute-start.5
  129.6 33.4 %collective-permute-done.6 = f32[4,64]{1,0:T(4,128)S(1)} collective-permute-done((f32[4,64]{1,0:T(4,128)S(1)}, f32[4,64]{1,0:T(4,128)S(1)}, u32[]{:S(2)}, u32[]{:S(2)}) %collective-permute-start.6) | collective-permute-done | bytes 1056 | tf_op jit(solution)/shard_map/ppermute | solution.py:451
  163.1 1.8 %collective-permute-start.8 = (f32[4,64]{1,0:T(4,128)S(1)}, f32[4,64]{1,0:T(4,128)S(1)}, u32[]{:S(2)}, u32[]{:S(2)}) collective-permute-start(f32[4,64]{1,0:T(4,128)S(1)} %bitcast.41), channel_id=1, source_target_pairs={{0,2},{1,3},{2,0},{3,1},{4,6},{5,7},{6,4},{7,5},{8,10},{9,11},{10,... | collective-permute-start | bytes 3080 | tf_op jit(solution)/shard_map/ppermute | solution.py:451
  165.0 1.1 collective-permute-done.9
  166.1 0.7 collective-permute-done.8
  167.0 0.7 copy.70
  167.7 3.0 %shard_map.118 = f32[8,4,1024]{2,1,0:T(4,128)} custom-call(bf16[64,2,16,1024]{3,2,1,0:T(8,128)(2,1)} %bitcast.18.shares_hbm), custom_call_target="tpu_custom_call" | custom-call | flops 2097152 | bytes 4194304 | tf_op jit(solution)/shard_map/pallas_call | solution.py:426
  (60 shorter events, 3.6 us)
Async XLA Ops:
  4.3 8.2 %copy-start.6 = (s32[16,16,4]{1,2,0:T(4,128)S(1)}, s32[16,16,4]{1,2,0:T(4,128)}, u32[]{:S(2)}) copy-start(s32[16,16,4]{1,2,0:T(4,128)} %param.12) | copy-start | bytes 12292
  4.3 51.0 %all-to-all-start = ((bf16[8,256,768]{2,1,0:T(8,128)(2,1)}), bf16[8,256,768]{2,1,0:T(8,128)(2,1)S(1)}, u32[]{:S(2)}, u32[]{:S(2)}) async-start(bf16[8,256,768]{2,1,0:T(8,128)(2,1)} %shard_map.112), calls=%async_computation | async-start | bytes 6291456 | tf_op jit(solution)/shard_map/all_to_all | solution.py:486
  12.7 5.2 %collective-permute-start = (s32[1,2,2,2,64]{4,3,2,1,0:T(2,128)S(1)}, s32[1,2,2,2,64]{4,3,2,1,0:T(2,128)S(1)}, u32[]{:S(2)}, u32[]{:S(2)}) collective-permute-start(s32[1,2,2,2,64]{4,3,2,1,0:T(2,128)S(1)} %select_n.182), channel_id=1, source_target_pairs={{0,8},{1,9},{2,10},{3,11},{4,12},{5,13},{6,14},{7,15},{8,0},{9,1},... | collective-permute-start | bytes 6152 | tf_op jit(solution)/shard_map/ppermute | solution.py:451
  17.9 11.2 %collective-permute-start.1 = (s32[2,1,2,2,64]{4,3,2,1,0:T(2,128)S(1)}, s32[2,1,2,2,64]{4,3,2,1,0:T(2,128)S(1)}, u32[]{:S(2)}, u32[]{:S(2)}) collective-permute-start(s32[2,1,2,2,64]{4,3,2,1,0:T(2,128)S(1)} %broadcast_select_fusion.9), channel_id=1, source_target_pairs={{0,4},{1,5},{2,6},{3,7},{4,0},{5,1},{6,2},{7,3},{8,12},{9,13},{10,... | collective-permute-start | bytes 6152 | tf_op jit(solution)/shard_map/ppermute | solution.py:451
  55.3 20.7 %copy-start.5 = (f32[4,1024]{1,0:T(4,128)S(1)}, f32[4,1024]{1,0:T(4,128)}, u32[]{:S(2)}) copy-start(f32[4,1024]{1,0:T(4,128)} %param.15) | copy-start | bytes 49156
  55.3 20.7 %copy-start.7 = (f32[4,1024]{1,0:T(4,128)S(1)}, f32[4,1024]{1,0:T(4,128)}, u32[]{:S(2)}) copy-start(f32[4,1024]{1,0:T(4,128)} %param.17) | copy-start | bytes 49156
  55.3 10.8 %collective-permute-start.2 = (s32[2,2,1,2,64]{4,3,2,1,0:T(2,128)S(1)}, s32[2,2,1,2,64]{4,3,2,1,0:T(2,128)S(1)}, u32[]{:S(2)}, u32[]{:S(2)}) collective-permute-start(s32[2,2,1,2,64]{4,3,2,1,0:T(2,128)S(1)} %broadcast_select_fusion.13), channel_id=1, source_target_pairs={{0,2},{1,3},{2,0},{3,1},{4,6},{5,7},{6,4},{7,5},{8,10},{9,11},{10,... | collective-permute-start | bytes 6152 | tf_op jit(solution)/shard_map/ppermute | solution.py:451
  66.2 23.9 %all-to-all-start.1 = ((bf16[8,256,256]{2,1,0:T(8,128)(2,1)}), bf16[8,256,256]{2,1,0:T(8,128)(2,1)S(1)}, u32[]{:S(2)}, u32[]{:S(2)}) async-start(bf16[8,256,256]{2,1,0:T(8,128)(2,1)} %shard_map.113), calls=%async_computation.1 | async-start | bytes 2097152 | tf_op jit(solution)/shard_map/all_to_all | solution.py:492
  75.6 1.5 collective-permute-start.3
  77.8 12.2 %copy-start = (s32[256,4]{1,0:T(8,128)S(1)}, s32[256,4]{1,0:T(8,128)}, u32[]{:S(2)}) copy-start(s32[256,4]{1,0:T(8,128)} %reshape.125.target) | copy-start | bytes 12292
  98.6 4.5 %collective-permute-start.10 = (bf16[2,2,256,1024]{3,2,1,0:T(8,128)(2,1)}, bf16[2,2,256,1024]{3,2,1,0:T(8,128)(2,1)S(1)}, u32[]{:S(2)}, u32[]{:S(2)}) collective-permute-start(bf16[2,2,256,1024]{3,2,1,0:T(8,128)(2,1)} %get-tuple-element.32), channel_id=1, source_target_pairs={{0,1},{1,0},{2,3},{3,2},{4,5},{5,4},{6,7},{7,6},{8,9},{9,8},{10,11... | collective-permute-start | bytes 6291464 | tf_op jit(solution)/shard_map/ppermute | solution.py:451
  101.0 0.7 copy-start.1
  106.3 6.7 %copy-start.2 = (f32[256,2]{1,0:T(8,128)S(1)}, f32[256,2]{1,0:T(8,128)}, u32[]{:S(2)}) copy-start(f32[256,2]{1,0:T(8,128)} %copy-done.1) | copy-start | bytes 6148
  106.4 61.4 %all-to-all-start.2 = ((bf16[128,16,1024]{2,1,0:T(8,128)(2,1)}), bf16[128,16,1024]{2,1,0:T(8,128)(2,1)}, u32[]{:S(2)}, u32[]{:S(2)}) async-start(bf16[128,16,1024]{2,1,0:T(8,128)(2,1)} %shard_map.117), calls=%async_computation.2 | async-start | bytes 8388608 | tf_op jit(solution)/shard_map/all_to_all | solution.py:504
  113.2 1.9 %copy-start.3 = (bf16[4,256,1024]{2,1,0:T(8,128)(2,1)S(1)}, bf16[4,256,1024]{2,1,0:T(8,128)(2,1)}, u32[]{:S(2)}) copy-start(bf16[4,256,1024]{2,1,0:T(8,128)(2,1)} %shard_map.114.looked_hbm) | copy-start | bytes 6291460
  120.6 2.2 %copy-start.4 = (bf16[2048,1024]{1,0:T(8,128)(2,1)S(1)}, bf16[2048,1024]{1,0:T(8,128)(2,1)}, u32[]{:S(2)}) copy-start(bf16[2048,1024]{1,0:T(8,128)(2,1)} %depth_hbm.1) | copy-start | bytes 12582916
  125.4 37.6 %collective-permute-start.6 = (f32[4,64]{1,0:T(4,128)S(1)}, f32[4,64]{1,0:T(4,128)S(1)}, u32[]{:S(2)}, u32[]{:S(2)}) collective-permute-start(f32[4,64]{1,0:T(4,128)S(1)} %get-tuple-element.64), channel_id=1, source_target_pairs={{0,12},{1,13},{2,14},{3,15},{4,8},{5,9},{6,10},{7,11},{8,4},{9,5},... | collective-permute-start | bytes 3080 | tf_op jit(solution)/shard_map/ppermute | solution.py:451
  128.2 34.8 %collective-permute-start.5 = (f32[4,64]{1,0:T(4,128)S(1)}, f32[4,64]{1,0:T(4,128)S(1)}, u32[]{:S(2)}, u32[]{:S(2)}) collective-permute-start(f32[4,64]{1,0:T(4,128)S(1)} %get-tuple-element.65), channel_id=1, source_target_pairs={{0,8},{1,9},{2,10},{3,11},{4,12},{5,13},{6,14},{7,15},{8,0},{9,1},... | collective-permute-start | bytes 3080 | tf_op jit(solution)/shard_map/ppermute | solution.py:451
  129.0 34.0 %collective-permute-start.4 = (f32[4,64]{1,0:T(4,128)S(1)}, f32[4,64]{1,0:T(4,128)S(1)}, u32[]{:S(2)}, u32[]{:S(2)}) collective-permute-start(f32[4,64]{1,0:T(4,128)S(1)} %get-tuple-element.66), channel_id=1, source_target_pairs={{0,4},{1,5},{2,6},{3,7},{4,0},{5,1},{6,2},{7,3},{8,12},{9,13},{10,... | collective-permute-start | bytes 3080 | tf_op jit(solution)/shard_map/ppermute | solution.py:451
  163.1 3.1 %collective-permute-start.9 = (f32[4,64]{1,0:T(4,128)S(1)}, f32[4,64]{1,0:T(4,128)S(1)}, u32[]{:S(2)}, u32[]{:S(2)}) collective-permute-start(f32[4,64]{1,0:T(4,128)S(1)} %bitcast.44), channel_id=1, source_target_pairs={{0,3},{1,2},{2,1},{3,0},{4,7},{5,6},{6,5},{7,4},{8,11},{9,10},{10,... | collective-permute-start | bytes 3080 | tf_op jit(solution)/shard_map/ppermute | solution.py:451
  163.1 3.7 %collective-permute-start.8 = (f32[4,64]{1,0:T(4,128)S(1)}, f32[4,64]{1,0:T(4,128)S(1)}, u32[]{:S(2)}, u32[]{:S(2)}) collective-permute-start(f32[4,64]{1,0:T(4,128)S(1)} %bitcast.41), channel_id=1, source_target_pairs={{0,2},{1,3},{2,0},{3,1},{4,6},{5,7},{6,4},{7,5},{8,10},{9,11},{10,... | collective-permute-start | bytes 3080 | tf_op jit(solution)/shard_map/ppermute | solution.py:451
  165.0 1.8 %collective-permute-start.7 = (f32[4,64]{1,0:T(4,128)S(1)}, f32[4,64]{1,0:T(4,128)S(1)}, u32[]{:S(2)}, u32[]{:S(2)}) collective-permute-start(f32[4,64]{1,0:T(4,128)S(1)} %bitcast.38), channel_id=1, source_target_pairs={{0,1},{1,0},{2,3},{3,2},{4,5},{5,4},{6,7},{7,6},{8,9},{9,8},{10,11... | collective-permute-start | bytes 3080 | tf_op jit(solution)/shard_map/ppermute | solution.py:451

commit v5 on v4

--- a/solution.py
+++ b/solution.py
@@ -28,45 +28,52 @@
     row = lax.broadcasted_iota(jnp.int32, (FRAMES, FRAMES), 0)
     col = lax.broadcasted_iota(jnp.int32, (FRAMES, FRAMES), 1)
     across = (((1,), (1,)), ((), ()))
-    for block in range(SEQ):
-        for head in range(2):
-            at = head * HEAD_DIM
-            q = qkv[block, :, at : at + HEAD_DIM]
-            diag = lax.dot_general(
-                q,
-                qkv[block, :, PAIR + at : PAIR + at + HEAD_DIM],
-                across,
-                preferred_element_type=jnp.float32,
-            )
-            diag = jnp.where(col <= row, diag, -jnp.inf)
-            top = jnp.max(diag, axis=1, keepdims=True)
-            if block:
-                keys = qkv[:block, :, PAIR + at : PAIR + at + HEAD_DIM]
-                past = lax.dot_general(
-                    q,
-                    keys.reshape(block * FRAMES, HEAD_DIM),
-                    across,
-                    preferred_element_type=jnp.float32,
-                )
-                top = jnp.maximum(top, jnp.max(past, axis=1, keepdims=True))
-            weights = jnp.exp2((diag - top) * to_exp2)
-            total = jnp.sum(weights, axis=1, keepdims=True)
-            acc = jnp.dot(
-                weights.astype(jnp.bfloat16),
-                qkv[block, :, 2 * PAIR + at : 2 * PAIR + at + HEAD_DIM],
-                preferred_element_type=jnp.float32,
-            )
-            if block:
-                weights = jnp.exp2((past - top) * to_exp2)
-                total = total + jnp.sum(weights, axis=1, keepdims=True)
-                vals = qkv[:block, :, 2 * PAIR + at : 2 * PAIR + at + HEAD_DIM]
-                acc = acc + jnp.dot(
-                    weights.astype(jnp.bfloat16),
-                    vals.reshape(block * FRAMES, HEAD_DIM),
-                    preferred_element_type=jnp.float32,
-                )
-            out[block, :, at : at + HEAD_DIM] = (acc / total).astype(jnp.bfloat16)
-        stores[block].start()
+    ones = jnp.ones((LENGTH, HEAD_DIM), jnp.bfloat16)
+
+    def scores(block, head):
+        at = head * HEAD_DIM
+        q = qkv[block, :, at : at + HEAD_DIM]
+        diag = lax.dot_general(
+            q,
+            qkv[block, :, PAIR + at : PAIR + at + HEAD_DIM],
+            across,
+            preferred_element_type=jnp.float32,
+        )
+        if not block:
+            return (diag,)
+        keys = qkv[:block, :, PAIR + at : PAIR + at + HEAD_DIM]
+        past = lax.dot_general(
+            q,
+            keys.reshape(block * FRAMES, HEAD_DIM),
+            across,
+            preferred_element_type=jnp.float32,
+        )
+        return (diag, past)
+
+    def combine(block, head, parts):
+        at = 2 * PAIR + head * HEAD_DIM
+        parts = (jnp.where(col <= row, parts[0], -jnp.inf),) + parts[1:]
+        tops = [jnp.max(part, axis=1, keepdims=True) for part in parts]
+        top = tops[0] if not block else jnp.maximum(*tops)
+        acc = None
+        for part, first, last in zip(parts, (block, 0), (block + 1, block)):
+            weights = jnp.exp2((part - top) * to_exp2).astype(jnp.bfloat16)
+            vals = qkv[first:last, :, at : at + HEAD_DIM].reshape(-1, HEAD_DIM)
+            vals = jnp.concatenate((vals, ones[: vals.shape[0]]), axis=1)
+            term = jnp.dot(weights, vals, preferred_element_type=jnp.float32)
+            acc = term if acc is None else acc + term
+        out[block, :, head * HEAD_DIM : (head + 1) * HEAD_DIM] = (
+            acc[:, :HEAD_DIM] / acc[:, HEAD_DIM:]
+        ).astype(jnp.bfloat16)
+
+    tasks = [(block, head) for block in range(SEQ) for head in range(2)]
+    present = scores(*tasks[0])
+    for i, (block, head) in enumerate(tasks):
+        following = scores(*tasks[i + 1]) if i + 1 < len(tasks) else None
+        combine(block, head, present)
+        present = following
+        if head == 1:
+            stores[block].start()
     for copy in stores:
         copy.wait()
 

time: 171 us -> 168 us (0.982)
  Pallas kernels: 36.2 us -> 33.2 us
    pallas_call x1, Pallas kernels: 9.52 us -> 6.54 us  [attend(): pl.pallas_call(attend_kernel, out_shape=pltpu.HBM((SEQ, FRAMES, PAIR), jn...]
  transfers between devices with their start and end apart: 14 -> 14, of which waited for: 8 -> 8; matrix products, arithmetic and copies ran while one was open for 13% -> 14% of each run, Pallas kernels for 10% -> 9%
where the time goes in v5:
time: 168 us
  waiting for transfers between devices  71.9 us (43%)
  starting transfers between devices  36.7 us (22%)
  Pallas kernels  33.2 us (20%)
  local copies, waits for them, and re-layouts  13.8 us (8%)
  matrix products  7.74 us (5%)
  other arithmetic  3.28 us (2%)
    ppermute x11, waiting for transfers between devices, swap_wide(): return lax.ppermute(array, 'wide', [(i, i ^ stride) for i in range(WIDE)])  39.4 us
    all_to_all x1, waiting for transfers between devices, shards(): qkv = lax.all_to_all(packed, 'seq', 0, 0, tiled=True)  26.2 us
    ppermute x11, starting transfers between devices, swap_wide(): return lax.ppermute(array, 'wide', [(i, i ^ stride) for i in range(WIDE)])  12.5 us
    unnamed x18, local copies, waits for them, and re-layouts  12.1 us
    all_to_all x1, starting transfers between devices, shards(): context = lax.all_to_all(context, 'seq', 0, 0, tiled=True)  9.4 us
    pallas_call x1, Pallas kernels, depth_first(): pl.pallas_call(first_kernel, out_shape=(jax.ShapeDtypeStruct((FRAMES, DEP...  8.5 us
    all_to_all x1, starting transfers between devices, shards(): qkv = lax.all_to_all(packed, 'seq', 0, 0, tiled=True)  8.15 us
    all_to_all x1, starting transfers between devices, shards(): lax.all_to_all(outer(acts_mine, came), ('seq', 'wide'), 0, 0, tiled=True)  6.61 us
  transfers between devices with their start and end apart: 14, of which 8 were waited for; matrix products, arithmetic and copies ran while one was open for 14% of the time, Pallas kernels for 9%

profile of v5, /device:TPU:2, one launch (start us, length us, event | category | flops | bytes accessed | tf_op | source)
XLA Modules:
  0.0 167.7 jit_solution(3461878230414195111)
XLA Ops:
  0.6 3.6 %shard_map.112 = bf16[8,256,768]{2,1,0:T(8,128)(2,1)} custom-call(bf16[1,256,2048]{2,1,0:T(8,128)(2,1)} %queries.1, bf16[1,256,2048]{2,1,0:T(8,128)(2,1)} %key_vectors.1, bf16[1,256,2048]{2,1,0:T(8,128)(2,1)} %values.1), custom_call_target="tpu_custom_call" | custom-call | bytes 6291456 | tf_op jit(solution)/shard_map/pallas_call | solution.py:141
  4.3 8.2 %all-to-all-start = ((bf16[8,256,768]{2,1,0:T(8,128)(2,1)}), bf16[8,256,768]{2,1,0:T(8,128)(2,1)S(1)}, u32[]{:S(2)}, u32[]{:S(2)}) async-start(bf16[8,256,768]{2,1,0:T(8,128)(2,1)} %shard_map.112), calls=%async_computation | async-start | bytes 6291456 | tf_op jit(solution)/shard_map/all_to_all | solution.py:493
  12.7 3.3 %collective-permute-start = (s32[1,2,2,2,64]{4,3,2,1,0:T(2,128)S(1)}, s32[1,2,2,2,64]{4,3,2,1,0:T(2,128)S(1)}, u32[]{:S(2)}, u32[]{:S(2)}) collective-permute-start(s32[1,2,2,2,64]{4,3,2,1,0:T(2,128)S(1)} %select_n.182), channel_id=1, source_target_pairs={{0,8},{1,9},{2,10},{3,11},{4,12},{5,13},{6,14},{7,15},{8,0},{9,1},... | collective-permute-start | bytes 6152 | tf_op jit(solution)/shard_map/ppermute | solution.py:458
  16.2 1.7 %collective-permute-done = s32[1,2,2,2,64]{4,3,2,1,0:T(2,128)S(1)} collective-permute-done((s32[1,2,2,2,64]{4,3,2,1,0:T(2,128)S(1)}, s32[1,2,2,2,64]{4,3,2,1,0:T(2,128)S(1)}, u32[]{:S(2)}, u32[]{:S(2)}) %collective-permute-start) | collective-permute-done | bytes 2080 | tf_op jit(solution)/shard_map/ppermute | solution.py:458
  17.9 1.7 collective-permute-start.1
  19.5 9.5 %copy.75 = bf16[1024,4,1024]{2,0,1:T(8,128)(2,1)} copy(bf16[1024,4,1024]{2,1,0:T(4,128)(2,1)} %param.16) | data formatting | bytes 16777216 | tf_op args[7]
  29.1 26.2 %all-to-all-done.qkv = bf16[8,256,768]{2,1,0:T(8,128)(2,1)S(1)} async-done(((bf16[8,256,768]{2,1,0:T(8,128)(2,1)}), bf16[8,256,768]{2,1,0:T(8,128)(2,1)S(1)}, u32[]{:S(2)}, u32[]{:S(2)}) %all-to-all-start) | async-done | bytes 3145760 | tf_op jit(solution)/shard_map/all_to_all | solution.py:493
  55.3 1.1 collective-permute-start.2
  56.4 6.5 %shard_map.113 = bf16[8,256,256]{2,1,0:T(8,128)(2,1)} custom-call(bf16[8,256,768]{2,1,0:T(8,128)(2,1)S(1)} %all-to-all-done.qkv), custom_call_target="tpu_custom_call" | custom-call | flops 2415919104 | bytes 4194304 | tf_op jit(solution)/shard_map/pallas_call | solution.py:89
  63.0 9.4 %all-to-all-start.1 = ((bf16[8,256,256]{2,1,0:T(8,128)(2,1)}), bf16[8,256,256]{2,1,0:T(8,128)(2,1)S(1)}, u32[]{:S(2)}, u32[]{:S(2)}) async-start(bf16[8,256,256]{2,1,0:T(8,128)(2,1)} %shard_map.113), calls=%async_computation.1 | async-start | bytes 2097152 | tf_op jit(solution)/shard_map/all_to_all | solution.py:499
  72.8 1.0 collective-permute-done.3
  73.8 0.8 reshape.125.target
  74.6 6.0 %shard_map.114.looked_hbm = bf16[4,256,1024]{2,1,0:T(8,128)(2,1)} custom-call(s32[256,4]{1,0:T(8,128)} %reshape.125.target, bf16[3,1024,1024]{2,1,0:T(8,128)(2,1)} %table_hbm.1), custom_call_target="tpu_custom_call" | custom-call | flops 1610612736 | bytes 10485760 | tf_op jit(solution)/shard_map/pallas_call | solution.py:183
  80.6 6.3 %all-to-all-done.1.ctx = bf16[8,256,256]{2,1,0:T(8,128)(2,1)S(1)} async-done(((bf16[8,256,256]{2,1,0:T(8,128)(2,1)}), bf16[8,256,256]{2,1,0:T(8,128)(2,1)S(1)}, u32[]{:S(2)}, u32[]{:S(2)}) %all-to-all-start.1) | async-done | bytes 1048608 | tf_op jit(solution)/shard_map/all_to_all | solution.py:499
  86.9 8.5 %shard_map.115 = (f32[256,1024]{1,0:T(8,128)S(1)}, bf16[2,2,256,1024]{3,2,1,0:T(8,128)(2,1)}, f32[256,2]{1,0:T(8,128)S(1)}, bf16[2,256,1024]{2,1,0:T(8,128)(2,1)S(1)}, bf16[2,1024,1024]{2,1,0:T(8,128)(2,1)S(1)}) custom-call(s32[2]{0:T(128)S(1)} %pad_add_fusion.4.book, bf16[8,256,256]{2,1,0:T(8,128)(2,1)S(1)} %all-to-all-done.1.ctx, ...), custom_call_target="tpu_custom_call" | custom-call | flops 1073741824 | bytes 8388608 | tf_op jit(solution)/shard_map/pallas_call | solution.py:324
  95.5 2.3 %shard_map.116 = (bf16[2,2,256,1024]{3,2,1,0:T(8,128)(2,1)S(1)}, f32[256,2]{1,0:T(8,128)S(1)}) custom-call(s32[1]{0:T(128)} %bitcast.book, f32[256,1024]{1,0:T(8,128)S(1)} %get-tuple-element.26.projected, bf16[2,256,1024]{2,1,0:T(8,128)(2,1)S(1)} %get-tuple-element.27.embed, bf16[2,1024,1024]{2,1,0:T(8,128)(2,1)S(1)} %get-tuple-element.28.heads, ...), custom_call_target="tpu_custom_call" | custom-call | flops 1073741824 | bytes 8388608 | tf_op jit(solution)/shard_map/pallas_call | solution.py:351
  98.5 1.4 collective-permute-done.10.theirs
  99.8 3.3 %shard_map.117 = bf16[128,16,1024]{2,1,0:T(8,128)(2,1)} custom-call(bf16[2,2,256,1024]{3,2,1,0:T(8,128)(2,1)S(1)} %get-tuple-element.31.mine, bf16[2,2,256,1024]{3,2,1,0:T(8,128)(2,1)S(1)} %collective-permute-done.10.theirs), custom_call_target="tpu_custom_call" | custom-call | flops 2147483648 | bytes 8388608 | tf_op jit(solution)/shard_map/pallas_call | solution.py:391
  103.2 6.6 %all-to-all-start.2 = ((bf16[128,16,1024]{2,1,0:T(8,128)(2,1)}), bf16[128,16,1024]{2,1,0:T(8,128)(2,1)}, u32[]{:S(2)}, u32[]{:S(2)}) async-start(bf16[128,16,1024]{2,1,0:T(8,128)(2,1)} %shard_map.117), calls=%async_computation.2 | async-start | bytes 8388608 | tf_op jit(solution)/shard_map/all_to_all | solution.py:511
  110.0 1.5 select_bitcast_fusion.1
  111.9 5.5 %multiply_reduce_fusion.1 = (f32[4,256]{1,0:T(4,128)S(1)}, f32[4,256]{1,0:T(4,128)S(1)}, f32[4,256,1024]{2,1,0:T(8,128)S(1)}) fusion(bf16[4,256,1024]{2,1,0:T(8,128)(2,1)S(1)} %copy-done.3, f32[256,1024]{1,0:T(8,128)S(1)} %get-tuple-element.26.projected, f32[4,1024]{1,0:T(4,128)S(1)} %copy-done.5, bf16[4,1024,1024]{2,1,0:T(8,128)(2,1)} %bitcast.33, ...), kind=kOutput, calls=%fused_computation.4 | convolution fusion | flops 2155870208 | bytes 17850368 | tf_op jit(solution)/shard_map/cnv,cev->cne/dot_general | solution.py:524
  117.4 1.3 fusion
  118.7 0.8 copy-done.4
  119.6 2.3 %convolution_convert_fusion = bf16[256,2048]{1,0:T(8,128)(2,1)} fusion(bf16[2048,1024]{1,0:T(8,128)(2,1)S(1)} %copy-done.4, bf16[256,1024]{1,0:T(8,128)(2,1)S(1)} %fusion), kind=kOutput, calls=%fused_computation.6 | convolution fusion | flops 1074266112 | bytes 5767168 | tf_op jit(solution)/shard_map/dot_general | solution.py:527
  122.2 2.8 %collective-permute-start.6 = (f32[4,64]{1,0:T(4,128)S(1)}, f32[4,64]{1,0:T(4,128)S(1)}, u32[]{:S(2)}, u32[]{:S(2)}) collective-permute-start(f32[4,64]{1,0:T(4,128)S(1)} %get-tuple-element.64), channel_id=1, source_target_pairs={{0,12},{1,13},{2,14},{3,15},{4,8},{5,9},{6,10},{7,11},{8,4},{9,5},... | collective-permute-start | bytes 3080 | tf_op jit(solution)/shard_map/ppermute | solution.py:458
  125.1 0.8 collective-permute-start.5
  126.4 33.4 %collective-permute-done.6 = f32[4,64]{1,0:T(4,128)S(1)} collective-permute-done((f32[4,64]{1,0:T(4,128)S(1)}, f32[4,64]{1,0:T(4,128)S(1)}, u32[]{:S(2)}, u32[]{:S(2)}) %collective-permute-start.6) | collective-permute-done | bytes 1056 | tf_op jit(solution)/shard_map/ppermute | solution.py:458
  160.0 1.8 %collective-permute-start.8 = (f32[4,64]{1,0:T(4,128)S(1)}, f32[4,64]{1,0:T(4,128)S(1)}, u32[]{:S(2)}, u32[]{:S(2)}) collective-permute-start(f32[4,64]{1,0:T(4,128)S(1)} %bitcast.41), channel_id=1, source_target_pairs={{0,2},{1,3},{2,0},{3,1},{4,6},{5,7},{6,4},{7,5},{8,10},{9,11},{10,... | collective-permute-start | bytes 3080 | tf_op jit(solution)/shard_map/ppermute | solution.py:458
  161.8 1.1 collective-permute-done.9
  163.0 0.7 collective-permute-done.8
  163.9 0.7 copy.70
  164.6 3.0 %shard_map.118 = f32[8,4,1024]{2,1,0:T(4,128)} custom-call(bf16[64,2,16,1024]{3,2,1,0:T(8,128)(2,1)} %bitcast.18.shares_hbm), custom_call_target="tpu_custom_call" | custom-call | flops 2097152 | bytes 4194304 | tf_op jit(solution)/shard_map/pallas_call | solution.py:433
  (60 shorter events, 3.5 us)
Async XLA Ops:
  4.3 8.2 %copy-start.6 = (s32[16,16,4]{1,2,0:T(4,128)S(1)}, s32[16,16,4]{1,2,0:T(4,128)}, u32[]{:S(2)}) copy-start(s32[16,16,4]{1,2,0:T(4,128)} %param.12) | copy-start | bytes 12292
  4.3 51.0 %all-to-all-start = ((bf16[8,256,768]{2,1,0:T(8,128)(2,1)}), bf16[8,256,768]{2,1,0:T(8,128)(2,1)S(1)}, u32[]{:S(2)}, u32[]{:S(2)}) async-start(bf16[8,256,768]{2,1,0:T(8,128)(2,1)} %shard_map.112), calls=%async_computation | async-start | bytes 6291456 | tf_op jit(solution)/shard_map/all_to_all | solution.py:493
  12.7 5.2 %collective-permute-start = (s32[1,2,2,2,64]{4,3,2,1,0:T(2,128)S(1)}, s32[1,2,2,2,64]{4,3,2,1,0:T(2,128)S(1)}, u32[]{:S(2)}, u32[]{:S(2)}) collective-permute-start(s32[1,2,2,2,64]{4,3,2,1,0:T(2,128)S(1)} %select_n.182), channel_id=1, source_target_pairs={{0,8},{1,9},{2,10},{3,11},{4,12},{5,13},{6,14},{7,15},{8,0},{9,1},... | collective-permute-start | bytes 6152 | tf_op jit(solution)/shard_map/ppermute | solution.py:458
  17.9 11.2 %collective-permute-start.1 = (s32[2,1,2,2,64]{4,3,2,1,0:T(2,128)S(1)}, s32[2,1,2,2,64]{4,3,2,1,0:T(2,128)S(1)}, u32[]{:S(2)}, u32[]{:S(2)}) collective-permute-start(s32[2,1,2,2,64]{4,3,2,1,0:T(2,128)S(1)} %broadcast_select_fusion.9), channel_id=1, source_target_pairs={{0,4},{1,5},{2,6},{3,7},{4,0},{5,1},{6,2},{7,3},{8,12},{9,13},{10,... | collective-permute-start | bytes 6152 | tf_op jit(solution)/shard_map/ppermute | solution.py:458
  55.3 17.5 %copy-start.5 = (f32[4,1024]{1,0:T(4,128)S(1)}, f32[4,1024]{1,0:T(4,128)}, u32[]{:S(2)}) copy-start(f32[4,1024]{1,0:T(4,128)} %param.15) | copy-start | bytes 49156
  55.3 17.5 %copy-start.7 = (f32[4,1024]{1,0:T(4,128)S(1)}, f32[4,1024]{1,0:T(4,128)}, u32[]{:S(2)}) copy-start(f32[4,1024]{1,0:T(4,128)} %param.17) | copy-start | bytes 49156
  55.3 7.6 %collective-permute-start.2 = (s32[2,2,1,2,64]{4,3,2,1,0:T(2,128)S(1)}, s32[2,2,1,2,64]{4,3,2,1,0:T(2,128)S(1)}, u32[]{:S(2)}, u32[]{:S(2)}) collective-permute-start(s32[2,2,1,2,64]{4,3,2,1,0:T(2,128)S(1)} %broadcast_select_fusion.13), channel_id=1, source_target_pairs={{0,2},{1,3},{2,0},{3,1},{4,6},{5,7},{6,4},{7,5},{8,10},{9,11},{10,... | collective-permute-start | bytes 6152 | tf_op jit(solution)/shard_map/ppermute | solution.py:458
  63.0 23.9 %all-to-all-start.1 = ((bf16[8,256,256]{2,1,0:T(8,128)(2,1)}), bf16[8,256,256]{2,1,0:T(8,128)(2,1)S(1)}, u32[]{:S(2)}, u32[]{:S(2)}) async-start(bf16[8,256,256]{2,1,0:T(8,128)(2,1)} %shard_map.113), calls=%async_computation.1 | async-start | bytes 2097152 | tf_op jit(solution)/shard_map/all_to_all | solution.py:499
  72.4 1.4 collective-permute-start.3
  74.6 12.3 %copy-start = (s32[256,4]{1,0:T(8,128)S(1)}, s32[256,4]{1,0:T(8,128)}, u32[]{:S(2)}) copy-start(s32[256,4]{1,0:T(8,128)} %reshape.125.target) | copy-start | bytes 12292
  95.4 4.5 %collective-permute-start.10 = (bf16[2,2,256,1024]{3,2,1,0:T(8,128)(2,1)}, bf16[2,2,256,1024]{3,2,1,0:T(8,128)(2,1)S(1)}, u32[]{:S(2)}, u32[]{:S(2)}) collective-permute-start(bf16[2,2,256,1024]{3,2,1,0:T(8,128)(2,1)} %get-tuple-element.32), channel_id=1, source_target_pairs={{0,1},{1,0},{2,3},{3,2},{4,5},{5,4},{6,7},{7,6},{8,9},{9,8},{10,11... | collective-permute-start | bytes 6291464 | tf_op jit(solution)/shard_map/ppermute | solution.py:458
  97.8 0.7 copy-start.1
  103.1 6.7 %copy-start.2 = (f32[256,2]{1,0:T(8,128)S(1)}, f32[256,2]{1,0:T(8,128)}, u32[]{:S(2)}) copy-start(f32[256,2]{1,0:T(8,128)} %copy-done.1) | copy-start | bytes 6148
  103.2 61.4 %all-to-all-start.2 = ((bf16[128,16,1024]{2,1,0:T(8,128)(2,1)}), bf16[128,16,1024]{2,1,0:T(8,128)(2,1)}, u32[]{:S(2)}, u32[]{:S(2)}) async-start(bf16[128,16,1024]{2,1,0:T(8,128)(2,1)} %shard_map.117), calls=%async_computation.2 | async-start | bytes 8388608 | tf_op jit(solution)/shard_map/all_to_all | solution.py:511
  110.0 1.9 %copy-start.3 = (bf16[4,256,1024]{2,1,0:T(8,128)(2,1)S(1)}, bf16[4,256,1024]{2,1,0:T(8,128)(2,1)}, u32[]{:S(2)}) copy-start(bf16[4,256,1024]{2,1,0:T(8,128)(2,1)} %shard_map.114.looked_hbm) | copy-start | bytes 6291460
  117.4 2.2 %copy-start.4 = (bf16[2048,1024]{1,0:T(8,128)(2,1)S(1)}, bf16[2048,1024]{1,0:T(8,128)(2,1)}, u32[]{:S(2)}) copy-start(bf16[2048,1024]{1,0:T(8,128)(2,1)} %depth_hbm.1) | copy-start | bytes 12582916
  122.2 37.6 %collective-permute-start.6 = (f32[4,64]{1,0:T(4,128)S(1)}, f32[4,64]{1,0:T(4,128)S(1)}, u32[]{:S(2)}, u32[]{:S(2)}) collective-permute-start(f32[4,64]{1,0:T(4,128)S(1)} %get-tuple-element.64), channel_id=1, source_target_pairs={{0,12},{1,13},{2,14},{3,15},{4,8},{5,9},{6,10},{7,11},{8,4},{9,5},... | collective-permute-start | bytes 3080 | tf_op jit(solution)/shard_map/ppermute | solution.py:458
  125.1 34.8 %collective-permute-start.5 = (f32[4,64]{1,0:T(4,128)S(1)}, f32[4,64]{1,0:T(4,128)S(1)}, u32[]{:S(2)}, u32[]{:S(2)}) collective-permute-start(f32[4,64]{1,0:T(4,128)S(1)} %get-tuple-element.65), channel_id=1, source_target_pairs={{0,8},{1,9},{2,10},{3,11},{4,12},{5,13},{6,14},{7,15},{8,0},{9,1},... | collective-permute-start | bytes 3080 | tf_op jit(solution)/shard_map/ppermute | solution.py:458
  125.9 34.0 %collective-permute-start.4 = (f32[4,64]{1,0:T(4,128)S(1)}, f32[4,64]{1,0:T(4,128)S(1)}, u32[]{:S(2)}, u32[]{:S(2)}) collective-permute-start(f32[4,64]{1,0:T(4,128)S(1)} %get-tuple-element.66), channel_id=1, source_target_pairs={{0,4},{1,5},{2,6},{3,7},{4,0},{5,1},{6,2},{7,3},{8,12},{9,13},{10,... | collective-permute-start | bytes 3080 | tf_op jit(solution)/shard_map/ppermute | solution.py:458
  159.9 3.1 %collective-permute-start.9 = (f32[4,64]{1,0:T(4,128)S(1)}, f32[4,64]{1,0:T(4,128)S(1)}, u32[]{:S(2)}, u32[]{:S(2)}) collective-permute-start(f32[4,64]{1,0:T(4,128)S(1)} %bitcast.44), channel_id=1, source_target_pairs={{0,3},{1,2},{2,1},{3,0},{4,7},{5,6},{6,5},{7,4},{8,11},{9,10},{10,... | collective-permute-start | bytes 3080 | tf_op jit(solution)/shard_map/ppermute | solution.py:458
  160.0 3.7 %collective-permute-start.8 = (f32[4,64]{1,0:T(4,128)S(1)}, f32[4,64]{1,0:T(4,128)S(1)}, u32[]{:S(2)}, u32[]{:S(2)}) collective-permute-start(f32[4,64]{1,0:T(4,128)S(1)} %bitcast.41), channel_id=1, source_target_pairs={{0,2},{1,3},{2,0},{3,1},{4,6},{5,7},{6,4},{7,5},{8,10},{9,11},{10,... | collective-permute-start | bytes 3080 | tf_op jit(solution)/shard_map/ppermute | solution.py:458
  161.8 1.8 %collective-permute-start.7 = (f32[4,64]{1,0:T(4,128)S(1)}, f32[4,64]{1,0:T(4,128)S(1)}, u32[]{:S(2)}, u32[]{:S(2)}) collective-permute-start(f32[4,64]{1,0:T(4,128)S(1)} %bitcast.38), channel_id=1, source_target_pairs={{0,1},{1,0},{2,3},{3,2},{4,5},{5,4},{6,7},{7,6},{8,9},{9,8},{10,11... | collective-permute-start | bytes 3080 | tf_op jit(solution)/shard_map/ppermute | solution.py:458

commit v6 on v5

--- a/solution.py
+++ b/solution.py
@@ -198,10 +198,11 @@
     )(target, table)
 
 
-def depth_head(projected, embed, gain, heads, bias, target):
+def depth_head(projected, embed, gain, heads, bias, target, keep):
     mixed = projected + embed.astype(jnp.float32)
     scale = lax.rsqrt(jnp.mean(mixed * mixed, axis=1, keepdims=True) + 1e-05)
     hidden = (mixed * scale * gain).astype(jnp.bfloat16)
+    keep(hidden)
     logits = jnp.dot(hidden, heads, preferred_element_type=jnp.float32) + bias
     top = jnp.max(logits, axis=1, keepdims=True)
     shifted = jnp.exp(logits - top)
@@ -210,7 +211,7 @@
     picked = jnp.sum(jnp.where(onehot, logits, 0.0), axis=1, keepdims=True)
     losses = top + jnp.log(total) - picked
     dlogits = (shifted / total - onehot.astype(jnp.float32)).astype(jnp.bfloat16)
-    return hidden, dlogits, losses
+    return dlogits, losses
 
 
 def depth_pair(
@@ -223,13 +224,16 @@
         if begin:
             begin(j)
         token = jnp.sum(jnp.where(lane == c, target[...], 0), axis=1, keepdims=True)
-        hidden, dlogits, loss = depth_head(
-            projected[...], embed[j], gain[c], heads[j], bias[c], token
+
+        def keep(kind, value, j=j):
+            acts[kind, j] = value
+            if finish:
+                finish(kind, j)
+
+        dlogits, loss = depth_head(
+            projected[...], embed[j], gain[c], heads[j], bias[c], token, partial(keep, 0)
         )
-        acts[0, j] = hidden
-        acts[1, j] = dlogits
-        if finish:
-            finish(j)
+        keep(1, dlogits)
         both.append(loss)
     pair_lane = lax.broadcasted_iota(jnp.int32, (FRAMES, 2), 1)
     losses[...] = jnp.where(pair_lane == 0, both[0], both[1])
@@ -279,14 +283,19 @@
         staged.append(
             pltpu.make_async_copy(heads_hbm.at[c], next_heads.at[j], next_sems.at[1, j])
         )
-    for copy in depth_copies + book_copies[0] + book_copies[1] + staged:
+    for copy in depth_copies + book_copies[0]:
         copy.start()
     total = None
     for part in range(SEQ):
         depth_copies[part].wait()
+        if part == SEQ // 2:
+            for copy in book_copies[1]:
+                copy.start()
         term = jnp.dot(ctx[part], depth_in[rows[part]], preferred_element_type=jnp.float32)
         total = term if total is None else total + term
     projected[...] = total
+    for copy in staged:
+        copy.start()
     stores = [
         [
             pltpu.make_async_copy(acts.at[kind, j], acts_hbm.at[kind, j], out_sems.at[kind, j])
@@ -299,9 +308,8 @@
         for copy in book_copies[j]:
             copy.wait()
 
-    def finish(j):
-        for copy in stores[j]:
-            copy.start()
+    def finish(kind, j):
+        stores[j][kind].start()
 
     depth_pair(book, projected, embed, heads, gain, bias, target, acts, losses, begin, finish)
     for copy in staged + stores[0] + stores[1]:

time: 168 us -> 167 us (level)
  no operation moved by 1% of the time
where the time goes in v6:
time: 167 us; the launch traced here: 166 us
  waiting for transfers between devices  71.9 us (43%)
  starting transfers between devices  36.6 us (22%)
  Pallas kernels  31.8 us (19%)
  local copies, waits for them, and re-layouts  13.8 us (8%)
  matrix products  7.73 us (5%)
  other arithmetic  3.28 us (2%)
    ppermute x11, waiting for transfers between devices, swap_wide(): return lax.ppermute(array, 'wide', [(i, i ^ stride) for i in range(WIDE)])  39.4 us
    all_to_all x1, waiting for transfers between devices, shards(): qkv = lax.all_to_all(packed, 'seq', 0, 0, tiled=True)  26.2 us
    ppermute x11, starting transfers between devices, swap_wide(): return lax.ppermute(array, 'wide', [(i, i ^ stride) for i in range(WIDE)])  12.5 us
    unnamed x18, local copies, waits for them, and re-layouts  12.1 us
    all_to_all x1, starting transfers between devices, shards(): context = lax.all_to_all(context, 'seq', 0, 0, tiled=True)  9.4 us
    all_to_all x1, starting transfers between devices, shards(): qkv = lax.all_to_all(packed, 'seq', 0, 0, tiled=True)  8.15 us
    pallas_call x1, Pallas kernels, depth_first(): pl.pallas_call(first_kernel, out_shape=(jax.ShapeDtypeStruct((FRAMES, DEP...  7.11 us
    all_to_all x1, starting transfers between devices, shards(): lax.all_to_all(outer(acts_mine, came), ('seq', 'wide'), 0, 0, tiled=True)  6.6 us
  transfers between devices with their start and end apart: 14, of which 8 were waited for; matrix products, arithmetic and copies ran while one was open for 14% of the time, Pallas kernels for 9%

profile of v6, /device:TPU:2, one launch (start us, length us, event | category | flops | bytes accessed | tf_op | source)
XLA Modules:
  0.0 166.3 jit_solution(16470337764840103491)
XLA Ops:
  0.6 3.6 %shard_map.112 = bf16[8,256,768]{2,1,0:T(8,128)(2,1)} custom-call(bf16[1,256,2048]{2,1,0:T(8,128)(2,1)} %queries.1, bf16[1,256,2048]{2,1,0:T(8,128)(2,1)} %key_vectors.1, bf16[1,256,2048]{2,1,0:T(8,128)(2,1)} %values.1), custom_call_target="tpu_custom_call" | custom-call | bytes 6291456 | tf_op jit(solution)/shard_map/pallas_call | solution.py:141
  4.3 8.2 %all-to-all-start = ((bf16[8,256,768]{2,1,0:T(8,128)(2,1)}), bf16[8,256,768]{2,1,0:T(8,128)(2,1)S(1)}, u32[]{:S(2)}, u32[]{:S(2)}) async-start(bf16[8,256,768]{2,1,0:T(8,128)(2,1)} %shard_map.112), calls=%async_computation | async-start | bytes 6291456 | tf_op jit(solution)/shard_map/all_to_all | solution.py:501
  12.7 3.3 %collective-permute-start = (s32[1,2,2,2,64]{4,3,2,1,0:T(2,128)S(1)}, s32[1,2,2,2,64]{4,3,2,1,0:T(2,128)S(1)}, u32[]{:S(2)}, u32[]{:S(2)}) collective-permute-start(s32[1,2,2,2,64]{4,3,2,1,0:T(2,128)S(1)} %select_n.182), channel_id=1, source_target_pairs={{0,8},{1,9},{2,10},{3,11},{4,12},{5,13},{6,14},{7,15},{8,0},{9,1},... | collective-permute-start | bytes 6152 | tf_op jit(solution)/shard_map/ppermute | solution.py:466
  16.2 1.7 %collective-permute-done = s32[1,2,2,2,64]{4,3,2,1,0:T(2,128)S(1)} collective-permute-done((s32[1,2,2,2,64]{4,3,2,1,0:T(2,128)S(1)}, s32[1,2,2,2,64]{4,3,2,1,0:T(2,128)S(1)}, u32[]{:S(2)}, u32[]{:S(2)}) %collective-permute-start) | collective-permute-done | bytes 2080 | tf_op jit(solution)/shard_map/ppermute | solution.py:466
  17.9 1.7 collective-permute-start.1
  19.5 9.5 %copy.75 = bf16[1024,4,1024]{2,0,1:T(8,128)(2,1)} copy(bf16[1024,4,1024]{2,1,0:T(4,128)(2,1)} %param.16) | data formatting | bytes 16777216 | tf_op args[7]
  29.1 26.2 %all-to-all-done.qkv = bf16[8,256,768]{2,1,0:T(8,128)(2,1)S(1)} async-done(((bf16[8,256,768]{2,1,0:T(8,128)(2,1)}), bf16[8,256,768]{2,1,0:T(8,128)(2,1)S(1)}, u32[]{:S(2)}, u32[]{:S(2)}) %all-to-all-start) | async-done | bytes 3145760 | tf_op jit(solution)/shard_map/all_to_all | solution.py:501
  55.3 1.1 collective-permute-start.2
  56.4 6.5 %shard_map.113 = bf16[8,256,256]{2,1,0:T(8,128)(2,1)} custom-call(bf16[8,256,768]{2,1,0:T(8,128)(2,1)S(1)} %all-to-all-done.qkv), custom_call_target="tpu_custom_call" | custom-call | flops 2415919104 | bytes 4194304 | tf_op jit(solution)/shard_map/pallas_call | solution.py:89
  63.0 9.4 %all-to-all-start.1 = ((bf16[8,256,256]{2,1,0:T(8,128)(2,1)}), bf16[8,256,256]{2,1,0:T(8,128)(2,1)S(1)}, u32[]{:S(2)}, u32[]{:S(2)}) async-start(bf16[8,256,256]{2,1,0:T(8,128)(2,1)} %shard_map.113), calls=%async_computation.1 | async-start | bytes 2097152 | tf_op jit(solution)/shard_map/all_to_all | solution.py:507
  72.8 1.0 collective-permute-done.3
  73.8 0.8 reshape.125.target
  74.6 6.0 %shard_map.114.looked_hbm = bf16[4,256,1024]{2,1,0:T(8,128)(2,1)} custom-call(s32[256,4]{1,0:T(8,128)} %reshape.125.target, bf16[3,1024,1024]{2,1,0:T(8,128)(2,1)} %table_hbm.1), custom_call_target="tpu_custom_call" | custom-call | flops 1610612736 | bytes 10485760 | tf_op jit(solution)/shard_map/pallas_call | solution.py:183
  80.6 6.3 %all-to-all-done.1.ctx = bf16[8,256,256]{2,1,0:T(8,128)(2,1)S(1)} async-done(((bf16[8,256,256]{2,1,0:T(8,128)(2,1)}), bf16[8,256,256]{2,1,0:T(8,128)(2,1)S(1)}, u32[]{:S(2)}, u32[]{:S(2)}) %all-to-all-start.1) | async-done | bytes 1048608 | tf_op jit(solution)/shard_map/all_to_all | solution.py:507
  86.9 7.1 %shard_map.115 = (f32[256,1024]{1,0:T(8,128)S(1)}, bf16[2,2,256,1024]{3,2,1,0:T(8,128)(2,1)}, f32[256,2]{1,0:T(8,128)S(1)}, bf16[2,256,1024]{2,1,0:T(8,128)(2,1)S(1)}, bf16[2,1024,1024]{2,1,0:T(8,128)(2,1)S(1)}) custom-call(s32[2]{0:T(128)S(1)} %pad_add_fusion.4.book, bf16[8,256,256]{2,1,0:T(8,128)(2,1)S(1)} %all-to-all-done.1.ctx, ...), custom_call_target="tpu_custom_call" | custom-call | flops 1073741824 | bytes 8388608 | tf_op jit(solution)/shard_map/pallas_call | solution.py:332
  94.1 2.3 %shard_map.116 = (bf16[2,2,256,1024]{3,2,1,0:T(8,128)(2,1)S(1)}, f32[256,2]{1,0:T(8,128)S(1)}) custom-call(s32[1]{0:T(128)} %bitcast.book, f32[256,1024]{1,0:T(8,128)S(1)} %get-tuple-element.26.projected, bf16[2,256,1024]{2,1,0:T(8,128)(2,1)S(1)} %get-tuple-element.27.embed, bf16[2,1024,1024]{2,1,0:T(8,128)(2,1)S(1)} %get-tuple-element.28.heads, ...), custom_call_target="tpu_custom_call" | custom-call | flops 1073741824 | bytes 8388608 | tf_op jit(solution)/shard_map/pallas_call | solution.py:359
  97.1 1.4 collective-permute-done.10.theirs
  98.5 3.3 %shard_map.117 = bf16[128,16,1024]{2,1,0:T(8,128)(2,1)} custom-call(bf16[2,2,256,1024]{3,2,1,0:T(8,128)(2,1)S(1)} %get-tuple-element.31.mine, bf16[2,2,256,1024]{3,2,1,0:T(8,128)(2,1)S(1)} %collective-permute-done.10.theirs), custom_call_target="tpu_custom_call" | custom-call | flops 2147483648 | bytes 8388608 | tf_op jit(solution)/shard_map/pallas_call | solution.py:399
  101.8 6.6 %all-to-all-start.2 = ((bf16[128,16,1024]{2,1,0:T(8,128)(2,1)}), bf16[128,16,1024]{2,1,0:T(8,128)(2,1)}, u32[]{:S(2)}, u32[]{:S(2)}) async-start(bf16[128,16,1024]{2,1,0:T(8,128)(2,1)} %shard_map.117), calls=%async_computation.2 | async-start | bytes 8388608 | tf_op jit(solution)/shard_map/all_to_all | solution.py:519
  108.6 1.5 select_bitcast_fusion.1
  110.5 5.5 %multiply_reduce_fusion.1 = (f32[4,256]{1,0:T(4,128)S(1)}, f32[4,256]{1,0:T(4,128)S(1)}, f32[4,256,1024]{2,1,0:T(8,128)S(1)}) fusion(bf16[4,256,1024]{2,1,0:T(8,128)(2,1)S(1)} %copy-done.3, f32[256,1024]{1,0:T(8,128)S(1)} %get-tuple-element.26.projected, f32[4,1024]{1,0:T(4,128)S(1)} %copy-done.5, bf16[4,1024,1024]{2,1,0:T(8,128)(2,1)} %bitcast.33, ...), kind=kOutput, calls=%fused_computation.4 | convolution fusion | flops 2155870208 | bytes 17850368 | tf_op jit(solution)/shard_map/cnv,cev->cne/dot_general | solution.py:532
  116.0 1.3 fusion
  117.3 0.8 copy-done.4
  118.2 2.3 %convolution_convert_fusion = bf16[256,2048]{1,0:T(8,128)(2,1)} fusion(bf16[2048,1024]{1,0:T(8,128)(2,1)S(1)} %copy-done.4, bf16[256,1024]{1,0:T(8,128)(2,1)S(1)} %fusion), kind=kOutput, calls=%fused_computation.6 | convolution fusion | flops 1074266112 | bytes 5767168 | tf_op jit(solution)/shard_map/dot_general | solution.py:535
  120.8 2.8 %collective-permute-start.6 = (f32[4,64]{1,0:T(4,128)S(1)}, f32[4,64]{1,0:T(4,128)S(1)}, u32[]{:S(2)}, u32[]{:S(2)}) collective-permute-start(f32[4,64]{1,0:T(4,128)S(1)} %get-tuple-element.64), channel_id=1, source_target_pairs={{0,12},{1,13},{2,14},{3,15},{4,8},{5,9},{6,10},{7,11},{8,4},{9,5},... | collective-permute-start | bytes 3080 | tf_op jit(solution)/shard_map/ppermute | solution.py:466
  123.6 0.8 collective-permute-start.5
  125.0 33.4 %collective-permute-done.6 = f32[4,64]{1,0:T(4,128)S(1)} collective-permute-done((f32[4,64]{1,0:T(4,128)S(1)}, f32[4,64]{1,0:T(4,128)S(1)}, u32[]{:S(2)}, u32[]{:S(2)}) %collective-permute-start.6) | collective-permute-done | bytes 1056 | tf_op jit(solution)/shard_map/ppermute | solution.py:466
  158.6 1.8 %collective-permute-start.8 = (f32[4,64]{1,0:T(4,128)S(1)}, f32[4,64]{1,0:T(4,128)S(1)}, u32[]{:S(2)}, u32[]{:S(2)}) collective-permute-start(f32[4,64]{1,0:T(4,128)S(1)} %bitcast.41), channel_id=1, source_target_pairs={{0,2},{1,3},{2,0},{3,1},{4,6},{5,7},{6,4},{7,5},{8,10},{9,11},{10,... | collective-permute-start | bytes 3080 | tf_op jit(solution)/shard_map/ppermute | solution.py:466
  160.4 1.1 collective-permute-done.9
  161.5 0.7 collective-permute-done.8
  162.4 0.7 copy.70
  163.1 3.0 %shard_map.118 = f32[8,4,1024]{2,1,0:T(4,128)} custom-call(bf16[64,2,16,1024]{3,2,1,0:T(8,128)(2,1)} %bitcast.18.shares_hbm), custom_call_target="tpu_custom_call" | custom-call | flops 2097152 | bytes 4194304 | tf_op jit(solution)/shard_map/pallas_call | solution.py:441
  (60 shorter events, 3.5 us)
Async XLA Ops:
  4.3 8.2 %copy-start.6 = (s32[16,16,4]{1,2,0:T(4,128)S(1)}, s32[16,16,4]{1,2,0:T(4,128)}, u32[]{:S(2)}) copy-start(s32[16,16,4]{1,2,0:T(4,128)} %param.12) | copy-start | bytes 12292
  4.3 51.0 %all-to-all-start = ((bf16[8,256,768]{2,1,0:T(8,128)(2,1)}), bf16[8,256,768]{2,1,0:T(8,128)(2,1)S(1)}, u32[]{:S(2)}, u32[]{:S(2)}) async-start(bf16[8,256,768]{2,1,0:T(8,128)(2,1)} %shard_map.112), calls=%async_computation | async-start | bytes 6291456 | tf_op jit(solution)/shard_map/all_to_all | solution.py:501
  12.7 5.2 %collective-permute-start = (s32[1,2,2,2,64]{4,3,2,1,0:T(2,128)S(1)}, s32[1,2,2,2,64]{4,3,2,1,0:T(2,128)S(1)}, u32[]{:S(2)}, u32[]{:S(2)}) collective-permute-start(s32[1,2,2,2,64]{4,3,2,1,0:T(2,128)S(1)} %select_n.182), channel_id=1, source_target_pairs={{0,8},{1,9},{2,10},{3,11},{4,12},{5,13},{6,14},{7,15},{8,0},{9,1},... | collective-permute-start | bytes 6152 | tf_op jit(solution)/shard_map/ppermute | solution.py:466
  17.9 11.2 %collective-permute-start.1 = (s32[2,1,2,2,64]{4,3,2,1,0:T(2,128)S(1)}, s32[2,1,2,2,64]{4,3,2,1,0:T(2,128)S(1)}, u32[]{:S(2)}, u32[]{:S(2)}) collective-permute-start(s32[2,1,2,2,64]{4,3,2,1,0:T(2,128)S(1)} %broadcast_select_fusion.9), channel_id=1, source_target_pairs={{0,4},{1,5},{2,6},{3,7},{4,0},{5,1},{6,2},{7,3},{8,12},{9,13},{10,... | collective-permute-start | bytes 6152 | tf_op jit(solution)/shard_map/ppermute | solution.py:466
  55.3 17.5 %copy-start.5 = (f32[4,1024]{1,0:T(4,128)S(1)}, f32[4,1024]{1,0:T(4,128)}, u32[]{:S(2)}) copy-start(f32[4,1024]{1,0:T(4,128)} %param.15) | copy-start | bytes 49156
  55.3 17.5 %copy-start.7 = (f32[4,1024]{1,0:T(4,128)S(1)}, f32[4,1024]{1,0:T(4,128)}, u32[]{:S(2)}) copy-start(f32[4,1024]{1,0:T(4,128)} %param.17) | copy-start | bytes 49156
  55.3 7.6 %collective-permute-start.2 = (s32[2,2,1,2,64]{4,3,2,1,0:T(2,128)S(1)}, s32[2,2,1,2,64]{4,3,2,1,0:T(2,128)S(1)}, u32[]{:S(2)}, u32[]{:S(2)}) collective-permute-start(s32[2,2,1,2,64]{4,3,2,1,0:T(2,128)S(1)} %broadcast_select_fusion.13), channel_id=1, source_target_pairs={{0,2},{1,3},{2,0},{3,1},{4,6},{5,7},{6,4},{7,5},{8,10},{9,11},{10,... | collective-permute-start | bytes 6152 | tf_op jit(solution)/shard_map/ppermute | solution.py:466
  63.0 23.9 %all-to-all-start.1 = ((bf16[8,256,256]{2,1,0:T(8,128)(2,1)}), bf16[8,256,256]{2,1,0:T(8,128)(2,1)S(1)}, u32[]{:S(2)}, u32[]{:S(2)}) async-start(bf16[8,256,256]{2,1,0:T(8,128)(2,1)} %shard_map.113), calls=%async_computation.1 | async-start | bytes 2097152 | tf_op jit(solution)/shard_map/all_to_all | solution.py:507
  72.4 1.4 collective-permute-start.3
  74.6 12.3 %copy-start = (s32[256,4]{1,0:T(8,128)S(1)}, s32[256,4]{1,0:T(8,128)}, u32[]{:S(2)}) copy-start(s32[256,4]{1,0:T(8,128)} %reshape.125.target) | copy-start | bytes 12292
  94.0 4.5 %collective-permute-start.10 = (bf16[2,2,256,1024]{3,2,1,0:T(8,128)(2,1)}, bf16[2,2,256,1024]{3,2,1,0:T(8,128)(2,1)S(1)}, u32[]{:S(2)}, u32[]{:S(2)}) collective-permute-start(bf16[2,2,256,1024]{3,2,1,0:T(8,128)(2,1)} %get-tuple-element.32), channel_id=1, source_target_pairs={{0,1},{1,0},{2,3},{3,2},{4,5},{5,4},{6,7},{7,6},{8,9},{9,8},{10,11... | collective-permute-start | bytes 6291464 | tf_op jit(solution)/shard_map/ppermute | solution.py:466
  96.4 0.7 copy-start.1
  101.8 6.7 %copy-start.2 = (f32[256,2]{1,0:T(8,128)S(1)}, f32[256,2]{1,0:T(8,128)}, u32[]{:S(2)}) copy-start(f32[256,2]{1,0:T(8,128)} %copy-done.1) | copy-start | bytes 6148
  101.8 61.4 %all-to-all-start.2 = ((bf16[128,16,1024]{2,1,0:T(8,128)(2,1)}), bf16[128,16,1024]{2,1,0:T(8,128)(2,1)}, u32[]{:S(2)}, u32[]{:S(2)}) async-start(bf16[128,16,1024]{2,1,0:T(8,128)(2,1)} %shard_map.117), calls=%async_computation.2 | async-start | bytes 8388608 | tf_op jit(solution)/shard_map/all_to_all | solution.py:519
  108.6 1.9 %copy-start.3 = (bf16[4,256,1024]{2,1,0:T(8,128)(2,1)S(1)}, bf16[4,256,1024]{2,1,0:T(8,128)(2,1)}, u32[]{:S(2)}) copy-start(bf16[4,256,1024]{2,1,0:T(8,128)(2,1)} %shard_map.114.looked_hbm) | copy-start | bytes 6291460
  116.0 2.2 %copy-start.4 = (bf16[2048,1024]{1,0:T(8,128)(2,1)S(1)}, bf16[2048,1024]{1,0:T(8,128)(2,1)}, u32[]{:S(2)}) copy-start(bf16[2048,1024]{1,0:T(8,128)(2,1)} %depth_hbm.1) | copy-start | bytes 12582916
  120.8 37.6 %collective-permute-start.6 = (f32[4,64]{1,0:T(4,128)S(1)}, f32[4,64]{1,0:T(4,128)S(1)}, u32[]{:S(2)}, u32[]{:S(2)}) collective-permute-start(f32[4,64]{1,0:T(4,128)S(1)} %get-tuple-element.64), channel_id=1, source_target_pairs={{0,12},{1,13},{2,14},{3,15},{4,8},{5,9},{6,10},{7,11},{8,4},{9,5},... | collective-permute-start | bytes 3080 | tf_op jit(solution)/shard_map/ppermute | solution.py:466
  123.6 34.8 %collective-permute-start.5 = (f32[4,64]{1,0:T(4,128)S(1)}, f32[4,64]{1,0:T(4,128)S(1)}, u32[]{:S(2)}, u32[]{:S(2)}) collective-permute-start(f32[4,64]{1,0:T(4,128)S(1)} %get-tuple-element.65), channel_id=1, source_target_pairs={{0,8},{1,9},{2,10},{3,11},{4,12},{5,13},{6,14},{7,15},{8,0},{9,1},... | collective-permute-start | bytes 3080 | tf_op jit(solution)/shard_map/ppermute | solution.py:466
  124.4 34.0 %collective-permute-start.4 = (f32[4,64]{1,0:T(4,128)S(1)}, f32[4,64]{1,0:T(4,128)S(1)}, u32[]{:S(2)}, u32[]{:S(2)}) collective-permute-start(f32[4,64]{1,0:T(4,128)S(1)} %get-tuple-element.66), channel_id=1, source_target_pairs={{0,4},{1,5},{2,6},{3,7},{4,0},{5,1},{6,2},{7,3},{8,12},{9,13},{10,... | collective-permute-start | bytes 3080 | tf_op jit(solution)/shard_map/ppermute | solution.py:466
  158.5 3.1 %collective-permute-start.9 = (f32[4,64]{1,0:T(4,128)S(1)}, f32[4,64]{1,0:T(4,128)S(1)}, u32[]{:S(2)}, u32[]{:S(2)}) collective-permute-start(f32[4,64]{1,0:T(4,128)S(1)} %bitcast.44), channel_id=1, source_target_pairs={{0,3},{1,2},{2,1},{3,0},{4,7},{5,6},{6,5},{7,4},{8,11},{9,10},{10,... | collective-permute-start | bytes 3080 | tf_op jit(solution)/shard_map/ppermute | solution.py:466
  158.6 3.7 %collective-permute-start.8 = (f32[4,64]{1,0:T(4,128)S(1)}, f32[4,64]{1,0:T(4,128)S(1)}, u32[]{:S(2)}, u32[]{:S(2)}) collective-permute-start(f32[4,64]{1,0:T(4,128)S(1)} %bitcast.41), channel_id=1, source_target_pairs={{0,2},{1,3},{2,0},{3,1},{4,6},{5,7},{6,4},{7,5},{8,10},{9,11},{10,... | collective-permute-start | bytes 3080 | tf_op jit(solution)/shard_map/ppermute | solution.py:466
  160.4 1.8 %collective-permute-start.7 = (f32[4,64]{1,0:T(4,128)S(1)}, f32[4,64]{1,0:T(4,128)S(1)}, u32[]{:S(2)}, u32[]{:S(2)}) collective-permute-start(f32[4,64]{1,0:T(4,128)S(1)} %bitcast.38), channel_id=1, source_target_pairs={{0,1},{1,0},{2,3},{3,2},{4,5},{5,4},{6,7},{7,6},{8,9},{9,8},{10,11... | collective-permute-start | bytes 3080 | tf_op jit(solution)/shard_map/ppermute | solution.py:466

commit v7 on v6

--- a/solution.py
+++ b/solution.py
@@ -231,7 +231,7 @@
                 finish(kind, j)
 
         dlogits, loss = depth_head(
-            projected[...], embed[j], gain[c], heads[j], bias[c], token, partial(keep, 0)
+            projected[...], embed[j][...], gain[c], heads[j][...], bias[c], token, partial(keep, 0)
         )
         keep(1, dlogits)
         both.append(loss)
@@ -274,15 +274,10 @@
         ]
         for j in range(2)
     ]
-    staged = []
-    for j in range(2):
-        c = book[1] + j
-        staged.append(
-            pltpu.make_async_copy(looked_hbm.at[c], next_embed.at[j], next_sems.at[0, j])
-        )
-        staged.append(
-            pltpu.make_async_copy(heads_hbm.at[c], next_heads.at[j], next_sems.at[1, j])
-        )
+    staged = [
+        pltpu.make_async_copy(looked_hbm.at[book[1]], next_embed, next_sems.at[0]),
+        pltpu.make_async_copy(heads_hbm.at[book[1]], next_heads, next_sems.at[1]),
+    ]
     for copy in depth_copies + book_copies[0]:
         copy.start()
     total = None
@@ -311,13 +306,44 @@
     def finish(kind, j):
         stores[j][kind].start()
 
+    embed = (embed.at[0], embed.at[1])
+    heads = (heads.at[0], heads.at[1])
     depth_pair(book, projected, embed, heads, gain, bias, target, acts, losses, begin, finish)
     for copy in staged + stores[0] + stores[1]:
         copy.wait()
 
 
-def second_kernel(book, projected, embed, heads, gain, bias, target, acts, losses):
-    depth_pair(book, projected, embed, heads, gain, bias, target, acts, losses)
+def second_kernel(
+    book,
+    projected,
+    first_embed,
+    first_head,
+    gain,
+    bias,
+    target,
+    looked_hbm,
+    heads_hbm,
+    acts,
+    losses,
+    last_embed,
+    last_head,
+    sems,
+):
+    copies = [
+        pltpu.make_async_copy(looked_hbm.at[book[0] + 1], last_embed, sems.at[0]),
+        pltpu.make_async_copy(heads_hbm.at[book[0] + 1], last_head, sems.at[1]),
+    ]
+    for copy in copies:
+        copy.start()
+
+    def begin(j):
+        if j:
+            for copy in copies:
+                copy.wait()
+
+    embed = (first_embed, last_embed)
+    heads = (first_head, last_head)
+    depth_pair(book, projected, embed, heads, gain, bias, target, acts, losses, begin)
 
 
 DEPTH_COST = pl.CostEstimate(
@@ -335,8 +361,8 @@
             jax.ShapeDtypeStruct((FRAMES, DEPTH_DIM), jnp.float32),
             pltpu.HBM(ACTS, jnp.bfloat16),
             jax.ShapeDtypeStruct((FRAMES, 2), jnp.float32),
-            pltpu.VMEM((2, FRAMES, DEPTH_DIM), jnp.bfloat16),
-            pltpu.VMEM((2, DEPTH_DIM, VOCAB), jnp.bfloat16),
+            pltpu.VMEM((FRAMES, DEPTH_DIM), jnp.bfloat16),
+            pltpu.VMEM((DEPTH_DIM, VOCAB), jnp.bfloat16),
         ),
         in_specs=[SMEM] + [VMEM] * 4 + [HBM] * 3,
         out_specs=(VMEM, HBM, VMEM, VMEM, VMEM),
@@ -347,7 +373,7 @@
             pltpu.VMEM((2, DEPTH_DIM, VOCAB), jnp.bfloat16),
             pltpu.SemaphoreType.DMA((SEQ,)),
             pltpu.SemaphoreType.DMA((2, 2)),
-            pltpu.SemaphoreType.DMA((2, 2)),
+            pltpu.SemaphoreType.DMA((2,)),
             pltpu.SemaphoreType.DMA((2, 2)),
         ],
         compiler_params=pltpu.CompilerParams(vmem_limit_bytes=DEPTH_GRANT),
@@ -355,18 +381,23 @@
     )(books, context, *small, depth_in, looked, heads)
 
 
-def depth_second(book, projected, embed, heads, small):
+def depth_second(book, projected, embed, head, small, looked, heads):
     return pl.pallas_call(
         second_kernel,
         out_shape=(
             jax.ShapeDtypeStruct(ACTS, jnp.bfloat16),
             jax.ShapeDtypeStruct((FRAMES, 2), jnp.float32),
         ),
-        in_specs=[SMEM] + [VMEM] * 6,
+        in_specs=[SMEM] + [VMEM] * 6 + [HBM] * 2,
         out_specs=(VMEM, VMEM),
+        scratch_shapes=[
+            pltpu.VMEM((FRAMES, DEPTH_DIM), jnp.bfloat16),
+            pltpu.VMEM((DEPTH_DIM, VOCAB), jnp.bfloat16),
+            pltpu.SemaphoreType.DMA((2,)),
+        ],
         compiler_params=pltpu.CompilerParams(vmem_limit_bytes=DEPTH_GRANT),
         cost_estimate=DEPTH_COST,
-    )(book.reshape(1), projected, embed, heads, *small)
+    )(book.reshape(1), projected, embed, head, *small, looked, heads)
 
 
 def outer_kernel(mine, theirs, out_hbm, out, sems):
@@ -511,11 +542,12 @@
     mine = 2 * core
     other = 2 - mine
     looked = lookup(targets, code_embed)
+    in_hbm = [pltpu.with_memory_space_constraint(a, pltpu.HBM) for a in (depth_in, looked, heads)]
     projected, acts_other, losses_other, *staged = depth_first(
-        jnp.stack([other, mine]), context, small, depth_in, pltpu.with_memory_space_constraint(looked, pltpu.HBM), heads
+        jnp.stack([other, mine]), context, small, *in_hbm
     )
     came = swap_wide(acts_other, 1)
-    acts_mine, losses_mine = depth_second(mine, projected, *staged, small)
+    acts_mine, losses_mine = depth_second(mine, projected, *staged, small, *in_hbm[1:])
     shares = lax.all_to_all(outer(acts_mine, came), ("seq", "wide"), 0, 0, tiled=True)
     grad_scale = (VOCAB / (SEQ * WIDE * FRAMES)) ** 0.5
     head_grads = total(shares, grad_scale)

time: 167 us -> 167 us (level)
  transfers between devices with their start and end apart: 14 -> 14, of which waited for: 8 -> 8; matrix products, arithmetic and copies ran while one was open for 14% -> 14% of each run, Pallas kernels for 9% -> 10%
where the time goes in v7:
time: 167 us; the launch traced here: 166 us
  waiting for transfers between devices  70.6 us (42%)
  starting transfers between devices  36.7 us (22%)
  Pallas kernels  33.1 us (20%)
  local copies, waits for them, and re-layouts  13.8 us (8%)
  matrix products  7.74 us (5%)
  other arithmetic  3.28 us (2%)
    ppermute x11, waiting for transfers between devices, swap_wide(): return lax.ppermute(array, 'wide', [(i, i ^ stride) for i in range(WIDE)])  38.1 us
    all_to_all x1, waiting for transfers between devices, shards(): qkv = lax.all_to_all(packed, 'seq', 0, 0, tiled=True)  26.2 us
    ppermute x11, starting transfers between devices, swap_wide(): return lax.ppermute(array, 'wide', [(i, i ^ stride) for i in range(WIDE)])  12.5 us
    unnamed x18, local copies, waits for them, and re-layouts  12.1 us
    all_to_all x1, starting transfers between devices, shards(): context = lax.all_to_all(context, 'seq', 0, 0, tiled=True)  9.4 us
    all_to_all x1, starting transfers between devices, shards(): qkv = lax.all_to_all(packed, 'seq', 0, 0, tiled=True)  8.15 us
    pallas_call x1, Pallas kernels, depth_first(): pl.pallas_call(first_kernel, out_shape=(jax.ShapeDtypeStruct((FRAMES, DEP...  7.09 us
    all_to_all x1, starting transfers between devices, shards(): lax.all_to_all(outer(acts_mine, came), ('seq', 'wide'), 0, 0, tiled=True)  6.64 us
  transfers between devices with their start and end apart: 14, of which 8 were waited for; matrix products, arithmetic and copies ran while one was open for 14% of the time, Pallas kernels for 10%

profile of v7, /device:TPU:2, one launch (start us, length us, event | category | flops | bytes accessed | tf_op | source)
XLA Modules:
  0.0 166.3 jit_solution(7738798989152070401)
XLA Ops:
  0.6 3.6 %shard_map.112 = bf16[8,256,768]{2,1,0:T(8,128)(2,1)} custom-call(bf16[1,256,2048]{2,1,0:T(8,128)(2,1)} %queries.1, bf16[1,256,2048]{2,1,0:T(8,128)(2,1)} %key_vectors.1, bf16[1,256,2048]{2,1,0:T(8,128)(2,1)} %values.1), custom_call_target="tpu_custom_call" | custom-call | bytes 6291456 | tf_op jit(solution)/shard_map/pallas_call | solution.py:141
  4.3 8.2 %all-to-all-start = ((bf16[8,256,768]{2,1,0:T(8,128)(2,1)}), bf16[8,256,768]{2,1,0:T(8,128)(2,1)S(1)}, u32[]{:S(2)}, u32[]{:S(2)}) async-start(bf16[8,256,768]{2,1,0:T(8,128)(2,1)} %shard_map.112), calls=%async_computation | async-start | bytes 6291456 | tf_op jit(solution)/shard_map/all_to_all | solution.py:532
  12.7 3.3 %collective-permute-start = (s32[1,2,2,2,64]{4,3,2,1,0:T(2,128)S(1)}, s32[1,2,2,2,64]{4,3,2,1,0:T(2,128)S(1)}, u32[]{:S(2)}, u32[]{:S(2)}) collective-permute-start(s32[1,2,2,2,64]{4,3,2,1,0:T(2,128)S(1)} %select_n.182), channel_id=1, source_target_pairs={{0,8},{1,9},{2,10},{3,11},{4,12},{5,13},{6,14},{7,15},{8,0},{9,1},... | collective-permute-start | bytes 6152 | tf_op jit(solution)/shard_map/ppermute | solution.py:497
  16.2 1.7 %collective-permute-done = s32[1,2,2,2,64]{4,3,2,1,0:T(2,128)S(1)} collective-permute-done((s32[1,2,2,2,64]{4,3,2,1,0:T(2,128)S(1)}, s32[1,2,2,2,64]{4,3,2,1,0:T(2,128)S(1)}, u32[]{:S(2)}, u32[]{:S(2)}) %collective-permute-start) | collective-permute-done | bytes 2080 | tf_op jit(solution)/shard_map/ppermute | solution.py:497
  17.9 1.7 collective-permute-start.1
  19.5 9.5 %copy.75 = bf16[1024,4,1024]{2,0,1:T(8,128)(2,1)} copy(bf16[1024,4,1024]{2,1,0:T(4,128)(2,1)} %param.16) | data formatting | bytes 16777216 | tf_op args[7]
  29.1 26.2 %all-to-all-done.qkv = bf16[8,256,768]{2,1,0:T(8,128)(2,1)S(1)} async-done(((bf16[8,256,768]{2,1,0:T(8,128)(2,1)}), bf16[8,256,768]{2,1,0:T(8,128)(2,1)S(1)}, u32[]{:S(2)}, u32[]{:S(2)}) %all-to-all-start) | async-done | bytes 3145760 | tf_op jit(solution)/shard_map/all_to_all | solution.py:532
  55.3 1.1 collective-permute-start.2
  56.4 6.5 %shard_map.113 = bf16[8,256,256]{2,1,0:T(8,128)(2,1)} custom-call(bf16[8,256,768]{2,1,0:T(8,128)(2,1)S(1)} %all-to-all-done.qkv), custom_call_target="tpu_custom_call" | custom-call | flops 2415919104 | bytes 4194304 | tf_op jit(solution)/shard_map/pallas_call | solution.py:89
  63.0 9.4 %all-to-all-start.1 = ((bf16[8,256,256]{2,1,0:T(8,128)(2,1)}), bf16[8,256,256]{2,1,0:T(8,128)(2,1)S(1)}, u32[]{:S(2)}, u32[]{:S(2)}) async-start(bf16[8,256,256]{2,1,0:T(8,128)(2,1)} %shard_map.113), calls=%async_computation.1 | async-start | bytes 2097152 | tf_op jit(solution)/shard_map/all_to_all | solution.py:538
  72.8 1.0 collective-permute-done.3
  73.8 0.8 reshape.125.target
  74.6 6.0 %shard_map.114.looked_hbm = bf16[4,256,1024]{2,1,0:T(8,128)(2,1)} custom-call(s32[256,4]{1,0:T(8,128)} %reshape.125.target, bf16[3,1024,1024]{2,1,0:T(8,128)(2,1)} %table_hbm.1), custom_call_target="tpu_custom_call" | custom-call | flops 1610612736 | bytes 10485760 | tf_op jit(solution)/shard_map/pallas_call | solution.py:183
  80.6 6.3 %all-to-all-done.1.ctx = bf16[8,256,256]{2,1,0:T(8,128)(2,1)S(1)} async-done(((bf16[8,256,256]{2,1,0:T(8,128)(2,1)}), bf16[8,256,256]{2,1,0:T(8,128)(2,1)S(1)}, u32[]{:S(2)}, u32[]{:S(2)}) %all-to-all-start.1) | async-done | bytes 1048608 | tf_op jit(solution)/shard_map/all_to_all | solution.py:538
  86.9 7.1 %shard_map.115 = (f32[256,1024]{1,0:T(8,128)S(1)}, bf16[2,2,256,1024]{3,2,1,0:T(8,128)(2,1)}, f32[256,2]{1,0:T(8,128)S(1)}, bf16[256,1024]{1,0:T(8,128)(2,1)S(1)}, bf16[1024,1024]{1,0:T(8,128)(2,1)S(1)}) custom-call(s32[2]{0:T(128)S(1)} %pad_add_fusion.4.book, bf16[8,256,256]{2,1,0:T(8,128)(2,1)S(1)} %all-to-all-done.1.ctx, ...), custom_call_target="tpu_custom_call" | custom-call | flops 1073741824 | bytes 8388608 | tf_op jit(solution)/shard_map/pallas_call | solution.py:358
  94.1 3.6 %shard_map.116 = (bf16[2,2,256,1024]{3,2,1,0:T(8,128)(2,1)S(1)}, f32[256,2]{1,0:T(8,128)S(1)}) custom-call(s32[1]{0:T(128)} %bitcast.book, f32[256,1024]{1,0:T(8,128)S(1)} %get-tuple-element.26.projected, bf16[256,1024]{1,0:T(8,128)(2,1)S(1)} %get-tuple-element.27.first_embed, bf16[1024,1024]{1,0:T(8,128)(2,1)S(1)} %get-tuple-element.28.first_head, ...), custom_call_target="tpu_custom_call" | custom-call | flops 1073741824 | bytes 8388608 | tf_op jit(solution)/shard_map/pallas_call | solution.py:385
  97.7 0.6 copy-done.1
  98.4 3.3 %shard_map.117 = bf16[128,16,1024]{2,1,0:T(8,128)(2,1)} custom-call(bf16[2,2,256,1024]{3,2,1,0:T(8,128)(2,1)S(1)} %get-tuple-element.31.mine, bf16[2,2,256,1024]{3,2,1,0:T(8,128)(2,1)S(1)} %collective-permute-done.10.theirs), custom_call_target="tpu_custom_call" | custom-call | flops 2147483648 | bytes 8388608 | tf_op jit(solution)/shard_map/pallas_call | solution.py:430
  101.7 6.6 %all-to-all-start.2 = ((bf16[128,16,1024]{2,1,0:T(8,128)(2,1)}), bf16[128,16,1024]{2,1,0:T(8,128)(2,1)}, u32[]{:S(2)}, u32[]{:S(2)}) async-start(bf16[128,16,1024]{2,1,0:T(8,128)(2,1)} %shard_map.117), calls=%async_computation.2 | async-start | bytes 8388608 | tf_op jit(solution)/shard_map/all_to_all | solution.py:551
  108.6 1.5 select_bitcast_fusion.1
  110.5 5.5 %multiply_reduce_fusion.1 = (f32[4,256]{1,0:T(4,128)S(1)}, f32[4,256]{1,0:T(4,128)S(1)}, f32[4,256,1024]{2,1,0:T(8,128)S(1)}) fusion(bf16[4,256,1024]{2,1,0:T(8,128)(2,1)S(1)} %copy-done.3, f32[256,1024]{1,0:T(8,128)S(1)} %get-tuple-element.26.projected, f32[4,1024]{1,0:T(4,128)S(1)} %copy-done.5, bf16[4,1024,1024]{2,1,0:T(8,128)(2,1)} %bitcast.34, ...), kind=kOutput, calls=%fused_computation.4 | convolution fusion | flops 2155870208 | bytes 17850368 | tf_op jit(solution)/shard_map/cnv,cev->cne/dot_general | solution.py:564
  116.0 1.3 fusion
  117.3 0.8 copy-done.4
  118.2 2.3 %convolution_convert_fusion = bf16[256,2048]{1,0:T(8,128)(2,1)} fusion(bf16[2048,1024]{1,0:T(8,128)(2,1)S(1)} %copy-done.4, bf16[256,1024]{1,0:T(8,128)(2,1)S(1)} %fusion), kind=kOutput, calls=%fused_computation.6 | convolution fusion | flops 1074266112 | bytes 5767168 | tf_op jit(solution)/shard_map/dot_general | solution.py:567
  120.8 2.8 %collective-permute-start.6 = (f32[4,64]{1,0:T(4,128)S(1)}, f32[4,64]{1,0:T(4,128)S(1)}, u32[]{:S(2)}, u32[]{:S(2)}) collective-permute-start(f32[4,64]{1,0:T(4,128)S(1)} %get-tuple-element.64), channel_id=1, source_target_pairs={{0,12},{1,13},{2,14},{3,15},{4,8},{5,9},{6,10},{7,11},{8,4},{9,5},... | collective-permute-start | bytes 3080 | tf_op jit(solution)/shard_map/ppermute | solution.py:497
  123.6 0.8 collective-permute-start.5
  125.0 33.4 %collective-permute-done.6 = f32[4,64]{1,0:T(4,128)S(1)} collective-permute-done((f32[4,64]{1,0:T(4,128)S(1)}, f32[4,64]{1,0:T(4,128)S(1)}, u32[]{:S(2)}, u32[]{:S(2)}) %collective-permute-start.6) | collective-permute-done | bytes 1056 | tf_op jit(solution)/shard_map/ppermute | solution.py:497
  158.5 1.8 %collective-permute-start.8 = (f32[4,64]{1,0:T(4,128)S(1)}, f32[4,64]{1,0:T(4,128)S(1)}, u32[]{:S(2)}, u32[]{:S(2)}) collective-permute-start(f32[4,64]{1,0:T(4,128)S(1)} %bitcast.42), channel_id=1, source_target_pairs={{0,2},{1,3},{2,0},{3,1},{4,6},{5,7},{6,4},{7,5},{8,10},{9,11},{10,... | collective-permute-start | bytes 3080 | tf_op jit(solution)/shard_map/ppermute | solution.py:497
  160.4 1.1 collective-permute-done.9
  161.5 0.7 collective-permute-done.8
  162.4 0.7 copy.70
  163.1 3.0 %shard_map.118 = f32[8,4,1024]{2,1,0:T(4,128)} custom-call(bf16[64,2,16,1024]{3,2,1,0:T(8,128)(2,1)} %bitcast.18.shares_hbm), custom_call_target="tpu_custom_call" | custom-call | flops 2097152 | bytes 4194304 | tf_op jit(solution)/shard_map/pallas_call | solution.py:472
  (60 shorter events, 3.0 us)
Async XLA Ops:
  4.3 8.2 %copy-start.6 = (s32[16,16,4]{1,2,0:T(4,128)S(1)}, s32[16,16,4]{1,2,0:T(4,128)}, u32[]{:S(2)}) copy-start(s32[16,16,4]{1,2,0:T(4,128)} %param.12) | copy-start | bytes 12292
  4.3 51.0 %all-to-all-start = ((bf16[8,256,768]{2,1,0:T(8,128)(2,1)}), bf16[8,256,768]{2,1,0:T(8,128)(2,1)S(1)}, u32[]{:S(2)}, u32[]{:S(2)}) async-start(bf16[8,256,768]{2,1,0:T(8,128)(2,1)} %shard_map.112), calls=%async_computation | async-start | bytes 6291456 | tf_op jit(solution)/shard_map/all_to_all | solution.py:532
  12.7 5.2 %collective-permute-start = (s32[1,2,2,2,64]{4,3,2,1,0:T(2,128)S(1)}, s32[1,2,2,2,64]{4,3,2,1,0:T(2,128)S(1)}, u32[]{:S(2)}, u32[]{:S(2)}) collective-permute-start(s32[1,2,2,2,64]{4,3,2,1,0:T(2,128)S(1)} %select_n.182), channel_id=1, source_target_pairs={{0,8},{1,9},{2,10},{3,11},{4,12},{5,13},{6,14},{7,15},{8,0},{9,1},... | collective-permute-start | bytes 6152 | tf_op jit(solution)/shard_map/ppermute | solution.py:497
  17.9 11.2 %collective-permute-start.1 = (s32[2,1,2,2,64]{4,3,2,1,0:T(2,128)S(1)}, s32[2,1,2,2,64]{4,3,2,1,0:T(2,128)S(1)}, u32[]{:S(2)}, u32[]{:S(2)}) collective-permute-start(s32[2,1,2,2,64]{4,3,2,1,0:T(2,128)S(1)} %broadcast_select_fusion.9), channel_id=1, source_target_pairs={{0,4},{1,5},{2,6},{3,7},{4,0},{5,1},{6,2},{7,3},{8,12},{9,13},{10,... | collective-permute-start | bytes 6152 | tf_op jit(solution)/shard_map/ppermute | solution.py:497
  55.3 17.5 %copy-start.5 = (f32[4,1024]{1,0:T(4,128)S(1)}, f32[4,1024]{1,0:T(4,128)}, u32[]{:S(2)}) copy-start(f32[4,1024]{1,0:T(4,128)} %param.15) | copy-start | bytes 49156
  55.3 17.5 %copy-start.7 = (f32[4,1024]{1,0:T(4,128)S(1)}, f32[4,1024]{1,0:T(4,128)}, u32[]{:S(2)}) copy-start(f32[4,1024]{1,0:T(4,128)} %param.17) | copy-start | bytes 49156
  55.3 7.6 %collective-permute-start.2 = (s32[2,2,1,2,64]{4,3,2,1,0:T(2,128)S(1)}, s32[2,2,1,2,64]{4,3,2,1,0:T(2,128)S(1)}, u32[]{:S(2)}, u32[]{:S(2)}) collective-permute-start(s32[2,2,1,2,64]{4,3,2,1,0:T(2,128)S(1)} %broadcast_select_fusion.13), channel_id=1, source_target_pairs={{0,2},{1,3},{2,0},{3,1},{4,6},{5,7},{6,4},{7,5},{8,10},{9,11},{10,... | collective-permute-start | bytes 6152 | tf_op jit(solution)/shard_map/ppermute | solution.py:497
  63.0 23.9 %all-to-all-start.1 = ((bf16[8,256,256]{2,1,0:T(8,128)(2,1)}), bf16[8,256,256]{2,1,0:T(8,128)(2,1)S(1)}, u32[]{:S(2)}, u32[]{:S(2)}) async-start(bf16[8,256,256]{2,1,0:T(8,128)(2,1)} %shard_map.113), calls=%async_computation.1 | async-start | bytes 2097152 | tf_op jit(solution)/shard_map/all_to_all | solution.py:538
  72.4 1.4 collective-permute-start.3
  74.6 12.3 %copy-start = (s32[256,4]{1,0:T(8,128)S(1)}, s32[256,4]{1,0:T(8,128)}, u32[]{:S(2)}) copy-start(s32[256,4]{1,0:T(8,128)} %reshape.125.target) | copy-start | bytes 12292
  94.0 4.5 %collective-permute-start.10 = (bf16[2,2,256,1024]{3,2,1,0:T(8,128)(2,1)}, bf16[2,2,256,1024]{3,2,1,0:T(8,128)(2,1)S(1)}, u32[]{:S(2)}, u32[]{:S(2)}) collective-permute-start(bf16[2,2,256,1024]{3,2,1,0:T(8,128)(2,1)} %get-tuple-element.32), channel_id=1, source_target_pairs={{0,1},{1,0},{2,3},{3,2},{4,5},{5,4},{6,7},{7,6},{8,9},{9,8},{10,11... | collective-permute-start | bytes 6291464 | tf_op jit(solution)/shard_map/ppermute | solution.py:497
  97.7 0.7 copy-start.1
  101.7 6.8 %copy-start.2 = (f32[256,2]{1,0:T(8,128)S(1)}, f32[256,2]{1,0:T(8,128)}, u32[]{:S(2)}) copy-start(f32[256,2]{1,0:T(8,128)} %copy-done.1) | copy-start | bytes 6148
  101.7 61.4 %all-to-all-start.2 = ((bf16[128,16,1024]{2,1,0:T(8,128)(2,1)}), bf16[128,16,1024]{2,1,0:T(8,128)(2,1)}, u32[]{:S(2)}, u32[]{:S(2)}) async-start(bf16[128,16,1024]{2,1,0:T(8,128)(2,1)} %shard_map.117), calls=%async_computation.2 | async-start | bytes 8388608 | tf_op jit(solution)/shard_map/all_to_all | solution.py:551
  108.6 1.9 %copy-start.3 = (bf16[4,256,1024]{2,1,0:T(8,128)(2,1)S(1)}, bf16[4,256,1024]{2,1,0:T(8,128)(2,1)}, u32[]{:S(2)}) copy-start(bf16[4,256,1024]{2,1,0:T(8,128)(2,1)} %shard_map.114.looked_hbm) | copy-start | bytes 6291460
  116.0 2.2 %copy-start.4 = (bf16[2048,1024]{1,0:T(8,128)(2,1)S(1)}, bf16[2048,1024]{1,0:T(8,128)(2,1)}, u32[]{:S(2)}) copy-start(bf16[2048,1024]{1,0:T(8,128)(2,1)} %depth_hbm.1) | copy-start | bytes 12582916
  120.8 37.6 %collective-permute-start.6 = (f32[4,64]{1,0:T(4,128)S(1)}, f32[4,64]{1,0:T(4,128)S(1)}, u32[]{:S(2)}, u32[]{:S(2)}) collective-permute-start(f32[4,64]{1,0:T(4,128)S(1)} %get-tuple-element.64), channel_id=1, source_target_pairs={{0,12},{1,13},{2,14},{3,15},{4,8},{5,9},{6,10},{7,11},{8,4},{9,5},... | collective-permute-start | bytes 3080 | tf_op jit(solution)/shard_map/ppermute | solution.py:497
  123.6 34.8 %collective-permute-start.5 = (f32[4,64]{1,0:T(4,128)S(1)}, f32[4,64]{1,0:T(4,128)S(1)}, u32[]{:S(2)}, u32[]{:S(2)}) collective-permute-start(f32[4,64]{1,0:T(4,128)S(1)} %get-tuple-element.65), channel_id=1, source_target_pairs={{0,8},{1,9},{2,10},{3,11},{4,12},{5,13},{6,14},{7,15},{8,0},{9,1},... | collective-permute-start | bytes 3080 | tf_op jit(solution)/shard_map/ppermute | solution.py:497
  124.4 34.0 %collective-permute-start.4 = (f32[4,64]{1,0:T(4,128)S(1)}, f32[4,64]{1,0:T(4,128)S(1)}, u32[]{:S(2)}, u32[]{:S(2)}) collective-permute-start(f32[4,64]{1,0:T(4,128)S(1)} %get-tuple-element.66), channel_id=1, source_target_pairs={{0,4},{1,5},{2,6},{3,7},{4,0},{5,1},{6,2},{7,3},{8,12},{9,13},{10,... | collective-permute-start | bytes 3080 | tf_op jit(solution)/shard_map/ppermute | solution.py:497
  158.4 3.1 %collective-permute-start.9 = (f32[4,64]{1,0:T(4,128)S(1)}, f32[4,64]{1,0:T(4,128)S(1)}, u32[]{:S(2)}, u32[]{:S(2)}) collective-permute-start(f32[4,64]{1,0:T(4,128)S(1)} %bitcast.45), channel_id=1, source_target_pairs={{0,3},{1,2},{2,1},{3,0},{4,7},{5,6},{6,5},{7,4},{8,11},{9,10},{10,... | collective-permute-start | bytes 3080 | tf_op jit(solution)/shard_map/ppermute | solution.py:497
  158.5 3.7 %collective-permute-start.8 = (f32[4,64]{1,0:T(4,128)S(1)}, f32[4,64]{1,0:T(4,128)S(1)}, u32[]{:S(2)}, u32[]{:S(2)}) collective-permute-start(f32[4,64]{1,0:T(4,128)S(1)} %bitcast.42), channel_id=1, source_target_pairs={{0,2},{1,3},{2,0},{3,1},{4,6},{5,7},{6,4},{7,5},{8,10},{9,11},{10,... | collective-permute-start | bytes 3080 | tf_op jit(solution)/shard_map/ppermute | solution.py:497
  160.4 1.8 %collective-permute-start.7 = (f32[4,64]{1,0:T(4,128)S(1)}, f32[4,64]{1,0:T(4,128)S(1)}, u32[]{:S(2)}, u32[]{:S(2)}) collective-permute-start(f32[4,64]{1,0:T(4,128)S(1)} %bitcast.39), channel_id=1, source_target_pairs={{0,1},{1,0},{2,3},{3,2},{4,5},{5,4},{6,7},{7,6},{8,9},{9,8},{10,11... | collective-permute-start | bytes 3080 | tf_op jit(solution)/shard_map/ppermute | solution.py:497

commit v8 on v7

--- a/solution.py
+++ b/solution.py
@@ -105,7 +105,7 @@
 
 
 def pack_kernel(queries, key_vectors, values, out, held, in_sems, out_sems):
-    rows = FRAMES // 4
+    rows = FRAMES // 2
     sources = (queries, key_vectors, values)
     loads = [
         [
@@ -116,13 +116,13 @@
             )
             for kind, ref in enumerate(sources)
         ]
-        for i in range(4)
+        for i in range(2)
     ]
     for group in loads:
         for copy in group:
             copy.start()
     stores = []
-    for i in range(4):
+    for i in range(2):
         for kind in range(3):
             loads[i][kind].wait()
             for part in range(SEQ):
@@ -145,8 +145,8 @@
         out_specs=HBM,
         scratch_shapes=[
             pltpu.VMEM((3, FRAMES, FEATURES), jnp.bfloat16),
-            pltpu.SemaphoreType.DMA((4, 3)),
-            pltpu.SemaphoreType.DMA((4, 3, SEQ)),
+            pltpu.SemaphoreType.DMA((2, 3)),
+            pltpu.SemaphoreType.DMA((2, 3, SEQ)),
         ],
         compiler_params=pltpu.CompilerParams(vmem_limit_bytes=GRANT),
         cost_estimate=pl.CostEstimate(flops=0, bytes_accessed=6 * 2**20, transcendentals=0),

time: 167 us -> 166 us (level)
  no operation moved by 1% of the time
where the time goes in v8:
time: 166 us
  waiting for transfers between devices  70.6 us (43%)
  starting transfers between devices  36.7 us (22%)
  Pallas kernels  32.7 us (20%)
  local copies, waits for them, and re-layouts  13.8 us (8%)
  matrix products  7.74 us (5%)
  other arithmetic  3.28 us (2%)
    ppermute x11, waiting for transfers between devices, swap_wide(): return lax.ppermute(array, 'wide', [(i, i ^ stride) for i in range(WIDE)])  38.1 us
    all_to_all x1, waiting for transfers between devices, shards(): qkv = lax.all_to_all(packed, 'seq', 0, 0, tiled=True)  26.2 us
    ppermute x11, starting transfers between devices, swap_wide(): return lax.ppermute(array, 'wide', [(i, i ^ stride) for i in range(WIDE)])  12.5 us
    unnamed x18, local copies, waits for them, and re-layouts  12.1 us
    all_to_all x1, starting transfers between devices, shards(): context = lax.all_to_all(context, 'seq', 0, 0, tiled=True)  9.4 us
    all_to_all x1, starting transfers between devices, shards(): qkv = lax.all_to_all(packed, 'seq', 0, 0, tiled=True)  8.15 us
    pallas_call x1, Pallas kernels, depth_first(): pl.pallas_call(first_kernel, out_shape=(jax.ShapeDtypeStruct((FRAMES, DEP...  7.09 us
    all_to_all x1, starting transfers between devices, shards(): lax.all_to_all(outer(acts_mine, came), ('seq', 'wide'), 0, 0, tiled=True)  6.64 us
  transfers between devices with their start and end apart: 14, of which 8 were waited for; matrix products, arithmetic and copies ran while one was open for 14% of the time, Pallas kernels for 10%

profile of v8, /device:TPU:2, one launch (start us, length us, event | category | flops | bytes accessed | tf_op | source)
XLA Modules:
  0.0 166.0 jit_solution(15770254325817637908)
XLA Ops:
  0.6 3.3 %shard_map.112 = bf16[8,256,768]{2,1,0:T(8,128)(2,1)} custom-call(bf16[1,256,2048]{2,1,0:T(8,128)(2,1)} %queries.1, bf16[1,256,2048]{2,1,0:T(8,128)(2,1)} %key_vectors.1, bf16[1,256,2048]{2,1,0:T(8,128)(2,1)} %values.1), custom_call_target="tpu_custom_call" | custom-call | bytes 6291456 | tf_op jit(solution)/shard_map/pallas_call | solution.py:141
  3.9 8.2 %all-to-all-start = ((bf16[8,256,768]{2,1,0:T(8,128)(2,1)}), bf16[8,256,768]{2,1,0:T(8,128)(2,1)S(1)}, u32[]{:S(2)}, u32[]{:S(2)}) async-start(bf16[8,256,768]{2,1,0:T(8,128)(2,1)} %shard_map.112), calls=%async_computation | async-start | bytes 6291456 | tf_op jit(solution)/shard_map/all_to_all | solution.py:532
  12.3 3.3 %collective-permute-start = (s32[1,2,2,2,64]{4,3,2,1,0:T(2,128)S(1)}, s32[1,2,2,2,64]{4,3,2,1,0:T(2,128)S(1)}, u32[]{:S(2)}, u32[]{:S(2)}) collective-permute-start(s32[1,2,2,2,64]{4,3,2,1,0:T(2,128)S(1)} %select_n.182), channel_id=1, source_target_pairs={{0,8},{1,9},{2,10},{3,11},{4,12},{5,13},{6,14},{7,15},{8,0},{9,1},... | collective-permute-start | bytes 6152 | tf_op jit(solution)/shard_map/ppermute | solution.py:497
  15.8 1.7 %collective-permute-done = s32[1,2,2,2,64]{4,3,2,1,0:T(2,128)S(1)} collective-permute-done((s32[1,2,2,2,64]{4,3,2,1,0:T(2,128)S(1)}, s32[1,2,2,2,64]{4,3,2,1,0:T(2,128)S(1)}, u32[]{:S(2)}, u32[]{:S(2)}) %collective-permute-start) | collective-permute-done | bytes 2080 | tf_op jit(solution)/shard_map/ppermute | solution.py:497
  17.5 1.7 collective-permute-start.1
  19.2 9.5 %copy.75 = bf16[1024,4,1024]{2,0,1:T(8,128)(2,1)} copy(bf16[1024,4,1024]{2,1,0:T(4,128)(2,1)} %param.16) | data formatting | bytes 16777216 | tf_op args[7]
  28.7 26.2 %all-to-all-done.qkv = bf16[8,256,768]{2,1,0:T(8,128)(2,1)S(1)} async-done(((bf16[8,256,768]{2,1,0:T(8,128)(2,1)}), bf16[8,256,768]{2,1,0:T(8,128)(2,1)S(1)}, u32[]{:S(2)}, u32[]{:S(2)}) %all-to-all-start) | async-done | bytes 3145760 | tf_op jit(solution)/shard_map/all_to_all | solution.py:532
  54.9 1.1 collective-permute-start.2
  56.0 6.5 %shard_map.113 = bf16[8,256,256]{2,1,0:T(8,128)(2,1)} custom-call(bf16[8,256,768]{2,1,0:T(8,128)(2,1)S(1)} %all-to-all-done.qkv), custom_call_target="tpu_custom_call" | custom-call | flops 2415919104 | bytes 4194304 | tf_op jit(solution)/shard_map/pallas_call | solution.py:89
  62.6 9.4 %all-to-all-start.1 = ((bf16[8,256,256]{2,1,0:T(8,128)(2,1)}), bf16[8,256,256]{2,1,0:T(8,128)(2,1)S(1)}, u32[]{:S(2)}, u32[]{:S(2)}) async-start(bf16[8,256,256]{2,1,0:T(8,128)(2,1)} %shard_map.113), calls=%async_computation.1 | async-start | bytes 2097152 | tf_op jit(solution)/shard_map/all_to_all | solution.py:538
  72.4 1.0 collective-permute-done.3
  73.5 0.8 reshape.125.target
  74.3 6.0 %shard_map.114.looked_hbm = bf16[4,256,1024]{2,1,0:T(8,128)(2,1)} custom-call(s32[256,4]{1,0:T(8,128)} %reshape.125.target, bf16[3,1024,1024]{2,1,0:T(8,128)(2,1)} %table_hbm.1), custom_call_target="tpu_custom_call" | custom-call | flops 1610612736 | bytes 10485760 | tf_op jit(solution)/shard_map/pallas_call | solution.py:183
  80.2 6.3 %all-to-all-done.1.ctx = bf16[8,256,256]{2,1,0:T(8,128)(2,1)S(1)} async-done(((bf16[8,256,256]{2,1,0:T(8,128)(2,1)}), bf16[8,256,256]{2,1,0:T(8,128)(2,1)S(1)}, u32[]{:S(2)}, u32[]{:S(2)}) %all-to-all-start.1) | async-done | bytes 1048608 | tf_op jit(solution)/shard_map/all_to_all | solution.py:538
  86.5 7.1 %shard_map.115 = (f32[256,1024]{1,0:T(8,128)S(1)}, bf16[2,2,256,1024]{3,2,1,0:T(8,128)(2,1)}, f32[256,2]{1,0:T(8,128)S(1)}, bf16[256,1024]{1,0:T(8,128)(2,1)S(1)}, bf16[1024,1024]{1,0:T(8,128)(2,1)S(1)}) custom-call(s32[2]{0:T(128)S(1)} %pad_add_fusion.4.book, bf16[8,256,256]{2,1,0:T(8,128)(2,1)S(1)} %all-to-all-done.1.ctx, ...), custom_call_target="tpu_custom_call" | custom-call | flops 1073741824 | bytes 8388608 | tf_op jit(solution)/shard_map/pallas_call | solution.py:358
  93.7 3.6 %shard_map.116 = (bf16[2,2,256,1024]{3,2,1,0:T(8,128)(2,1)S(1)}, f32[256,2]{1,0:T(8,128)S(1)}) custom-call(s32[1]{0:T(128)} %bitcast.book, f32[256,1024]{1,0:T(8,128)S(1)} %get-tuple-element.26.projected, bf16[256,1024]{1,0:T(8,128)(2,1)S(1)} %get-tuple-element.27.first_embed, bf16[1024,1024]{1,0:T(8,128)(2,1)S(1)} %get-tuple-element.28.first_head, ...), custom_call_target="tpu_custom_call" | custom-call | flops 1073741824 | bytes 8388608 | tf_op jit(solution)/shard_map/pallas_call | solution.py:385
  97.3 0.6 copy-done.1
  98.1 3.3 %shard_map.117 = bf16[128,16,1024]{2,1,0:T(8,128)(2,1)} custom-call(bf16[2,2,256,1024]{3,2,1,0:T(8,128)(2,1)S(1)} %get-tuple-element.31.mine, bf16[2,2,256,1024]{3,2,1,0:T(8,128)(2,1)S(1)} %collective-permute-done.10.theirs), custom_call_target="tpu_custom_call" | custom-call | flops 2147483648 | bytes 8388608 | tf_op jit(solution)/shard_map/pallas_call | solution.py:430
  101.4 6.6 %all-to-all-start.2 = ((bf16[128,16,1024]{2,1,0:T(8,128)(2,1)}), bf16[128,16,1024]{2,1,0:T(8,128)(2,1)}, u32[]{:S(2)}, u32[]{:S(2)}) async-start(bf16[128,16,1024]{2,1,0:T(8,128)(2,1)} %shard_map.117), calls=%async_computation.2 | async-start | bytes 8388608 | tf_op jit(solution)/shard_map/all_to_all | solution.py:551
  108.2 1.5 select_bitcast_fusion.1
  110.1 5.5 %multiply_reduce_fusion.1 = (f32[4,256]{1,0:T(4,128)S(1)}, f32[4,256]{1,0:T(4,128)S(1)}, f32[4,256,1024]{2,1,0:T(8,128)S(1)}) fusion(bf16[4,256,1024]{2,1,0:T(8,128)(2,1)S(1)} %copy-done.3, f32[256,1024]{1,0:T(8,128)S(1)} %get-tuple-element.26.projected, f32[4,1024]{1,0:T(4,128)S(1)} %copy-done.5, bf16[4,1024,1024]{2,1,0:T(8,128)(2,1)} %bitcast.34, ...), kind=kOutput, calls=%fused_computation.4 | convolution fusion | flops 2155870208 | bytes 17850368 | tf_op jit(solution)/shard_map/cnv,cev->cne/dot_general | solution.py:564
  115.6 1.3 fusion
  117.0 0.8 copy-done.4
  117.8 2.3 %convolution_convert_fusion = bf16[256,2048]{1,0:T(8,128)(2,1)} fusion(bf16[2048,1024]{1,0:T(8,128)(2,1)S(1)} %copy-done.4, bf16[256,1024]{1,0:T(8,128)(2,1)S(1)} %fusion), kind=kOutput, calls=%fused_computation.6 | convolution fusion | flops 1074266112 | bytes 5767168 | tf_op jit(solution)/shard_map/dot_general | solution.py:567
  120.5 2.8 %collective-permute-start.6 = (f32[4,64]{1,0:T(4,128)S(1)}, f32[4,64]{1,0:T(4,128)S(1)}, u32[]{:S(2)}, u32[]{:S(2)}) collective-permute-start(f32[4,64]{1,0:T(4,128)S(1)} %get-tuple-element.64), channel_id=1, source_target_pairs={{0,12},{1,13},{2,14},{3,15},{4,8},{5,9},{6,10},{7,11},{8,4},{9,5},... | collective-permute-start | bytes 3080 | tf_op jit(solution)/shard_map/ppermute | solution.py:497
  123.3 0.8 collective-permute-start.5
  124.6 33.4 %collective-permute-done.6 = f32[4,64]{1,0:T(4,128)S(1)} collective-permute-done((f32[4,64]{1,0:T(4,128)S(1)}, f32[4,64]{1,0:T(4,128)S(1)}, u32[]{:S(2)}, u32[]{:S(2)}) %collective-permute-start.6) | collective-permute-done | bytes 1056 | tf_op jit(solution)/shard_map/ppermute | solution.py:497
  158.2 1.8 %collective-permute-start.8 = (f32[4,64]{1,0:T(4,128)S(1)}, f32[4,64]{1,0:T(4,128)S(1)}, u32[]{:S(2)}, u32[]{:S(2)}) collective-permute-start(f32[4,64]{1,0:T(4,128)S(1)} %bitcast.42), channel_id=1, source_target_pairs={{0,2},{1,3},{2,0},{3,1},{4,6},{5,7},{6,4},{7,5},{8,10},{9,11},{10,... | collective-permute-start | bytes 3080 | tf_op jit(solution)/shard_map/ppermute | solution.py:497
  160.0 1.1 collective-permute-done.9
  161.2 0.7 collective-permute-done.8
  162.1 0.7 copy.70
  162.8 3.0 %shard_map.118 = f32[8,4,1024]{2,1,0:T(4,128)} custom-call(bf16[64,2,16,1024]{3,2,1,0:T(8,128)(2,1)} %bitcast.18.shares_hbm), custom_call_target="tpu_custom_call" | custom-call | flops 2097152 | bytes 4194304 | tf_op jit(solution)/shard_map/pallas_call | solution.py:472
  (60 shorter events, 3.0 us)
Async XLA Ops:
  3.9 8.2 %copy-start.6 = (s32[16,16,4]{1,2,0:T(4,128)S(1)}, s32[16,16,4]{1,2,0:T(4,128)}, u32[]{:S(2)}) copy-start(s32[16,16,4]{1,2,0:T(4,128)} %param.12) | copy-start | bytes 12292
  3.9 51.0 %all-to-all-start = ((bf16[8,256,768]{2,1,0:T(8,128)(2,1)}), bf16[8,256,768]{2,1,0:T(8,128)(2,1)S(1)}, u32[]{:S(2)}, u32[]{:S(2)}) async-start(bf16[8,256,768]{2,1,0:T(8,128)(2,1)} %shard_map.112), calls=%async_computation | async-start | bytes 6291456 | tf_op jit(solution)/shard_map/all_to_all | solution.py:532
  12.3 5.2 %collective-permute-start = (s32[1,2,2,2,64]{4,3,2,1,0:T(2,128)S(1)}, s32[1,2,2,2,64]{4,3,2,1,0:T(2,128)S(1)}, u32[]{:S(2)}, u32[]{:S(2)}) collective-permute-start(s32[1,2,2,2,64]{4,3,2,1,0:T(2,128)S(1)} %select_n.182), channel_id=1, source_target_pairs={{0,8},{1,9},{2,10},{3,11},{4,12},{5,13},{6,14},{7,15},{8,0},{9,1},... | collective-permute-start | bytes 6152 | tf_op jit(solution)/shard_map/ppermute | solution.py:497
  17.5 11.2 %collective-permute-start.1 = (s32[2,1,2,2,64]{4,3,2,1,0:T(2,128)S(1)}, s32[2,1,2,2,64]{4,3,2,1,0:T(2,128)S(1)}, u32[]{:S(2)}, u32[]{:S(2)}) collective-permute-start(s32[2,1,2,2,64]{4,3,2,1,0:T(2,128)S(1)} %broadcast_select_fusion.9), channel_id=1, source_target_pairs={{0,4},{1,5},{2,6},{3,7},{4,0},{5,1},{6,2},{7,3},{8,12},{9,13},{10,... | collective-permute-start | bytes 6152 | tf_op jit(solution)/shard_map/ppermute | solution.py:497
  54.9 17.5 %copy-start.5 = (f32[4,1024]{1,0:T(4,128)S(1)}, f32[4,1024]{1,0:T(4,128)}, u32[]{:S(2)}) copy-start(f32[4,1024]{1,0:T(4,128)} %param.15) | copy-start | bytes 49156
  54.9 17.5 %copy-start.7 = (f32[4,1024]{1,0:T(4,128)S(1)}, f32[4,1024]{1,0:T(4,128)}, u32[]{:S(2)}) copy-start(f32[4,1024]{1,0:T(4,128)} %param.17) | copy-start | bytes 49156
  54.9 7.7 %collective-permute-start.2 = (s32[2,2,1,2,64]{4,3,2,1,0:T(2,128)S(1)}, s32[2,2,1,2,64]{4,3,2,1,0:T(2,128)S(1)}, u32[]{:S(2)}, u32[]{:S(2)}) collective-permute-start(s32[2,2,1,2,64]{4,3,2,1,0:T(2,128)S(1)} %broadcast_select_fusion.13), channel_id=1, source_target_pairs={{0,2},{1,3},{2,0},{3,1},{4,6},{5,7},{6,4},{7,5},{8,10},{9,11},{10,... | collective-permute-start | bytes 6152 | tf_op jit(solution)/shard_map/ppermute | solution.py:497
  62.6 23.9 %all-to-all-start.1 = ((bf16[8,256,256]{2,1,0:T(8,128)(2,1)}), bf16[8,256,256]{2,1,0:T(8,128)(2,1)S(1)}, u32[]{:S(2)}, u32[]{:S(2)}) async-start(bf16[8,256,256]{2,1,0:T(8,128)(2,1)} %shard_map.113), calls=%async_computation.1 | async-start | bytes 2097152 | tf_op jit(solution)/shard_map/all_to_all | solution.py:538
  72.0 1.4 collective-permute-start.3
  74.3 12.3 %copy-start = (s32[256,4]{1,0:T(8,128)S(1)}, s32[256,4]{1,0:T(8,128)}, u32[]{:S(2)}) copy-start(s32[256,4]{1,0:T(8,128)} %reshape.125.target) | copy-start | bytes 12292
  93.6 4.5 %collective-permute-start.10 = (bf16[2,2,256,1024]{3,2,1,0:T(8,128)(2,1)}, bf16[2,2,256,1024]{3,2,1,0:T(8,128)(2,1)S(1)}, u32[]{:S(2)}, u32[]{:S(2)}) collective-permute-start(bf16[2,2,256,1024]{3,2,1,0:T(8,128)(2,1)} %get-tuple-element.32), channel_id=1, source_target_pairs={{0,1},{1,0},{2,3},{3,2},{4,5},{5,4},{6,7},{7,6},{8,9},{9,8},{10,11... | collective-permute-start | bytes 6291464 | tf_op jit(solution)/shard_map/ppermute | solution.py:497
  97.3 0.7 copy-start.1
  101.3 6.8 %copy-start.2 = (f32[256,2]{1,0:T(8,128)S(1)}, f32[256,2]{1,0:T(8,128)}, u32[]{:S(2)}) copy-start(f32[256,2]{1,0:T(8,128)} %copy-done.1) | copy-start | bytes 6148
  101.4 61.4 %all-to-all-start.2 = ((bf16[128,16,1024]{2,1,0:T(8,128)(2,1)}), bf16[128,16,1024]{2,1,0:T(8,128)(2,1)}, u32[]{:S(2)}, u32[]{:S(2)}) async-start(bf16[128,16,1024]{2,1,0:T(8,128)(2,1)} %shard_map.117), calls=%async_computation.2 | async-start | bytes 8388608 | tf_op jit(solution)/shard_map/all_to_all | solution.py:551
  108.2 1.9 %copy-start.3 = (bf16[4,256,1024]{2,1,0:T(8,128)(2,1)S(1)}, bf16[4,256,1024]{2,1,0:T(8,128)(2,1)}, u32[]{:S(2)}) copy-start(bf16[4,256,1024]{2,1,0:T(8,128)(2,1)} %shard_map.114.looked_hbm) | copy-start | bytes 6291460
  115.6 2.2 %copy-start.4 = (bf16[2048,1024]{1,0:T(8,128)(2,1)S(1)}, bf16[2048,1024]{1,0:T(8,128)(2,1)}, u32[]{:S(2)}) copy-start(bf16[2048,1024]{1,0:T(8,128)(2,1)} %depth_hbm.1) | copy-start | bytes 12582916
  120.5 37.6 %collective-permute-start.6 = (f32[4,64]{1,0:T(4,128)S(1)}, f32[4,64]{1,0:T(4,128)S(1)}, u32[]{:S(2)}, u32[]{:S(2)}) collective-permute-start(f32[4,64]{1,0:T(4,128)S(1)} %get-tuple-element.64), channel_id=1, source_target_pairs={{0,12},{1,13},{2,14},{3,15},{4,8},{5,9},{6,10},{7,11},{8,4},{9,5},... | collective-permute-start | bytes 3080 | tf_op jit(solution)/shard_map/ppermute | solution.py:497
  123.3 34.8 %collective-permute-start.5 = (f32[4,64]{1,0:T(4,128)S(1)}, f32[4,64]{1,0:T(4,128)S(1)}, u32[]{:S(2)}, u32[]{:S(2)}) collective-permute-start(f32[4,64]{1,0:T(4,128)S(1)} %get-tuple-element.65), channel_id=1, source_target_pairs={{0,8},{1,9},{2,10},{3,11},{4,12},{5,13},{6,14},{7,15},{8,0},{9,1},... | collective-permute-start | bytes 3080 | tf_op jit(solution)/shard_map/ppermute | solution.py:497
  124.1 34.0 %collective-permute-start.4 = (f32[4,64]{1,0:T(4,128)S(1)}, f32[4,64]{1,0:T(4,128)S(1)}, u32[]{:S(2)}, u32[]{:S(2)}) collective-permute-start(f32[4,64]{1,0:T(4,128)S(1)} %get-tuple-element.66), channel_id=1, source_target_pairs={{0,4},{1,5},{2,6},{3,7},{4,0},{5,1},{6,2},{7,3},{8,12},{9,13},{10,... | collective-permute-start | bytes 3080 | tf_op jit(solution)/shard_map/ppermute | solution.py:497
  158.1 3.1 %collective-permute-start.9 = (f32[4,64]{1,0:T(4,128)S(1)}, f32[4,64]{1,0:T(4,128)S(1)}, u32[]{:S(2)}, u32[]{:S(2)}) collective-permute-start(f32[4,64]{1,0:T(4,128)S(1)} %bitcast.45), channel_id=1, source_target_pairs={{0,3},{1,2},{2,1},{3,0},{4,7},{5,6},{6,5},{7,4},{8,11},{9,10},{10,... | collective-permute-start | bytes 3080 | tf_op jit(solution)/shard_map/ppermute | solution.py:497
  158.2 3.7 %collective-permute-start.8 = (f32[4,64]{1,0:T(4,128)S(1)}, f32[4,64]{1,0:T(4,128)S(1)}, u32[]{:S(2)}, u32[]{:S(2)}) collective-permute-start(f32[4,64]{1,0:T(4,128)S(1)} %bitcast.42), channel_id=1, source_target_pairs={{0,2},{1,3},{2,0},{3,1},{4,6},{5,7},{6,4},{7,5},{8,10},{9,11},{10,... | collective-permute-start | bytes 3080 | tf_op jit(solution)/shard_map/ppermute | solution.py:497
  160.0 1.8 %collective-permute-start.7 = (f32[4,64]{1,0:T(4,128)S(1)}, f32[4,64]{1,0:T(4,128)S(1)}, u32[]{:S(2)}, u32[]{:S(2)}) collective-permute-start(f32[4,64]{1,0:T(4,128)S(1)} %bitcast.39), channel_id=1, source_target_pairs={{0,1},{1,0},{2,3},{3,2},{4,5},{5,4},{6,7},{7,6},{8,9},{9,8},{10,11... | collective-permute-start | bytes 3080 | tf_op jit(solution)/shard_map/ppermute | solution.py:497
